TPU v7x, 256 devices: a whole 4x4x8 slice. The times are simulated.
256 devices in a mesh: gx: 32 (over x, z), gy: 8 (over y, core).
Axes of the slice: x: 4, y: 4, z: 8, core: 2. Of those that a mesh axis runs over, the one named last changes fastest.
Arguments:
- pressure_source: float32 [1024, 256, 256], P('gx', 'gy'), may hold values from -6 to 6
- phase: int32 [1024, 256, 256], P('gx', 'gy'), may hold values 0 or 1
Outputs:
- scaled_pressure: float32 [1024, 256, 256], P('gx', 'gy')
- residual: float32 [1024, 256, 256], P('gx', 'gy')
All inputs are finite; a program needn't handle non-finite values. No bound on the sum of `phase` on one device may be relied on, other than what follows from the above.
Results may differ from a plain program's by a relative error of at most 0.0003.
Values sent between devices are 32-bit elements; how exact they have to be, the bound alone decides.
No kernel may reach another device: no remote copies, remote signals or barrier semaphores. Data moves between devices by JAX's collectives and lax.ppermute only.
A program may use at most 192 MiB of HBM per device.

v0:
```python
import jax
import jax.numpy as jnp
from jax import lax
from jax.experimental import pallas as pl
from jax.experimental.pallas import tpu as pltpu
from jax.sharding import PartitionSpec as P

OMEGA = 0.8
KEEP = 0.2
WATER = 0.001
MIXED = 2.0 * WATER / (1.0 + WATER)
OUT = 0.25
F32 = jnp.float32
MIB = 1024 * 1024


def up_y(a):
    return pltpu.roll(a, a.shape[0] - 1, 0)


def dn_y(a):
    return pltpu.roll(a, 1, 0)


def up_z(a):
    return pltpu.roll(a, a.shape[1] - 1, 1)


def dn_z(a):
    return pltpu.roll(a, 1, 1)


def iota(shape, dim):
    return lax.broadcasted_iota(jnp.int32, shape, dim)


def ring(row, cut, rows):
    return jnp.where(row < cut, row, row - rows)


def restrict_weight(offset):
    near = (offset == 0) | (offset == 1)
    far = (offset == -1) | (offset == 2)
    return jnp.where(near, 0.375, jnp.where(far, 0.125, 0.0)).astype(F32)


def pair_weight(offset):
    return jnp.where((offset == 0) | (offset == 1), 1.0, 0.0).astype(F32)


def dot(a, b):
    return jnp.dot(a, b, precision=lax.Precision.HIGHEST, preferred_element_type=F32)


def face_code(a, b):
    s = a + b
    return jnp.where(s < 0.75, 1.0, jnp.where(s < 1.1, MIXED, WATER)).astype(F32)


def face_mean(a, b):
    product = a * b
    return jnp.where(product > 0.0, 2.0 * product / (a + b), jnp.maximum(a, b))


def weights_at(m, m_next, wx_prev, face, outside, full):
    lane = iota(m.shape, 1)
    last = m.shape[1] - 1
    wx = face(m, m_next)
    wy = face(m, up_y(m))
    m_up = up_z(m)
    if full:
        m_up = jnp.where(lane == last, outside, m_up)
    wz = face(m, m_up)
    wz_low = dn_z(wz)
    if full:
        wz_low = jnp.where(lane == 0, face(m, jnp.full_like(m, outside)), wz_low)
    d = (wx + wx_prev) + (wy + dn_y(wy)) + (wz + wz_low)
    q = jnp.where(m != outside, OMEGA / d, 0.0)
    if full:
        wz = jnp.where(lane == last, 0.0, wz)
    return wx, wy, wz, d, q


def weights_pass(lo, hi, m_ref, w, face, outside, full, first):
    wx_ref, wy_ref, wz_ref, d_ref, q_ref = w
    start = face(m_ref[lo - 1], m_ref[lo])
    wx_ref[lo - 1] = start

    def body(j, wx_prev):
        wx, wy, wz, d, q = weights_at(m_ref[j], m_ref[j + 1], wx_prev, face, outside, full)
        wx_ref[j] = wx
        wy_ref[j] = wy
        wz_ref[j] = wz
        d_ref[j] = d
        q_ref[j] = q
        first(j, q)
        return wx

    lax.fori_loop(lo, hi, body, start)


def flow(j, p, p_ref, w):
    wx_ref, wy_ref, wz_ref = w[:3]
    wy, wz = wy_ref[j], wz_ref[j]
    along_x = wx_ref[j] * p_ref[j + 1] + wx_ref[j - 1] * p_ref[j - 1]
    along_y = wy * up_y(p) + dn_y(wy * p)
    along_z = wz * up_z(p) + dn_z(wz * p)
    return along_x + along_y + along_z


def sweep(lo, hi, p_ref, out_ref, s_ref, w):
    def body(j, carry):
        p = p_ref[j]
        out_ref[j] = KEEP * p + w[4][j] * (s_ref[j] + flow(j, p, p_ref, w))
        return carry

    lax.fori_loop(lo, hi, body, 0)


def remainder(lo, hi, p_ref, out_ref, s_ref, w):
    def body(j, carry):
        p = p_ref[j]
        r = s_ref[j] + flow(j, p, p_ref, w) - w[3][j] * p
        out_ref[j] = jnp.where(w[4][j] > 0.0, r, 0.0)
        return carry

    lax.fori_loop(lo, hi, body, 0)


def restrict_x(r_ref, j):
    return (r_ref[j] + r_ref[j + 3]) * 0.125 + (r_ref[j + 1] + r_ref[j + 2]) * 0.375


def edge(axis):
    i = lax.axis_index(axis)
    return i == 0, i == lax.axis_size(axis) - 1


def blank(flag, value, other):
    return jnp.where(flag, other, value)


X0 = 5
N0 = 32 + 2 * X0


def pack0_kernel(s_lo, s_hi, f_lo, f_hi, xl_lo, xl_hi, xh_lo, xh_hi, dn_ref, upw_ref, s_ref, c_ref):
    low_x, high_x = edge("gx")
    sub = iota((8, 256), 0)
    for own_s, own_f, xl, xh, out_ref, row in (
        (s_lo, f_lo, xl_lo, xh_lo, dn_ref, 3),
        (s_hi, f_hi, xl_hi, xh_hi, upw_ref, 4),
    ):
        s_ref[0] = jnp.zeros((8, 256), F32)
        s_ref[N0 - 1] = jnp.zeros((8, 256), F32)
        s_ref[1:X0] = blank(low_x, xl[:4], 0.0)
        c_ref[0:X0] = blank(low_x, xl[4:], OUT)
        s_ref[X0 + 32 : N0 - 1] = blank(high_x, xh[:4], 0.0)
        c_ref[X0 + 32 : N0] = blank(high_x, xh[4:], OUT)
        s_ref[X0 : X0 + 32] = own_s[...]
        c_ref[X0 : X0 + 32] = own_f[...].astype(F32)
        is_source = sub < 4 if row == 3 else sub >= 4

        def message(j, s, out_ref=out_ref, is_source=is_source):
            out_ref[j] = jnp.where(is_source, s, pltpu.roll(c_ref[j], 4, 0))

        message(0, s_ref[0])
        message(N0 - 1, s_ref[N0 - 1])

        def body(j, wx_prev, row=row, message=message):
            c = c_ref[j]
            wx, _, _, _, q = weights_at(c, c_ref[j + 1], wx_prev, face_code, OUT, True)
            s = s_ref[j]
            message(j, jnp.where(sub == row, q * s, s))
            return wx

        lax.fori_loop(1, N0 - 1, body, face_code(c_ref[0], c_ref[1]))


def pack0(source, phase, xlo, xhi):
    own = lambda k: pl.BlockSpec((32, 8, 256), lambda i, k=k: (0, k, 0))
    halo = lambda k: pl.BlockSpec((9, 8, 256), lambda i, k=k: (0, k, 0))
    whole = pl.BlockSpec((N0, 8, 256), lambda i: (0, 0, 0))
    shape = jax.ShapeDtypeStruct((N0, 8, 256), F32)
    return pl.pallas_call(
        pack0_kernel,
        grid=(1,),
        in_specs=[own(0), own(3), own(0), own(3), halo(0), halo(3), halo(0), halo(3)],
        out_specs=[whole, whole],
        out_shape=[shape, shape],
        scratch_shapes=[pltpu.VMEM((N0, 8, 256), F32)] * 2,
        compiler_params=pltpu.CompilerParams(vmem_limit_bytes=16 * MIB),
        name="pack0",
    )(source, source, phase, phase, xlo, xlo, xhi, xhi)


N1 = 28
N2 = 28
N3 = 12


def copies(pairs, sems):
    return [pltpu.make_async_copy(a, b, sems.at[k]) for k, (a, b) in enumerate(pairs)]


def down0_kernel(
    s_in, f_in, xlo, xhi, ylo, yhi,
    src1, mob1, dn1, upw1, wx_o, wy_o, wz_o, d_o, q_o, s_o, p_o,
    s_ref, c_ref, wx, wy, wz, d_ref, q_ref, p1, p2, r_ref, t_ref, sems,
):
    low_x, high_x = edge("gx")
    low_y, high_y = edge("gy")
    own = slice(X0, X0 + 32)
    s_ref[0, :32] = jnp.zeros((32, 256), F32)
    s_ref[N0 - 1, :32] = jnp.zeros((32, 256), F32)
    s_ref[1:X0, :32] = blank(low_x, xlo[:4], 0.0)
    c_ref[0:X0, :32] = blank(low_x, xlo[4:], OUT)
    s_ref[X0 + 32 : N0 - 1, :32] = blank(high_x, xhi[:4], 0.0)
    c_ref[X0 + 32 : N0, :32] = blank(high_x, xhi[4:], OUT)
    sub = iota((8, 256), 0)
    above = sub < 4
    outer = (above & high_y) | (~above & low_y)

    def tile4(j, carry):
        hi, lo = yhi[j], ylo[j]
        s_ref[j, 32:] = jnp.where(outer, 0.0, jnp.where(above, hi, lo))
        c_ref[j, 32:] = jnp.where(outer, OUT, pltpu.roll(jnp.where(above, lo, hi), 4, 0))
        return carry

    lax.fori_loop(0, N0, tile4, 0)

    def own_planes(j, carry):
        s_ref[j + X0, :32] = s_in[j]
        c_ref[j + X0, :32] = f_in[j].astype(F32)
        return carry

    lax.fori_loop(0, 32, own_planes, 0)

    w = (wx, wy, wz, d_ref, q_ref)
    row = iota((40, 256), 0)
    seam = (row == 35) | (row == 36)

    def first(j, q):
        s = s_ref[j]
        p1[j] = jnp.where(seam, s, q * s)

    weights_pass(1, N0 - 1, c_ref, w, face_code, OUT, True, first)
    state = copies(
        [(wx, wx_o), (wy, wy_o), (wz, wz_o), (d_ref, d_o), (q_ref, q_o), (s_ref, s_o), (p2, p_o)], sems
    )
    for copy in state[:-1]:
        copy.start()
    sweep(2, N0 - 2, p1, p2, s_ref, w)
    state[-1].start()
    remainder(4, N0 - 4, p2, r_ref, s_ref, w)

    fine_z, coarse_z = iota((256, 128), 0), iota((256, 128), 1)
    fine_y = ring(iota((16, 40), 1), 36, 40)
    coarse_y = iota((16, 40), 0)
    rz = restrict_weight(fine_z - 2 * coarse_z)
    mz = pair_weight(fine_z - 2 * coarse_z)
    ry = restrict_weight(fine_y - 2 * coarse_y)
    my = pair_weight(fine_y - 2 * coarse_y)

    def halve(k, carry):
        t_ref[pl.ds(pl.multiple_of(k * 40, 8), 40)] = restrict_x(r_ref, 2 * k + 4)
        return carry

    lax.fori_loop(0, 16, halve, 0)
    coarse = dot(t_ref[...], rz)
    for k in range(16):
        src1[k] = dot(ry, coarse[k * 40 : k * 40 + 40])

    def count(k, carry):
        t_ref[pl.ds(pl.multiple_of(k * 40, 8), 40)] = c_ref[2 * k + X0] + c_ref[2 * k + X0 + 1]
        return carry

    lax.fori_loop(0, 16, count, 0)
    water = dot(t_ref[...], mz)
    for k in range(16):
        n = dot(my, water[k * 40 : k * 40 + 40])
        mob1[k] = 0.25 * ((8.0 - n) * 0.125 + n * (0.125 * WATER))
    dn1[:5] = src1[:5]
    dn1[5:] = mob1[:6]
    upw1[:5] = src1[11:]
    upw1[5:] = mob1[10:]
    for copy in state:
        copy.wait()


def down0(source, phase, xlo, xhi, ylo, yhi):
    big = jax.ShapeDtypeStruct((N0, 40, 256), F32)
    own1 = jax.ShapeDtypeStruct((16, 16, 128), F32)
    msg1 = jax.ShapeDtypeStruct((11, 16, 128), F32)
    vmem = pl.BlockSpec(memory_space=pltpu.VMEM)
    anyw = pl.BlockSpec(memory_space=pl.ANY)
    return pl.pallas_call(
        down0_kernel,
        in_specs=[vmem] * 6,
        out_specs=[vmem] * 4 + [anyw] * 7,
        out_shape=[own1, own1, msg1, msg1] + [big] * 7,
        scratch_shapes=[pltpu.VMEM((N0, 40, 256), F32)] * 10
        + [pltpu.VMEM((640, 256), F32), pltpu.SemaphoreType.DMA((7,))],
        compiler_params=pltpu.CompilerParams(vmem_limit_bytes=40 * MIB),
        name="down0",
    )(source, phase, xlo, xhi, ylo, yhi)


def pack1_kernel(src, mob, xlo, xhi, dn_ref, upw_ref):
    low_x, high_x = edge("gx")
    for rows, out in ((slice(0, 8), dn_ref), (slice(8, 16), upw_ref)):
        out[0, :8] = jnp.zeros((8, 128), F32)
        out[N1 - 1, :8] = jnp.zeros((8, 128), F32)
        out[1:6, :8] = blank(low_x, xlo[:5, rows], 0.0)
        out[0:6, 8:] = blank(low_x, xlo[5:, rows], 0.0)
        out[6:22, :8] = src[:, rows]
        out[6:22, 8:] = mob[:, rows]
        out[22:27, :8] = blank(high_x, xhi[:5, rows], 0.0)
        out[22:28, 8:] = blank(high_x, xhi[5:, rows], 0.0)


def pack1(src, mob, xlo, xhi):
    shape = jax.ShapeDtypeStruct((N1, 16, 128), F32)
    vmem = pl.BlockSpec(memory_space=pltpu.VMEM)
    return pl.pallas_call(
        pack1_kernel,
        in_specs=[vmem] * 4,
        out_specs=[vmem] * 2,
        out_shape=[shape, shape],
        name="pack1",
    )(src, mob, xlo, xhi)


def down1_kernel(
    src, mob, xlo, xhi, ylo, yhi,
    own2, dn2, upw2, s_ref, wx, wy, wz, q_ref, p2,
    m_ref, d_ref, p1, r_ref, t_ref, pk_ref,
):
    low_x, high_x = edge("gx")
    low_y, high_y = edge("gy")
    zero = jnp.zeros((32, 128), F32)
    s_ref[0] = zero
    s_ref[N1 - 1] = zero
    s_ref[1:6, :16] = blank(low_x, xlo[:5], 0.0)
    m_ref[0:6, :16] = blank(low_x, xlo[5:], 0.0)
    s_ref[6:22, :16] = src[...]
    m_ref[6:22, :16] = mob[...]
    s_ref[22:27, :16] = blank(high_x, xhi[:5], 0.0)
    m_ref[22:28, :16] = blank(high_x, xhi[5:], 0.0)
    s_ref[:, 16:24] = blank(high_y, yhi[:, :8], 0.0)
    m_ref[:, 16:24] = blank(high_y, yhi[:, 8:], 0.0)
    s_ref[:, 24:] = blank(low_y, ylo[:, :8], 0.0)
    m_ref[:, 24:] = blank(low_y, ylo[:, 8:], 0.0)
    w = (wx, wy, wz, d_ref, q_ref)

    def first(j, q):
        p1[j] = q * s_ref[j]

    weights_pass(1, N1 - 1, m_ref, w, face_mean, 0.0, True, first)
    sweep(2, N1 - 2, p1, p2, s_ref, w)
    remainder(3, N1 - 3, p2, r_ref, s_ref, w)

    lane_in, lane_out = iota((128, 128), 0), iota((128, 128), 1)
    rz = jnp.where(lane_out < 64, restrict_weight(lane_in - 2 * lane_out), 0.0)
    mz = pair_weight(lane_in - 2 * (lane_out - 64))
    row_out = iota((16, 32), 0)
    coarse_y = ring(row_out, 12, 16)
    held = (coarse_y >= -2) & (coarse_y <= 9)
    fine_y = ring(iota((16, 32), 1), 24, 32)
    ry = jnp.where(held, restrict_weight(fine_y - 2 * coarse_y), 0.0)
    my = jnp.where(held, pair_weight(fine_y - 2 * coarse_y), 0.0)
    zero16 = jnp.zeros((16, 128), F32)
    for k in range(10):
        t_ref[k * 32 : k * 32 + 32] = restrict_x(r_ref, 2 * k + 3)
    coarse = dot(t_ref[:320], rz)
    for k in range(12):
        t_ref[k * 32 : k * 32 + 32] = (m_ref[2 * k + 2] + m_ref[2 * k + 3]) * (0.25 * 0.125)
    mean = dot(t_ref[...], mz)
    for k in range(12):
        value = dot(my, mean[k * 32 : k * 32 + 32])
        if 1 <= k <= 10:
            value = value + dot(ry, coarse[(k - 1) * 32 : k * 32])
        pk_ref[k] = value
    own2[...] = pk_ref[2:10]
    dn2[...] = pk_ref[2:12]
    upw2[...] = pk_ref[0:10]


def down1(src, mob, xlo, xhi, ylo, yhi):
    big = jax.ShapeDtypeStruct((N1, 32, 128), F32)
    vmem = pl.BlockSpec(memory_space=pltpu.VMEM)
    return pl.pallas_call(
        down1_kernel,
        in_specs=[vmem] * 6,
        out_specs=[vmem] * 9,
        out_shape=[jax.ShapeDtypeStruct((k, 16, 128), F32) for k in (8, 10, 10)] + [big] * 6,
        scratch_shapes=[pltpu.VMEM((N1, 32, 128), F32)] * 4
        + [pltpu.VMEM((384, 128), F32), pltpu.VMEM((12, 16, 128), F32)],
        compiler_params=pltpu.CompilerParams(vmem_limit_bytes=16 * MIB),
        name="down1",
    )(src, mob, xlo, xhi, ylo, yhi)


def pack2_kernel(own, xlo, xhi, out):
    low_x, high_x = edge("gx")
    out[:10] = blank(low_x, xlo[...], 0.0)
    out[10:18] = own[...]
    out[18:] = blank(high_x, xhi[...], 0.0)


def pack2(own, xlo, xhi):
    vmem = pl.BlockSpec(memory_space=pltpu.VMEM)
    return pl.pallas_call(
        pack2_kernel,
        in_specs=[vmem] * 3,
        out_specs=vmem,
        out_shape=jax.ShapeDtypeStruct((N2, 16, 128), F32),
        name="pack2",
    )(own, xlo, xhi)


def up_kernel(
    ext, ylo, yhi, s1, wx1, wy1, wz1, q1, down1_ref,
    wx0_h, wy0_h, wz0_h, d0_h, q0_h, s0_h, p0_h,
    scaled, residual,
    wx0, wy0, wz0, d0, q0, s0, pa0, pb0,
    pa1, pb1,
    s2, m2, wx2, wy2, wz2, d2, q2, pa2, pb2, r2,
    s3, m3, wx3, wy3, wz3, d3, q3, pa3, pb3,
    t_ref, u_ref, v_ref, sems,
):
    state = copies(
        [(wx0_h, wx0), (wy0_h, wy0), (wz0_h, wz0), (d0_h, d0), (q0_h, q0), (s0_h, s0), (p0_h, pa0)], sems
    )
    for copy in state:
        copy.start()
    low_y, high_y = edge("gy")

    lane8, sub8 = iota((8, 128), 1), iota((8, 128), 0)

    def unpack(j, carry):
        def put(rows, packed):
            s2[j, rows] = packed
            m2[j, rows] = jnp.where(lane8 < 64, pltpu.roll(packed, 64, 1), 0.0)

        hi = blank(high_y, yhi[j], 0.0)
        lo = blank(low_y, ylo[j], 0.0)
        put(slice(0, 8), ext[j, :8])
        put(slice(8, 16), hi[:8])
        put(slice(16, 24), jnp.where(sub8 < 4, hi[8:], lo[8:]))
        put(slice(24, 32), lo[:8])
        return carry

    lax.fori_loop(0, N2, unpack, 0)
    w2 = (wx2, wy2, wz2, d2, q2)

    def first2(j, q):
        pa2[j] = q * s2[j]

    weights_pass(1, N2 - 1, m2, w2, face_mean, 0.0, False, first2)
    sweep(2, N2 - 2, pa2, pb2, s2, w2)
    remainder(3, N2 - 3, pb2, r2, s2, w2)

    lane_in, lane_out = iota((128, 128), 0), iota((128, 128), 1)
    down_z = lane_in - 2 * lane_out
    inner = (lane_in < 64) & (lane_out < 32)
    rz = jnp.where(inner, restrict_weight(down_z), 0.0)
    mz = jnp.where(inner, pair_weight(down_z), 0.0)
    coarse_y = ring(iota((16, 32), 0), 8, 16)
    fine_y = ring(iota((16, 32), 1), 20, 32)
    ry = restrict_weight(fine_y - 2 * coarse_y)
    my = pair_weight(fine_y - 2 * coarse_y)
    for k in range(10):
        t_ref[k * 32 : k * 32 + 32] = restrict_x(r2, 2 * k + 3)
    coarse = dot(t_ref[:320], rz)
    for k in range(12):
        t_ref[k * 32 : k * 32 + 32] = (m2[2 * k + 2] + m2[2 * k + 3]) * (0.25 * 0.125)
    mean = dot(t_ref[:384], mz)
    for k in range(12):
        m3[k] = dot(my, mean[k * 32 : k * 32 + 32])
        if 1 <= k <= 10:
            s3[k] = dot(ry, coarse[(k - 1) * 32 : k * 32])
    w3 = (wx3, wy3, wz3, d3, q3)

    def first3(j, q):
        pa3[j] = q * s3[j]

    weights_pass(1, N3 - 1, m3, w3, face_mean, 0.0, False, first3)
    sweep(2, N3 - 2, pa3, pb3, s3, w3)

    pz = pair_weight(lane_out - 2 * lane_in)
    pz = jnp.where(lane_in < 32, pz, 0.0)
    py = pair_weight(ring(iota((32, 16), 0), 20, 32) - 2 * ring(iota((32, 16), 1), 8, 16))
    for k in range(8):
        t_ref[k * 32 : k * 32 + 32] = dot(py, pb3[k + 2])
    u_ref[:256] = dot(t_ref[:256], pz)
    for k in range(8):
        rise = u_ref[k * 32 : k * 32 + 32]
        pb2[2 * k + 6] = pb2[2 * k + 6] + rise
        pb2[2 * k + 7] = pb2[2 * k + 7] + rise
    sweep(7, 21, pb2, pa2, s2, w2)
    sweep(8, 20, pa2, pb2, s2, w2)

    pz = pair_weight(lane_out - 2 * lane_in)
    py = pair_weight(ring(iota((32, 32), 0), 24, 32) - 2 * ring(iota((32, 32), 1), 20, 32))
    for k in range(12):
        t_ref[k * 32 : k * 32 + 32] = dot(py, pb2[k + 8])
    u_ref[:384] = dot(t_ref[:384], pz)
    for k in range(12):
        rise = u_ref[k * 32 : k * 32 + 32]
        pa1[2 * k + 2] = down1_ref[2 * k + 2] + rise
        pa1[2 * k + 3] = down1_ref[2 * k + 3] + rise
    w1 = (wx1, wy1, wz1, None, q1)
    sweep(3, 25, pa1, pb1, s1, w1)
    sweep(4, 24, pb1, pa1, s1, w1)

    pz = pair_weight(iota((128, 256), 1) - 2 * iota((128, 256), 0))
    py = pair_weight(ring(iota((40, 32), 0), 36, 40) - 2 * ring(iota((40, 32), 1), 24, 32))
    for k in range(20):
        t_ref[k * 40 : k * 40 + 40] = dot(py, pa1[k + 4])
    v_ref[...] = dot(t_ref[...], pz)
    for copy in state:
        copy.wait()

    def rise0(j, carry):
        k = (j - 1) // 2
        pa0[j] = pa0[j] + v_ref[pl.ds(pl.multiple_of(k * 40, 8), 40)]
        return carry

    lax.fori_loop(2, N0 - 2, rise0, 0)
    w0 = (wx0, wy0, wz0, d0, q0)
    sweep(3, N0 - 3, pa0, pb0, s0, w0)
    sweep(4, N0 - 4, pb0, pa0, s0, w0)

    def last(j, carry):
        p = pa0[j]
        dp = d0[j] * p
        scaled[j - X0] = dp[:32]
        residual[j - X0] = (s0[j] + flow(j, p, pa0, w0) - dp)[:32]
        return carry

    lax.fori_loop(X0, X0 + 32, last, 0)


def way_up(ext, ylo, yhi, level1, level0):
    vmem = pl.BlockSpec(memory_space=pltpu.VMEM)
    anyw = pl.BlockSpec(memory_space=pl.ANY)
    shape = jax.ShapeDtypeStruct((32, 32, 256), F32)
    buf = lambda count, *shape: [pltpu.VMEM(shape, F32)] * count
    return pl.pallas_call(
        up_kernel,
        in_specs=[vmem] * 9 + [anyw] * 7,
        out_specs=[vmem] * 2,
        out_shape=[shape, shape],
        scratch_shapes=buf(8, N0, 40, 256)
        + buf(2, N1, 32, 128)
        + buf(10, N2, 32, 128)
        + buf(9, N3, 16, 128)
        + buf(1, 800, 128)
        + buf(1, 384, 128)
        + buf(1, 800, 256)
        + [pltpu.SemaphoreType.DMA((7,))],
        compiler_params=pltpu.CompilerParams(vmem_limit_bytes=40 * MIB),
        name="way_up",
    )(ext, ylo, yhi, *level1, *level0)


def shift(a, axis, step):
    count = lax.axis_size(axis)
    return lax.ppermute(a, axis, [(i, (i + step) % count) for i in range(count)])


def both(to_low, to_high, axis):
    return shift(to_high, axis, 1), shift(to_low, axis, -1)


def shards(source, phase):
    to_low = jnp.concatenate([source[:4], phase[:5].astype(F32)])
    to_high = jnp.concatenate([source[28:], phase[27:].astype(F32)])
    xlo, xhi = both(to_low, to_high, "gx")
    ylo, yhi = both(*pack0(source, phase, xlo, xhi), "gy")
    src1, mob1, dn1, up1, *level0 = down0(source, phase, xlo, xhi, ylo, yhi)
    xlo, xhi = both(dn1, up1, "gx")
    ylo, yhi = both(*pack1(src1, mob1, xlo, xhi), "gy")
    own2, dn2, up2, *level1 = down1(src1, mob1, xlo, xhi, ylo, yhi)
    xlo, xhi = both(dn2, up2, "gx")
    ext = pack2(own2, xlo, xhi)
    ylo, yhi = both(ext, ext, "gy")
    scaled, residual = way_up(ext, ylo, yhi, level1, level0)
    return scaled, residual


def solution(mesh):
    spec = P("gx", "gy", None)
    return jax.shard_map(shards, mesh=mesh, in_specs=(spec, spec), out_specs=(spec, spec), check_vma=False)
```

profile of v0, /device:TPU:25, one launch (start us, length us, event | category | flops | bytes accessed | tf_op | source)
XLA Modules:
  0.0 165.7 jit_solution(4213987875516475031)
XLA Ops:
  0.6 0.0 copy-start.1
  0.6 0.0 copy-start
  0.7 1.1 fusion
  1.8 1.0 slice_convert_fusion
  2.8 1.7 %collective-permute-start = (f32[9,32,256]{2,1,0:T(8,128)S(1)}, f32[9,32,256]{2,1,0:T(8,128)S(1)}, u32[]{:S(2)}, u32[]{:S(2)}) collective-permute-start(f32[9,32,256]{2,1,0:T(8,128)S(1)} %pad_maximum_fusion), channel_id=1, source_target_pairs={{0,8},{8,16},{16,24},{24,32},{32,40},{40,48},{48,56},{56,64},{64,7... | collective-permute-start | bytes 884744 | tf_op jit(solution)/shard_map/ppermute | solution.py:570
  4.6 6.2 %collective-permute-start.1 = (f32[9,32,256]{2,1,0:T(8,128)S(1)}, f32[9,32,256]{2,1,0:T(8,128)S(1)}, u32[]{:S(2)}, u32[]{:S(2)}) collective-permute-start(f32[9,32,256]{2,1,0:T(8,128)S(1)} %pad_maximum_fusion.1), channel_id=1, source_target_pairs={{0,248},{8,0},{16,8},{24,16},{32,24},{40,32},{48,40},{56,48},{64,5... | collective-permute-start | bytes 884744 | tf_op jit(solution)/shard_map/ppermute | solution.py:570
  10.8 6.6 %collective-permute-done.xl_lo.xl_hi.xlo = f32[9,32,256]{2,1,0:T(8,128)S(1)} collective-permute-done((f32[9,32,256]{2,1,0:T(8,128)S(1)}, f32[9,32,256]{2,1,0:T(8,128)S(1)}, u32[]{:S(2)}, u32[]{:S(2)}) %collective-permute-start) | collective-permute-done | bytes 294944 | tf_op jit(solution)/shard_map/ppermute | solution.py:570
  17.4 0.0 collective-permute-done.1.xh_lo.xh_hi.xhi
  17.4 0.0 copy-done.1
  17.4 12.7 %pack0.1 = (f32[42,8,256]{2,1,0:T(8,128)S(1)}, f32[42,8,256]{2,1,0:T(8,128)S(1)}) custom-call(f32[32,32,256]{2,1,0:T(8,128)S(1)} %copy-done.1, f32[32,32,256]{2,1,0:T(8,128)S(1)} %copy-done.1, s32[32,32,256]{2,1,0:T(8,128)S(1)} %copy-done, s32[32,32,256]{2,1,0:T(8,128)S(1)} %copy-done, f32[9,32,256]{2,1,0:T(8,128)S(1)} %collective-permute-done.xl_lo.xl_hi.xlo, ...), custom_call_target="tpu_custom_call" | custom-call | tf_op jit(solution)/shard_map/pack0/pallas_call | solution.py:185
  30.1 1.1 collective-permute-start.2
  31.2 0.2 collective-permute-start.3
  31.4 4.0 %collective-permute-done.2.ylo = f32[42,8,256]{2,1,0:T(8,128)S(1)} collective-permute-done((f32[42,8,256]{2,1,0:T(8,128)S(1)}, f32[42,8,256]{2,1,0:T(8,128)S(1)}, u32[]{:S(2)}, u32[]{:S(2)}) %collective-permute-start.2) | collective-permute-done | bytes 344096 | tf_op jit(solution)/shard_map/ppermute | solution.py:570
  35.4 3.7 %collective-permute-done.3.yhi = f32[42,8,256]{2,1,0:T(8,128)S(1)} collective-permute-done((f32[42,8,256]{2,1,0:T(8,128)S(1)}, f32[42,8,256]{2,1,0:T(8,128)S(1)}, u32[]{:S(2)}, u32[]{:S(2)}) %collective-permute-start.3) | collective-permute-done | bytes 344096 | tf_op jit(solution)/shard_map/ppermute | solution.py:570
  39.1 20.0 %down0.1 = (f32[16,16,128]{2,1,0:T(8,128)S(1)}, f32[16,16,128]{2,1,0:T(8,128)S(1)}, f32[11,16,128]{2,1,0:T(8,128)S(1)}, f32[11,16,128]{2,1,0:T(8,128)S(1)}, f32[...) custom-call(f32[32,32,256]{2,1,0:T(8,128)S(1)} %copy-done.1, ...), custom_call_target="tpu_custom_call" | custom-call | tf_op jit(solution)/shard_map/down0/pallas_call | solution.py:297
  59.1 1.2 copy-done.2
  60.2 1.2 copy-done.4
  61.4 1.2 copy-done.6
  62.7 1.3 copy-done.8
  64.0 0.7 copy-done.11
  64.6 0.7 copy-done.13
  65.3 0.0 collective-permute-start.4
  65.3 4.9 %collective-permute-start.5 = (f32[11,16,128]{2,1,0:T(8,128)S(1)}, f32[11,16,128]{2,1,0:T(8,128)}, u32[]{:S(2)}, u32[]{:S(2)}) collective-permute-start(f32[11,16,128]{2,1,0:T(8,128)S(1)} %get-tuple-element.31), channel_id=1, source_target_pairs={{0,248},{8,0},{16,8},{24,16},{32,24},{40,32},{48,40},{56,48},{64,5... | collective-permute-start | bytes 270344 | tf_op jit(solution)/shard_map/ppermute | solution.py:570
  70.2 2.2 %collective-permute-done.4.xlo = f32[11,16,128]{2,1,0:T(8,128)S(1)} collective-permute-done((f32[11,16,128]{2,1,0:T(8,128)S(1)}, f32[11,16,128]{2,1,0:T(8,128)S(1)}, u32[]{:S(2)}, u32[]{:S(2)}) %collective-permute-start.4) | collective-permute-done | bytes 90144 | tf_op jit(solution)/shard_map/ppermute | solution.py:570
  72.4 0.0 collective-permute-done.5.xhi
  72.4 0.6 copy-done.27
  73.0 1.9 %pack1.1 = (f32[28,16,128]{2,1,0:T(8,128)}, f32[28,16,128]{2,1,0:T(8,128)}) custom-call(f32[16,16,128]{2,1,0:T(8,128)} %copy-done.11, f32[16,16,128]{2,1,0:T(8,128)} %copy-done.13, f32[11,16,128]{2,1,0:T(8,128)} %copy-done.27, f32[11,16,128]{2,1,0:T(8,128)} %collective-permute-done.5.xhi), custom_call_target="tpu_custom_call" | custom-call | tf_op jit(solution)/shard_map/pack1/pallas_call | solution.py:325
  74.9 1.3 collective-permute-start.6
  76.2 0.0 collective-permute-start.7
  76.2 3.3 %collective-permute-done.6.ylo = f32[28,16,128]{2,1,0:T(8,128)S(1)} collective-permute-done((f32[28,16,128]{2,1,0:T(8,128)}, f32[28,16,128]{2,1,0:T(8,128)S(1)}, u32[]{:S(2)}, u32[]{:S(2)}) %collective-permute-start.6) | collective-permute-done | bytes 229408 | tf_op jit(solution)/shard_map/ppermute | solution.py:570
  79.5 3.6 %collective-permute-done.7.yhi = f32[28,16,128]{2,1,0:T(8,128)S(1)} collective-permute-done((f32[28,16,128]{2,1,0:T(8,128)}, f32[28,16,128]{2,1,0:T(8,128)S(1)}, u32[]{:S(2)}, u32[]{:S(2)}) %collective-permute-start.7) | collective-permute-done | bytes 229408 | tf_op jit(solution)/shard_map/ppermute | solution.py:570
  83.1 0.9 copy-done.12
  84.0 0.9 copy-done.14
  84.9 0.9 copy-done.28
  85.8 10.0 %down1.1 = (f32[8,16,128]{2,1,0:T(8,128)S(1)}, f32[10,16,128]{2,1,0:T(8,128)S(1)}, f32[10,16,128]{2,1,0:T(8,128)S(1)}, f32[28,32,128]{2,1,0:T(8,128)S(1)}, f32[2...) custom-call(f32[16,16,128]{2,1,0:T(8,128)S(1)} %copy-done.12, ...), custom_call_target="tpu_custom_call" | custom-call | tf_op jit(solution)/shard_map/down1/pallas_call | solution.py:392
  95.8 0.8 copy-done.15
  96.5 0.8 copy-done.17
  97.3 0.8 copy-done.19
  98.1 0.8 copy-done.21
  98.9 0.8 copy-done.23
  99.7 0.8 copy-done.25
  100.4 0.6 copy-done.29
  101.1 0.0 collective-permute-start.8
  101.1 4.8 %collective-permute-start.9 = (f32[10,16,128]{2,1,0:T(8,128)S(1)}, f32[10,16,128]{2,1,0:T(8,128)S(1)}, u32[]{:S(2)}, u32[]{:S(2)}) collective-permute-start(f32[10,16,128]{2,1,0:T(8,128)S(1)} %get-tuple-element.36), channel_id=1, source_target_pairs={{0,248},{8,0},{16,8},{24,16},{32,24},{40,32},{48,40},{56,48},{64,5... | collective-permute-start | bytes 245768 | tf_op jit(solution)/shard_map/ppermute | solution.py:570
  105.8 1.8 %collective-permute-done.8.xlo = f32[10,16,128]{2,1,0:T(8,128)S(1)} collective-permute-done((f32[10,16,128]{2,1,0:T(8,128)S(1)}, f32[10,16,128]{2,1,0:T(8,128)S(1)}, u32[]{:S(2)}, u32[]{:S(2)}) %collective-permute-start.8) | collective-permute-done | bytes 81952 | tf_op jit(solution)/shard_map/ppermute | solution.py:570
  107.7 0.0 collective-permute-done.9.xhi
  107.7 0.6 copy-done.31
  108.3 1.7 %pack2.1.ext = f32[28,16,128]{2,1,0:T(8,128)} custom-call(f32[8,16,128]{2,1,0:T(8,128)} %copy-done.29, f32[10,16,128]{2,1,0:T(8,128)} %copy-done.30, f32[10,16,128]{2,1,0:T(8,128)} %copy-done.31), custom_call_target="tpu_custom_call" | custom-call | tf_op jit(solution)/shard_map/pack2/pallas_call | solution.py:413
  110.0 0.0 collective-permute-start.11
  110.0 3.0 %collective-permute-start.10 = (f32[28,16,128]{2,1,0:T(8,128)}, f32[28,16,128]{2,1,0:T(8,128)S(1)}, u32[]{:S(2)}, u32[]{:S(2)}) collective-permute-start(f32[28,16,128]{2,1,0:T(8,128)} %pack2.1.ext), channel_id=1, source_target_pairs={{0,1},{1,2},{2,3},{3,4},{4,5},{5,6},{6,7},{7,0},{8,9},{9,10},{10,1... | collective-permute-start | bytes 688136 | tf_op jit(solution)/shard_map/ppermute | solution.py:570
  113.0 3.9 %collective-permute-done.11.yhi = f32[28,16,128]{2,1,0:T(8,128)S(1)} collective-permute-done((f32[28,16,128]{2,1,0:T(8,128)}, f32[28,16,128]{2,1,0:T(8,128)S(1)}, u32[]{:S(2)}, u32[]{:S(2)}) %collective-permute-start.11) | collective-permute-done | bytes 229408 | tf_op jit(solution)/shard_map/ppermute | solution.py:570
  116.9 0.0 collective-permute-done.10.ylo
  116.9 1.5 copy-done.3
  118.3 1.5 copy-done.5
  119.8 1.5 copy-done.7
  121.3 1.5 copy-done.9
  122.7 0.9 copy-done.10
  123.7 1.0 copy-done.16
  124.7 1.0 copy-done.18
  125.7 1.0 copy-done.20
  126.7 1.0 copy-done.22
  127.7 1.0 copy-done.24
  128.8 1.0 copy-done.26
  129.8 35.7 %way_up.1 = (f32[32,32,256]{2,1,0:T(8,128)}, f32[32,32,256]{2,1,0:T(8,128)}) custom-call(f32[28,16,128]{2,1,0:T(8,128)S(1)} %copy-done.10, f32[28,16,128]{2,1,0:T(8,128)S(1)} %collective-permute-done.10.ylo, f32[28,16,128]{2,1,0:T(8,128)S(1)} %collective-permute-done.11.yhi, f32[28,32,128]{2,1,0:T(8,128)S(1)} %copy-done.16, f32[28,32,128]{2,1,0:T(8,128)S(1)} %copy-done.18, ...), custom_call_target="tpu_custom_call" | custom-call | tf_op jit(solution)/shard_map/way_up/pallas_call | solution.py:550
  (34 shorter events, 0.1 us)
Async XLA Ops:
  0.6 16.8 %copy-start.1 = (f32[32,32,256]{2,1,0:T(8,128)S(1)}, f32[32,32,256]{2,1,0:T(8,128)}, u32[]{:S(2)}) copy-start(f32[32,32,256]{2,1,0:T(8,128)} %s_in.1) | copy-start | bytes 3145732
  0.6 16.8 %copy-start = (s32[32,32,256]{2,1,0:T(8,128)S(1)}, s32[32,32,256]{2,1,0:T(8,128)}, u32[]{:S(2)}) copy-start(s32[32,32,256]{2,1,0:T(8,128)} %f_in.1) | copy-start | bytes 3145732
  2.8 14.6 %collective-permute-start = (f32[9,32,256]{2,1,0:T(8,128)S(1)}, f32[9,32,256]{2,1,0:T(8,128)S(1)}, u32[]{:S(2)}, u32[]{:S(2)}) collective-permute-start(f32[9,32,256]{2,1,0:T(8,128)S(1)} %pad_maximum_fusion), channel_id=1, source_target_pairs={{0,8},{8,16},{16,24},{24,32},{32,40},{40,48},{48,56},{56,64},{64,7... | collective-permute-start | bytes 884744 | tf_op jit(solution)/shard_map/ppermute | solution.py:570
  4.6 12.8 %collective-permute-start.1 = (f32[9,32,256]{2,1,0:T(8,128)S(1)}, f32[9,32,256]{2,1,0:T(8,128)S(1)}, u32[]{:S(2)}, u32[]{:S(2)}) collective-permute-start(f32[9,32,256]{2,1,0:T(8,128)S(1)} %pad_maximum_fusion.1), channel_id=1, source_target_pairs={{0,248},{8,0},{16,8},{24,16},{32,24},{40,32},{48,40},{56,48},{64,5... | collective-permute-start | bytes 884744 | tf_op jit(solution)/shard_map/ppermute | solution.py:570
  30.1 5.3 %collective-permute-start.2 = (f32[42,8,256]{2,1,0:T(8,128)S(1)}, f32[42,8,256]{2,1,0:T(8,128)S(1)}, u32[]{:S(2)}, u32[]{:S(2)}) collective-permute-start(f32[42,8,256]{2,1,0:T(8,128)S(1)} %get-tuple-element.26), channel_id=1, source_target_pairs={{0,1},{1,2},{2,3},{3,4},{4,5},{5,6},{6,7},{7,0},{8,9},{9,10},{10,1... | collective-permute-start | bytes 1032200 | tf_op jit(solution)/shard_map/ppermute | solution.py:570
  31.2 7.9 %collective-permute-start.3 = (f32[42,8,256]{2,1,0:T(8,128)S(1)}, f32[42,8,256]{2,1,0:T(8,128)S(1)}, u32[]{:S(2)}, u32[]{:S(2)}) collective-permute-start(f32[42,8,256]{2,1,0:T(8,128)S(1)} %get-tuple-element.27), channel_id=1, source_target_pairs={{0,7},{1,0},{2,1},{3,2},{4,3},{5,4},{6,5},{7,6},{8,15},{9,8},{10,9... | collective-permute-start | bytes 1032200 | tf_op jit(solution)/shard_map/ppermute | solution.py:570
  59.0 1.2 copy-start.2
  60.2 1.2 copy-start.4
  61.4 1.2 copy-start.6
  62.7 1.3 copy-start.8
  64.0 0.7 copy-start.11
  64.6 0.7 copy-start.13
  65.3 7.1 %collective-permute-start.4 = (f32[11,16,128]{2,1,0:T(8,128)S(1)}, f32[11,16,128]{2,1,0:T(8,128)S(1)}, u32[]{:S(2)}, u32[]{:S(2)}) collective-permute-start(f32[11,16,128]{2,1,0:T(8,128)S(1)} %get-tuple-element.30), channel_id=1, source_target_pairs={{0,8},{8,16},{16,24},{24,32},{32,40},{40,48},{48,56},{56,64},{64,7... | collective-permute-start | bytes 270344 | tf_op jit(solution)/shard_map/ppermute | solution.py:570
  65.3 7.1 %collective-permute-start.5 = (f32[11,16,128]{2,1,0:T(8,128)S(1)}, f32[11,16,128]{2,1,0:T(8,128)}, u32[]{:S(2)}, u32[]{:S(2)}) collective-permute-start(f32[11,16,128]{2,1,0:T(8,128)S(1)} %get-tuple-element.31), channel_id=1, source_target_pairs={{0,248},{8,0},{16,8},{24,16},{32,24},{40,32},{48,40},{56,48},{64,5... | collective-permute-start | bytes 270344 | tf_op jit(solution)/shard_map/ppermute | solution.py:570
  72.4 0.6 copy-start.27
  74.9 4.6 %collective-permute-start.6 = (f32[28,16,128]{2,1,0:T(8,128)}, f32[28,16,128]{2,1,0:T(8,128)S(1)}, u32[]{:S(2)}, u32[]{:S(2)}) collective-permute-start(f32[28,16,128]{2,1,0:T(8,128)} %get-tuple-element.32), channel_id=1, source_target_pairs={{0,1},{1,2},{2,3},{3,4},{4,5},{5,6},{6,7},{7,0},{8,9},{9,10},{10,1... | collective-permute-start | bytes 688136 | tf_op jit(solution)/shard_map/ppermute | solution.py:570
  76.2 6.9 %collective-permute-start.7 = (f32[28,16,128]{2,1,0:T(8,128)}, f32[28,16,128]{2,1,0:T(8,128)S(1)}, u32[]{:S(2)}, u32[]{:S(2)}) collective-permute-start(f32[28,16,128]{2,1,0:T(8,128)} %get-tuple-element.33), channel_id=1, source_target_pairs={{0,7},{1,0},{2,1},{3,2},{4,3},{5,4},{6,5},{7,6},{8,15},{9,8},{10,9... | collective-permute-start | bytes 688136 | tf_op jit(solution)/shard_map/ppermute | solution.py:570
  83.1 0.9 copy-start.12
  84.0 0.9 copy-start.14
  84.9 0.9 copy-start.28
  95.8 0.8 copy-start.15
  96.5 0.8 copy-start.17
  97.3 0.8 copy-start.19
  98.1 0.8 copy-start.21
  98.9 0.8 copy-start.23
  99.7 0.8 copy-start.25
  100.4 0.6 copy-start.29
  101.1 6.6 %collective-permute-start.8 = (f32[10,16,128]{2,1,0:T(8,128)S(1)}, f32[10,16,128]{2,1,0:T(8,128)S(1)}, u32[]{:S(2)}, u32[]{:S(2)}) collective-permute-start(f32[10,16,128]{2,1,0:T(8,128)S(1)} %get-tuple-element.35), channel_id=1, source_target_pairs={{0,8},{8,16},{16,24},{24,32},{32,40},{40,48},{48,56},{56,64},{64,7... | collective-permute-start | bytes 245768 | tf_op jit(solution)/shard_map/ppermute | solution.py:570
  101.1 6.6 %collective-permute-start.9 = (f32[10,16,128]{2,1,0:T(8,128)S(1)}, f32[10,16,128]{2,1,0:T(8,128)S(1)}, u32[]{:S(2)}, u32[]{:S(2)}) collective-permute-start(f32[10,16,128]{2,1,0:T(8,128)S(1)} %get-tuple-element.36), channel_id=1, source_target_pairs={{0,248},{8,0},{16,8},{24,16},{32,24},{40,32},{48,40},{56,48},{64,5... | collective-permute-start | bytes 245768 | tf_op jit(solution)/shard_map/ppermute | solution.py:570
  107.7 0.7 copy-start.30
  107.7 0.7 copy-start.31
  110.0 6.9 %collective-permute-start.11 = (f32[28,16,128]{2,1,0:T(8,128)}, f32[28,16,128]{2,1,0:T(8,128)S(1)}, u32[]{:S(2)}, u32[]{:S(2)}) collective-permute-start(f32[28,16,128]{2,1,0:T(8,128)} %pack2.1.ext), channel_id=1, source_target_pairs={{0,7},{1,0},{2,1},{3,2},{4,3},{5,4},{6,5},{7,6},{8,15},{9,8},{10,9... | collective-permute-start | bytes 688136 | tf_op jit(solution)/shard_map/ppermute | solution.py:570
  110.0 6.9 %collective-permute-start.10 = (f32[28,16,128]{2,1,0:T(8,128)}, f32[28,16,128]{2,1,0:T(8,128)S(1)}, u32[]{:S(2)}, u32[]{:S(2)}) collective-permute-start(f32[28,16,128]{2,1,0:T(8,128)} %pack2.1.ext), channel_id=1, source_target_pairs={{0,1},{1,2},{2,3},{3,4},{4,5},{5,6},{6,7},{7,0},{8,9},{9,10},{10,1... | collective-permute-start | bytes 688136 | tf_op jit(solution)/shard_map/ppermute | solution.py:570
  116.9 1.5 copy-start.3
  118.3 1.5 copy-start.5
  119.8 1.5 copy-start.7
  121.3 1.5 copy-start.9
  122.7 0.9 copy-start.10
  123.7 1.0 copy-start.16
  124.7 1.0 copy-start.18
  125.7 1.0 copy-start.20
  126.7 1.0 copy-start.22
  127.7 1.0 copy-start.24
  128.8 1.0 copy-start.26
where the time goes:
time: 167 us; the launch traced here: 166 us
  Pallas kernels  81.9 us (49%)
  local copies, waits for them, and re-layouts  29.5 us (18%)
  waiting for transfers between devices  29.1 us (17%)
  starting transfers between devices  23.2 us (14%)
    pallas_call x1, Pallas kernels, way_up(): pl.pallas_call(up_kernel, in_specs=[vmem] * 9 + [anyw] * 7, out_specs=[vm...  35.7 us
    ppermute x12, waiting for transfers between devices, shift(): lax.ppermute(a, axis, [(i, (i + step) % count) for i in range(count)])  29.1 us
    unnamed x64, local copies, waits for them, and re-layouts  28.4 us
    ppermute x12, starting transfers between devices, shift(): lax.ppermute(a, axis, [(i, (i + step) % count) for i in range(count)])  23.2 us
    pallas_call x1, Pallas kernels, down0(): pl.pallas_call(down0_kernel, in_specs=[vmem] * 6, out_specs=[vmem] * 4 +...  20 us
    pallas_call x1, Pallas kernels, pack0(): pl.pallas_call(pack0_kernel, grid=(1,), in_specs=[own(0), own(3), own(0),...  12.7 us
    pallas_call x1, Pallas kernels, down1(): pl.pallas_call(down1_kernel, in_specs=[vmem] * 6, out_specs=[vmem] * 9, o...  10 us
  transfers between devices with their start and end apart: 12, of which 8 were waited for; matrix products, arithmetic and copies ran while one was open for 0% of the time, Pallas kernels for 0%

commit v1 on v0

--- a/solution.py
+++ b/solution.py
@@ -15,19 +15,19 @@
 
 
 def up_y(a):
-    return pltpu.roll(a, a.shape[0] - 1, 0)
+    return pltpu.roll(a, a.shape[-2] - 1, a.ndim - 2)
 
 
 def dn_y(a):
-    return pltpu.roll(a, 1, 0)
+    return pltpu.roll(a, 1, a.ndim - 2)
 
 
 def up_z(a):
-    return pltpu.roll(a, a.shape[1] - 1, 1)
+    return pltpu.roll(a, a.shape[-1] - 1, a.ndim - 1)
 
 
 def dn_z(a):
-    return pltpu.roll(a, 1, 1)
+    return pltpu.roll(a, 1, a.ndim - 1)
 
 
 def iota(shape, dim):
@@ -62,10 +62,22 @@
     return jnp.where(product > 0.0, 2.0 * product / (a + b), jnp.maximum(a, b))
 
 
-def weights_at(m, m_next, wx_prev, face, outside, full):
-    lane = iota(m.shape, 1)
-    last = m.shape[1] - 1
-    wx = face(m, m_next)
+def blocks(lo, hi, size, work):
+    count, rest = divmod(hi - lo, size)
+
+    def body(i, carry):
+        work(lo + i * size, size)
+        return carry
+
+    lax.fori_loop(0, count, body, 0)
+    if rest:
+        work(hi - rest, rest)
+
+
+def weights_at(m_low, m, m_high, face, outside, full):
+    lane = iota(m.shape, m.ndim - 1)
+    last = m.shape[-1] - 1
+    wx, wx_low = face(m, m_high), face(m_low, m)
     wy = face(m, up_y(m))
     m_up = up_z(m)
     if full:
@@ -74,57 +86,72 @@
     wz_low = dn_z(wz)
     if full:
         wz_low = jnp.where(lane == 0, face(m, jnp.full_like(m, outside)), wz_low)
-    d = (wx + wx_prev) + (wy + dn_y(wy)) + (wz + wz_low)
+    d = (wx + wx_low) + (wy + dn_y(wy)) + (wz + wz_low)
     q = jnp.where(m != outside, OMEGA / d, 0.0)
     if full:
         wz = jnp.where(lane == last, 0.0, wz)
     return wx, wy, wz, d, q
 
 
-def weights_pass(lo, hi, m_ref, w, face, outside, full, first):
+def weights_pass(lo, hi, size, m_ref, w, face, outside, full, first):
     wx_ref, wy_ref, wz_ref, d_ref, q_ref = w
-    start = face(m_ref[lo - 1], m_ref[lo])
-    wx_ref[lo - 1] = start
-
-    def body(j, wx_prev):
-        wx, wy, wz, d, q = weights_at(m_ref[j], m_ref[j + 1], wx_prev, face, outside, full)
-        wx_ref[j] = wx
-        wy_ref[j] = wy
-        wz_ref[j] = wz
-        d_ref[j] = d
-        q_ref[j] = q
-        first(j, q)
-        return wx
-
-    lax.fori_loop(lo, hi, body, start)
-
-
-def flow(j, p, p_ref, w):
+    wx_ref[lo - 1] = face(m_ref[lo - 1], m_ref[lo])
+
+    def work(j, n):
+        here = pl.ds(j, n)
+        wx, wy, wz, d, q = weights_at(
+            m_ref[pl.ds(j - 1, n)], m_ref[here], m_ref[pl.ds(j + 1, n)], face, outside, full
+        )
+        start = first(here, q)
+        wx_ref[here] = wx
+        wy_ref[here] = wy
+        wz_ref[here] = wz
+        d_ref[here] = d
+        q_ref[here] = q
+        start()
+
+    blocks(lo, hi, size, work)
+
+
+def flow(j, n, p, p_ref, w):
     wx_ref, wy_ref, wz_ref = w[:3]
-    wy, wz = wy_ref[j], wz_ref[j]
-    along_x = wx_ref[j] * p_ref[j + 1] + wx_ref[j - 1] * p_ref[j - 1]
+    here, above, below = pl.ds(j, n), pl.ds(j + 1, n), pl.ds(j - 1, n)
+    wy, wz = wy_ref[here], wz_ref[here]
+    along_x = wx_ref[here] * p_ref[above] + wx_ref[below] * p_ref[below]
     along_y = wy * up_y(p) + dn_y(wy * p)
     along_z = wz * up_z(p) + dn_z(wz * p)
     return along_x + along_y + along_z
 
 
-def sweep(lo, hi, p_ref, out_ref, s_ref, w):
-    def body(j, carry):
-        p = p_ref[j]
-        out_ref[j] = KEEP * p + w[4][j] * (s_ref[j] + flow(j, p, p_ref, w))
-        return carry
-
-    lax.fori_loop(lo, hi, body, 0)
-
-
-def remainder(lo, hi, p_ref, out_ref, s_ref, w):
-    def body(j, carry):
-        p = p_ref[j]
-        r = s_ref[j] + flow(j, p, p_ref, w) - w[3][j] * p
-        out_ref[j] = jnp.where(w[4][j] > 0.0, r, 0.0)
-        return carry
-
-    lax.fori_loop(lo, hi, body, 0)
+def sweep(lo, hi, size, p_ref, out_ref, s_ref, w):
+    def work(j, n):
+        here = pl.ds(j, n)
+        p = p_ref[here]
+        out_ref[here] = KEEP * p + w[4][here] * (s_ref[here] + flow(j, n, p, p_ref, w))
+
+    blocks(lo, hi, size, work)
+
+
+def remainder(lo, hi, size, p_ref, out_ref, s_ref, w):
+    def work(j, n):
+        here = pl.ds(j, n)
+        p = p_ref[here]
+        r = s_ref[here] + flow(j, n, p, p_ref, w) - w[3][here] * p
+        out_ref[here] = jnp.where(w[4][here] > 0.0, r, 0.0)
+
+    blocks(lo, hi, size, work)
+
+
+def first_sweep(out_ref, s_ref):
+    def first(here, q):
+        p = q * s_ref[here]
+
+        def start():
+            out_ref[here] = p
+
+        return start
+
+    return first
 
 
 def restrict_x(r_ref, j):
@@ -161,20 +188,19 @@
         c_ref[X0 : X0 + 32] = own_f[...].astype(F32)
         is_source = sub < 4 if row == 3 else sub >= 4
 
-        def message(j, s, out_ref=out_ref, is_source=is_source):
-            out_ref[j] = jnp.where(is_source, s, pltpu.roll(c_ref[j], 4, 0))
-
-        message(0, s_ref[0])
-        message(N0 - 1, s_ref[N0 - 1])
-
-        def body(j, wx_prev, row=row, message=message):
-            c = c_ref[j]
-            wx, _, _, _, q = weights_at(c, c_ref[j + 1], wx_prev, face_code, OUT, True)
-            s = s_ref[j]
-            message(j, jnp.where(sub == row, q * s, s))
-            return wx
-
-        lax.fori_loop(1, N0 - 1, body, face_code(c_ref[0], c_ref[1]))
+        def message(here, s, out_ref=out_ref, is_source=is_source):
+            out_ref[here] = jnp.where(is_source, s, pltpu.roll(c_ref[here], 4, 1))
+
+        message(pl.ds(0, 1), s_ref[0:1])
+        message(pl.ds(N0 - 1, 1), s_ref[N0 - 1 :])
+
+        def work(j, n, row=row, message=message):
+            here = pl.ds(j, n)
+            q = weights_at(c_ref[pl.ds(j - 1, n)], c_ref[here], c_ref[pl.ds(j + 1, n)], face_code, OUT, True)[-1]
+            s = s_ref[here]
+            message(here, jnp.where(sub == row, q * s, s))
+
+        blocks(1, N0 - 1, 10, work)
 
 
 def pack0(source, phase, xlo, xhi):
@@ -189,7 +215,7 @@
         out_specs=[whole, whole],
         out_shape=[shape, shape],
         scratch_shapes=[pltpu.VMEM((N0, 8, 256), F32)] * 2,
-        compiler_params=pltpu.CompilerParams(vmem_limit_bytes=16 * MIB),
+        compiler_params=pltpu.CompilerParams(vmem_limit_bytes=6 * MIB),
         name="pack0",
     )(source, source, phase, phase, xlo, xlo, xhi, xhi)
 
@@ -199,14 +225,10 @@
 N3 = 12
 
 
-def copies(pairs, sems):
-    return [pltpu.make_async_copy(a, b, sems.at[k]) for k, (a, b) in enumerate(pairs)]
-
-
 def down0_kernel(
     s_in, f_in, xlo, xhi, ylo, yhi,
-    src1, mob1, dn1, upw1, wx_o, wy_o, wz_o, d_o, q_o, s_o, p_o,
-    s_ref, c_ref, wx, wy, wz, d_ref, q_ref, p1, p2, r_ref, t_ref, sems,
+    src1, mob1, dn1, upw1, wx, wy, wz, q_ref, s_ref, p2,
+    c_ref, d_ref, p1, r_ref, t_ref,
 ):
     low_x, high_x = edge("gx")
     low_y, high_y = edge("gy")
@@ -221,38 +243,36 @@
     above = sub < 4
     outer = (above & high_y) | (~above & low_y)
 
-    def tile4(j, carry):
-        hi, lo = yhi[j], ylo[j]
-        s_ref[j, 32:] = jnp.where(outer, 0.0, jnp.where(above, hi, lo))
-        c_ref[j, 32:] = jnp.where(outer, OUT, pltpu.roll(jnp.where(above, lo, hi), 4, 0))
-        return carry
-
-    lax.fori_loop(0, N0, tile4, 0)
-
-    def own_planes(j, carry):
-        s_ref[j + X0, :32] = s_in[j]
-        c_ref[j + X0, :32] = f_in[j].astype(F32)
-        return carry
-
-    lax.fori_loop(0, 32, own_planes, 0)
+    def tile4(j, n):
+        here = pl.ds(j, n)
+        hi, lo = yhi[here], ylo[here]
+        s_ref[here, 32:] = jnp.where(outer, 0.0, jnp.where(above, hi, lo))
+        c_ref[here, 32:] = jnp.where(outer, OUT, pltpu.roll(jnp.where(above, lo, hi), 4, 1))
+
+    blocks(0, N0, 7, tile4)
+
+    def own_planes(j, n):
+        s_ref[pl.ds(j + X0, n), :32] = s_in[pl.ds(j, n)]
+        c_ref[pl.ds(j + X0, n), :32] = f_in[pl.ds(j, n)].astype(F32)
+
+    blocks(0, 32, 4, own_planes)
 
     w = (wx, wy, wz, d_ref, q_ref)
     row = iota((40, 256), 0)
     seam = (row == 35) | (row == 36)
 
-    def first(j, q):
-        s = s_ref[j]
-        p1[j] = jnp.where(seam, s, q * s)
-
-    weights_pass(1, N0 - 1, c_ref, w, face_code, OUT, True, first)
-    state = copies(
-        [(wx, wx_o), (wy, wy_o), (wz, wz_o), (d_ref, d_o), (q_ref, q_o), (s_ref, s_o), (p2, p_o)], sems
-    )
-    for copy in state[:-1]:
-        copy.start()
-    sweep(2, N0 - 2, p1, p2, s_ref, w)
-    state[-1].start()
-    remainder(4, N0 - 4, p2, r_ref, s_ref, w)
+    def first(here, q):
+        s = s_ref[here]
+        p = jnp.where(seam, s, q * s)
+
+        def start():
+            p1[here] = p
+
+        return start
+
+    weights_pass(1, N0 - 1, 4, c_ref, w, face_code, OUT, True, first)
+    sweep(2, N0 - 2, 4, p1, p2, s_ref, w)
+    remainder(4, N0 - 4, 4, p2, r_ref, s_ref, w)
 
     fine_z, coarse_z = iota((256, 128), 0), iota((256, 128), 1)
     fine_y = ring(iota((16, 40), 1), 36, 40)
@@ -262,20 +282,21 @@
     ry = restrict_weight(fine_y - 2 * coarse_y)
     my = pair_weight(fine_y - 2 * coarse_y)
 
-    def halve(k, carry):
-        t_ref[pl.ds(pl.multiple_of(k * 40, 8), 40)] = restrict_x(r_ref, 2 * k + 4)
-        return carry
-
-    lax.fori_loop(0, 16, halve, 0)
+    def halve(k, n):
+        for i in range(n):
+            t_ref[pl.ds(pl.multiple_of((k + i) * 40, 8), 40)] = restrict_x(r_ref, 2 * (k + i) + 4)
+
+    blocks(0, 16, 4, halve)
     coarse = dot(t_ref[...], rz)
     for k in range(16):
         src1[k] = dot(ry, coarse[k * 40 : k * 40 + 40])
 
-    def count(k, carry):
-        t_ref[pl.ds(pl.multiple_of(k * 40, 8), 40)] = c_ref[2 * k + X0] + c_ref[2 * k + X0 + 1]
-        return carry
-
-    lax.fori_loop(0, 16, count, 0)
+    def count(k, n):
+        for i in range(n):
+            j = 2 * (k + i) + X0
+            t_ref[pl.ds(pl.multiple_of((k + i) * 40, 8), 40)] = c_ref[j] + c_ref[j + 1]
+
+    blocks(0, 16, 4, count)
     water = dot(t_ref[...], mz)
     for k in range(16):
         n = dot(my, water[k * 40 : k * 40 + 40])
@@ -284,24 +305,20 @@
     dn1[5:] = mob1[:6]
     upw1[:5] = src1[11:]
     upw1[5:] = mob1[10:]
-    for copy in state:
-        copy.wait()
 
 
 def down0(source, phase, xlo, xhi, ylo, yhi):
-    big = jax.ShapeDtypeStruct((N0, 40, 256), F32)
+    big = pltpu.VMEM((N0, 40, 256), F32)
     own1 = jax.ShapeDtypeStruct((16, 16, 128), F32)
     msg1 = jax.ShapeDtypeStruct((11, 16, 128), F32)
     vmem = pl.BlockSpec(memory_space=pltpu.VMEM)
-    anyw = pl.BlockSpec(memory_space=pl.ANY)
     return pl.pallas_call(
         down0_kernel,
         in_specs=[vmem] * 6,
-        out_specs=[vmem] * 4 + [anyw] * 7,
-        out_shape=[own1, own1, msg1, msg1] + [big] * 7,
-        scratch_shapes=[pltpu.VMEM((N0, 40, 256), F32)] * 10
-        + [pltpu.VMEM((640, 256), F32), pltpu.SemaphoreType.DMA((7,))],
-        compiler_params=pltpu.CompilerParams(vmem_limit_bytes=40 * MIB),
+        out_specs=[vmem] * 10,
+        out_shape=[own1, own1, msg1, msg1] + [big] * 6,
+        scratch_shapes=[pltpu.VMEM((N0, 40, 256), F32)] * 4 + [pltpu.VMEM((640, 256), F32)],
+        compiler_params=pltpu.CompilerParams(vmem_limit_bytes=16 * MIB),
         name="down0",
     )(source, phase, xlo, xhi, ylo, yhi)
 
@@ -327,6 +344,7 @@
         in_specs=[vmem] * 4,
         out_specs=[vmem] * 2,
         out_shape=[shape, shape],
+        compiler_params=pltpu.CompilerParams(vmem_limit_bytes=4 * MIB),
         name="pack1",
     )(src, mob, xlo, xhi)
 
@@ -353,12 +371,9 @@
     m_ref[:, 24:] = blank(low_y, ylo[:, 8:], 0.0)
     w = (wx, wy, wz, d_ref, q_ref)
 
-    def first(j, q):
-        p1[j] = q * s_ref[j]
-
-    weights_pass(1, N1 - 1, m_ref, w, face_mean, 0.0, True, first)
-    sweep(2, N1 - 2, p1, p2, s_ref, w)
-    remainder(3, N1 - 3, p2, r_ref, s_ref, w)
+    weights_pass(1, N1 - 1, 13, m_ref, w, face_mean, 0.0, True, first_sweep(p1, s_ref))
+    sweep(2, N1 - 2, 12, p1, p2, s_ref, w)
+    remainder(3, N1 - 3, 11, p2, r_ref, s_ref, w)
 
     lane_in, lane_out = iota((128, 128), 0), iota((128, 128), 1)
     rz = jnp.where(lane_out < 64, restrict_weight(lane_in - 2 * lane_out), 0.0)
@@ -387,16 +402,15 @@
 
 
 def down1(src, mob, xlo, xhi, ylo, yhi):
-    big = jax.ShapeDtypeStruct((N1, 32, 128), F32)
     vmem = pl.BlockSpec(memory_space=pltpu.VMEM)
     return pl.pallas_call(
         down1_kernel,
         in_specs=[vmem] * 6,
         out_specs=[vmem] * 9,
-        out_shape=[jax.ShapeDtypeStruct((k, 16, 128), F32) for k in (8, 10, 10)] + [big] * 6,
+        out_shape=[jax.ShapeDtypeStruct((k, 16, 128), F32) for k in (8, 10, 10)] + [pltpu.VMEM((N1, 32, 128), F32)] * 6,
         scratch_shapes=[pltpu.VMEM((N1, 32, 128), F32)] * 4
         + [pltpu.VMEM((384, 128), F32), pltpu.VMEM((12, 16, 128), F32)],
-        compiler_params=pltpu.CompilerParams(vmem_limit_bytes=16 * MIB),
+        compiler_params=pltpu.CompilerParams(vmem_limit_bytes=8 * MIB),
         name="down1",
     )(src, mob, xlo, xhi, ylo, yhi)
 
@@ -415,25 +429,21 @@
         in_specs=[vmem] * 3,
         out_specs=vmem,
         out_shape=jax.ShapeDtypeStruct((N2, 16, 128), F32),
+        compiler_params=pltpu.CompilerParams(vmem_limit_bytes=4 * MIB),
         name="pack2",
     )(own, xlo, xhi)
 
 
 def up_kernel(
     ext, ylo, yhi, s1, wx1, wy1, wz1, q1, down1_ref,
-    wx0_h, wy0_h, wz0_h, d0_h, q0_h, s0_h, p0_h,
+    wx0, wy0, wz0, q0, s0, down0_ref,
     scaled, residual,
-    wx0, wy0, wz0, d0, q0, s0, pa0, pb0,
+    pa0, pb0,
     pa1, pb1,
     s2, m2, wx2, wy2, wz2, d2, q2, pa2, pb2, r2,
     s3, m3, wx3, wy3, wz3, d3, q3, pa3, pb3,
-    t_ref, u_ref, v_ref, sems,
+    t_ref, u_ref, v_ref,
 ):
-    state = copies(
-        [(wx0_h, wx0), (wy0_h, wy0), (wz0_h, wz0), (d0_h, d0), (q0_h, q0), (s0_h, s0), (p0_h, pa0)], sems
-    )
-    for copy in state:
-        copy.start()
     low_y, high_y = edge("gy")
 
     lane8, sub8 = iota((8, 128), 1), iota((8, 128), 0)
@@ -454,12 +464,9 @@
     lax.fori_loop(0, N2, unpack, 0)
     w2 = (wx2, wy2, wz2, d2, q2)
 
-    def first2(j, q):
-        pa2[j] = q * s2[j]
-
-    weights_pass(1, N2 - 1, m2, w2, face_mean, 0.0, False, first2)
-    sweep(2, N2 - 2, pa2, pb2, s2, w2)
-    remainder(3, N2 - 3, pb2, r2, s2, w2)
+    weights_pass(1, N2 - 1, 13, m2, w2, face_mean, 0.0, False, first_sweep(pa2, s2))
+    sweep(2, N2 - 2, 12, pa2, pb2, s2, w2)
+    remainder(3, N2 - 3, 11, pb2, r2, s2, w2)
 
     lane_in, lane_out = iota((128, 128), 0), iota((128, 128), 1)
     down_z = lane_in - 2 * lane_out
@@ -482,11 +489,8 @@
             s3[k] = dot(ry, coarse[(k - 1) * 32 : k * 32])
     w3 = (wx3, wy3, wz3, d3, q3)
 
-    def first3(j, q):
-        pa3[j] = q * s3[j]
-
-    weights_pass(1, N3 - 1, m3, w3, face_mean, 0.0, False, first3)
-    sweep(2, N3 - 2, pa3, pb3, s3, w3)
+    weights_pass(1, N3 - 1, 10, m3, w3, face_mean, 0.0, False, first_sweep(pa3, s3))
+    sweep(2, N3 - 2, 8, pa3, pb3, s3, w3)
 
     pz = pair_weight(lane_out - 2 * lane_in)
     pz = jnp.where(lane_in < 32, pz, 0.0)
@@ -498,8 +502,8 @@
         rise = u_ref[k * 32 : k * 32 + 32]
         pb2[2 * k + 6] = pb2[2 * k + 6] + rise
         pb2[2 * k + 7] = pb2[2 * k + 7] + rise
-    sweep(7, 21, pb2, pa2, s2, w2)
-    sweep(8, 20, pa2, pb2, s2, w2)
+    sweep(7, 21, 7, pb2, pa2, s2, w2)
+    sweep(8, 20, 12, pa2, pb2, s2, w2)
 
     pz = pair_weight(lane_out - 2 * lane_in)
     py = pair_weight(ring(iota((32, 32), 0), 24, 32) - 2 * ring(iota((32, 32), 1), 20, 32))
@@ -511,56 +515,55 @@
         pa1[2 * k + 2] = down1_ref[2 * k + 2] + rise
         pa1[2 * k + 3] = down1_ref[2 * k + 3] + rise
     w1 = (wx1, wy1, wz1, None, q1)
-    sweep(3, 25, pa1, pb1, s1, w1)
-    sweep(4, 24, pb1, pa1, s1, w1)
+    sweep(3, 25, 11, pa1, pb1, s1, w1)
+    sweep(4, 24, 10, pb1, pa1, s1, w1)
 
     pz = pair_weight(iota((128, 256), 1) - 2 * iota((128, 256), 0))
     py = pair_weight(ring(iota((40, 32), 0), 36, 40) - 2 * ring(iota((40, 32), 1), 24, 32))
     for k in range(20):
         t_ref[k * 40 : k * 40 + 40] = dot(py, pa1[k + 4])
     v_ref[...] = dot(t_ref[...], pz)
-    for copy in state:
-        copy.wait()
-
-    def rise0(j, carry):
-        k = (j - 1) // 2
-        pa0[j] = pa0[j] + v_ref[pl.ds(pl.multiple_of(k * 40, 8), 40)]
-        return carry
-
-    lax.fori_loop(2, N0 - 2, rise0, 0)
-    w0 = (wx0, wy0, wz0, d0, q0)
-    sweep(3, N0 - 3, pa0, pb0, s0, w0)
-    sweep(4, N0 - 4, pb0, pa0, s0, w0)
-
-    def last(j, carry):
-        p = pa0[j]
-        dp = d0[j] * p
-        scaled[j - X0] = dp[:32]
-        residual[j - X0] = (s0[j] + flow(j, p, pa0, w0) - dp)[:32]
-        return carry
-
-    lax.fori_loop(X0, X0 + 32, last, 0)
+
+    def rise0(k, n):
+        for i in range(n):
+            rise = v_ref[pl.ds(pl.multiple_of((k + i) * 40, 8), 40)]
+            for j in (2 * (k + i) + 1, 2 * (k + i) + 2):
+                pa0[j] = down0_ref[j] + rise
+
+    pa0[2] = down0_ref[2] + v_ref[:40]
+    blocks(1, 19, 3, rise0)
+    pa0[N0 - 3] = down0_ref[N0 - 3] + v_ref[760:]
+    w0 = (wx0, wy0, wz0, None, q0)
+    sweep(3, N0 - 3, 4, pa0, pb0, s0, w0)
+    sweep(4, N0 - 4, 4, pb0, pa0, s0, w0)
+
+    def last(j, n):
+        here, out = pl.ds(j, n), pl.ds(j - X0, n)
+        p = pa0[here]
+        dp = (OMEGA / q0[here]) * p
+        scaled[out] = dp[:, :32]
+        residual[out] = (s0[here] + flow(j, n, p, pa0, w0) - dp)[:, :32]
+
+    blocks(X0, X0 + 32, 4, last)
 
 
 def way_up(ext, ylo, yhi, level1, level0):
     vmem = pl.BlockSpec(memory_space=pltpu.VMEM)
-    anyw = pl.BlockSpec(memory_space=pl.ANY)
     shape = jax.ShapeDtypeStruct((32, 32, 256), F32)
     buf = lambda count, *shape: [pltpu.VMEM(shape, F32)] * count
     return pl.pallas_call(
         up_kernel,
-        in_specs=[vmem] * 9 + [anyw] * 7,
+        in_specs=[vmem] * 15,
         out_specs=[vmem] * 2,
         out_shape=[shape, shape],
-        scratch_shapes=buf(8, N0, 40, 256)
+        scratch_shapes=buf(2, N0, 40, 256)
         + buf(2, N1, 32, 128)
         + buf(10, N2, 32, 128)
         + buf(9, N3, 16, 128)
         + buf(1, 800, 128)
         + buf(1, 384, 128)
-        + buf(1, 800, 256)
-        + [pltpu.SemaphoreType.DMA((7,))],
-        compiler_params=pltpu.CompilerParams(vmem_limit_bytes=40 * MIB),
+        + buf(1, 800, 256),
+        compiler_params=pltpu.CompilerParams(vmem_limit_bytes=20 * MIB),
         name="way_up",
     )(ext, ylo, yhi, *level1, *level0)
 

time: 167 us -> 86 us (0.51)
  Pallas kernels: 81.9 us -> 30.2 us
  local copies, waits for them, and re-layouts: 29.5 us -> 1.14 us
    pallas_call x2, Pallas kernels: 55.7 us -> 25.6 us  [the longest x1 14.9 us: way_up(): pl.pallas_call(up_kernel, in_specs=[vmem] * 15, out_specs=[vmem] * 2, out...]
    unnamed x64 -> x4, local copies, waits for them, and re-layouts: 28.4 us -> 0.01 us
    pallas_call x1, Pallas kernels: 12.7 us -> 1.75 us  [pack0(): pl.pallas_call(pack0_kernel, grid=(1,), in_specs=[own(0), own(3), own(0),...]
    pallas_call x1, Pallas kernels: 10 us -> 2.79 us  [down1(): pl.pallas_call(down1_kernel, in_specs=[vmem] * 6, out_specs=[vmem] * 9, o...]
    pallas_call x1, Pallas kernels: 1.85 us -> 0.04 us  [pack1(): pl.pallas_call(pack1_kernel, in_specs=[vmem] * 4, out_specs=[vmem] * 2, o...]
where the time goes in v1:
time: 86 us; the launch traced here: 85.2 us
  Pallas kernels  30.2 us (35%)
  waiting for transfers between devices  28.4 us (33%)
  starting transfers between devices  23.7 us (28%)
  local copies, waits for them, and re-layouts  1.14 us (1%)
  other arithmetic  1.06 us (1%)
    ppermute x12, waiting for transfers between devices, shift(): lax.ppermute(a, axis, [(i, (i + step) % count) for i in range(count)])  28.4 us
    ppermute x12, starting transfers between devices, shift(): lax.ppermute(a, axis, [(i, (i + step) % count) for i in range(count)])  23.7 us
    pallas_call x1, Pallas kernels, way_up(): pl.pallas_call(up_kernel, in_specs=[vmem] * 15, out_specs=[vmem] * 2, out...  14.9 us
    pallas_call x1, Pallas kernels, down0(): pl.pallas_call(down0_kernel, in_specs=[vmem] * 6, out_specs=[vmem] * 10,...  10.7 us
    pallas_call x1, Pallas kernels, down1(): pl.pallas_call(down1_kernel, in_specs=[vmem] * 6, out_specs=[vmem] * 9, o...  2.79 us
    pallas_call x1, Pallas kernels, pack0(): pl.pallas_call(pack0_kernel, grid=(1,), in_specs=[own(0), own(3), own(0),...  1.75 us
  transfers between devices with their start and end apart: 12, of which 8 were waited for; matrix products, arithmetic and copies ran while one was open for 0% of the time, Pallas kernels for 0%

profile of v1, /device:TPU:25, one launch (start us, length us, event | category | flops | bytes accessed | tf_op | source)
XLA Modules:
  0.0 85.2 jit_solution(8216371154704953669)
XLA Ops:
  0.6 0.0 copy-start.1
  0.6 0.0 copy-start
  0.7 1.1 %fusion = (f32[4,32,256]{2,1,0:T(8,128)S(1)}, f32[4,32,256]{2,1,0:T(8,128)S(1)}) fusion(f32[32,32,256]{2,1,0:T(8,128)} %s_in.1), kind=kLoop, calls=%fused_computation.4 | loop fusion | bytes 524288 | tf_op jit(solution)/shard_map/slice | solution.py:581
  1.8 1.0 %slice_convert_fusion = (f32[5,32,256]{2,1,0:T(8,128)S(1)}, f32[5,32,256]{2,1,0:T(8,128)S(1)}) fusion(s32[32,32,256]{2,1,0:T(8,128)} %f_in.1), kind=kLoop, calls=%fused_computation.2 | loop fusion | flops 81920 | bytes 655360 | tf_op jit(solution)/shard_map/convert_element_type | solution.py:581
  2.8 1.7 %collective-permute-start = (f32[9,32,256]{2,1,0:T(8,128)S(1)}, f32[9,32,256]{2,1,0:T(8,128)S(1)}, u32[]{:S(2)}, u32[]{:S(2)}) collective-permute-start(f32[9,32,256]{2,1,0:T(8,128)S(1)} %pad_maximum_fusion), channel_id=1, source_target_pairs={{0,8},{8,16},{16,24},{24,32},{32,40},{40,48},{48,56},{56,64},{64,7... | collective-permute-start | bytes 884744 | tf_op jit(solution)/shard_map/ppermute | solution.py:573
  4.6 6.2 %collective-permute-start.1 = (f32[9,32,256]{2,1,0:T(8,128)S(1)}, f32[9,32,256]{2,1,0:T(8,128)S(1)}, u32[]{:S(2)}, u32[]{:S(2)}) collective-permute-start(f32[9,32,256]{2,1,0:T(8,128)S(1)} %pad_maximum_fusion.1), channel_id=1, source_target_pairs={{0,248},{8,0},{16,8},{24,16},{32,24},{40,32},{48,40},{56,48},{64,5... | collective-permute-start | bytes 884744 | tf_op jit(solution)/shard_map/ppermute | solution.py:573
  10.8 6.6 %collective-permute-done.xl_lo.xl_hi.xlo = f32[9,32,256]{2,1,0:T(8,128)S(1)} collective-permute-done((f32[9,32,256]{2,1,0:T(8,128)S(1)}, f32[9,32,256]{2,1,0:T(8,128)S(1)}, u32[]{:S(2)}, u32[]{:S(2)}) %collective-permute-start) | collective-permute-done | bytes 294944 | tf_op jit(solution)/shard_map/ppermute | solution.py:573
  17.4 0.0 collective-permute-done.1.xh_lo.xh_hi.xhi
  17.4 0.0 copy-done.1
  17.4 0.0 copy-done
  17.4 1.7 %pack0.1 = (f32[42,8,256]{2,1,0:T(8,128)S(1)}, f32[42,8,256]{2,1,0:T(8,128)S(1)}) custom-call(f32[32,32,256]{2,1,0:T(8,128)S(1)} %copy-done.1, f32[32,32,256]{2,1,0:T(8,128)S(1)} %copy-done.1, s32[32,32,256]{2,1,0:T(8,128)S(1)} %copy-done, s32[32,32,256]{2,1,0:T(8,128)S(1)} %copy-done, f32[9,32,256]{2,1,0:T(8,128)S(1)} %collective-permute-done.xl_lo.xl_hi.xlo, ...), custom_call_target="tpu_custom_call" | custom-call | tf_op jit(solution)/shard_map/pack0/pallas_call | solution.py:211
  19.2 1.1 %collective-permute-start.2 = (f32[42,8,256]{2,1,0:T(8,128)S(1)}, f32[42,8,256]{2,1,0:T(8,128)S(1)}, u32[]{:S(2)}, u32[]{:S(2)}) collective-permute-start(f32[42,8,256]{2,1,0:T(8,128)S(1)} %get-tuple-element.25), channel_id=1, source_target_pairs={{0,1},{1,2},{2,3},{3,4},{4,5},{5,6},{6,7},{7,0},{8,9},{9,10},{10,1... | collective-permute-start | bytes 1032200 | tf_op jit(solution)/shard_map/ppermute | solution.py:573
  20.3 0.2 collective-permute-start.3
  20.5 4.0 %collective-permute-done.2.ylo = f32[42,8,256]{2,1,0:T(8,128)S(1)} collective-permute-done((f32[42,8,256]{2,1,0:T(8,128)S(1)}, f32[42,8,256]{2,1,0:T(8,128)S(1)}, u32[]{:S(2)}, u32[]{:S(2)}) %collective-permute-start.2) | collective-permute-done | bytes 344096 | tf_op jit(solution)/shard_map/ppermute | solution.py:573
  24.4 3.7 %collective-permute-done.3.yhi = f32[42,8,256]{2,1,0:T(8,128)S(1)} collective-permute-done((f32[42,8,256]{2,1,0:T(8,128)S(1)}, f32[42,8,256]{2,1,0:T(8,128)S(1)}, u32[]{:S(2)}, u32[]{:S(2)}) %collective-permute-start.3) | collective-permute-done | bytes 344096 | tf_op jit(solution)/shard_map/ppermute | solution.py:573
  28.1 10.7 %down0.1 = (f32[16,16,128]{2,1,0:T(8,128)S(1)}, f32[16,16,128]{2,1,0:T(8,128)S(1)}, f32[11,16,128]{2,1,0:T(8,128)S(1)}, f32[11,16,128]{2,1,0:T(8,128)S(1)}, f32[...) custom-call(f32[32,32,256]{2,1,0:T(8,128)S(1)} %copy-done.1, ...), custom_call_target="tpu_custom_call" | custom-call | tf_op jit(solution)/shard_map/down0/pallas_call | solution.py:315
  38.8 0.1 collective-permute-start.4
  38.9 5.0 %collective-permute-start.5 = (f32[11,16,128]{2,1,0:T(8,128)S(1)}, f32[11,16,128]{2,1,0:T(8,128)S(1)}, u32[]{:S(2)}, u32[]{:S(2)}) collective-permute-start(f32[11,16,128]{2,1,0:T(8,128)S(1)} %get-tuple-element.30), channel_id=1, source_target_pairs={{0,248},{8,0},{16,8},{24,16},{32,24},{40,32},{48,40},{56,48},{64,5... | collective-permute-start | bytes 270344 | tf_op jit(solution)/shard_map/ppermute | solution.py:573
  43.9 2.1 %collective-permute-done.4.xlo = f32[11,16,128]{2,1,0:T(8,128)S(1)} collective-permute-done((f32[11,16,128]{2,1,0:T(8,128)S(1)}, f32[11,16,128]{2,1,0:T(8,128)S(1)}, u32[]{:S(2)}, u32[]{:S(2)}) %collective-permute-start.4) | collective-permute-done | bytes 90144 | tf_op jit(solution)/shard_map/ppermute | solution.py:573
  46.0 0.0 collective-permute-done.5.xhi
  46.0 1.4 %collective-permute-start.6 = (f32[28,16,128]{2,1,0:T(8,128)S(1)}, f32[28,16,128]{2,1,0:T(8,128)S(1)}, u32[]{:S(2)}, u32[]{:S(2)}) collective-permute-start(f32[28,16,128]{2,1,0:T(8,128)S(1)} %get-tuple-element.31), channel_id=1, source_target_pairs={{0,1},{1,2},{2,3},{3,4},{4,5},{5,6},{6,7},{7,0},{8,9},{9,10},{10,1... | collective-permute-start | bytes 688136 | tf_op jit(solution)/shard_map/ppermute | solution.py:573
  47.4 0.0 collective-permute-start.7
  47.4 3.0 %collective-permute-done.6.ylo = f32[28,16,128]{2,1,0:T(8,128)S(1)} collective-permute-done((f32[28,16,128]{2,1,0:T(8,128)S(1)}, f32[28,16,128]{2,1,0:T(8,128)S(1)}, u32[]{:S(2)}, u32[]{:S(2)}) %collective-permute-start.6) | collective-permute-done | bytes 229408 | tf_op jit(solution)/shard_map/ppermute | solution.py:573
  50.4 3.7 %collective-permute-done.7.yhi = f32[28,16,128]{2,1,0:T(8,128)S(1)} collective-permute-done((f32[28,16,128]{2,1,0:T(8,128)S(1)}, f32[28,16,128]{2,1,0:T(8,128)S(1)}, u32[]{:S(2)}, u32[]{:S(2)}) %collective-permute-start.7) | collective-permute-done | bytes 229408 | tf_op jit(solution)/shard_map/ppermute | solution.py:573
  54.1 2.8 %down1.1 = (f32[8,16,128]{2,1,0:T(8,128)S(1)}, f32[10,16,128]{2,1,0:T(8,128)S(1)}, f32[10,16,128]{2,1,0:T(8,128)S(1)}, f32[28,32,128]{2,1,0:T(8,128)S(1)}, f32[2...) custom-call(f32[16,16,128]{2,1,0:T(8,128)S(1)} %get-tuple-element.27, ...), custom_call_target="tpu_custom_call" | custom-call | tf_op jit(solution)/shard_map/down1/pallas_call | solution.py:406
  56.8 0.0 collective-permute-start.8
  56.8 5.1 %collective-permute-start.9 = (f32[10,16,128]{2,1,0:T(8,128)S(1)}, f32[10,16,128]{2,1,0:T(8,128)S(1)}, u32[]{:S(2)}, u32[]{:S(2)}) collective-permute-start(f32[10,16,128]{2,1,0:T(8,128)S(1)} %get-tuple-element.35), channel_id=1, source_target_pairs={{0,248},{8,0},{16,8},{24,16},{32,24},{40,32},{48,40},{56,48},{64,5... | collective-permute-start | bytes 245768 | tf_op jit(solution)/shard_map/ppermute | solution.py:573
  62.0 1.6 %collective-permute-done.8.xlo = f32[10,16,128]{2,1,0:T(8,128)S(1)} collective-permute-done((f32[10,16,128]{2,1,0:T(8,128)S(1)}, f32[10,16,128]{2,1,0:T(8,128)S(1)}, u32[]{:S(2)}, u32[]{:S(2)}) %collective-permute-start.8) | collective-permute-done | bytes 81952 | tf_op jit(solution)/shard_map/ppermute | solution.py:573
  63.6 0.0 collective-permute-done.9.xhi
  63.6 0.0 collective-permute-start.11
  63.6 2.9 %collective-permute-start.10 = (f32[28,16,128]{2,1,0:T(8,128)S(1)}, f32[28,16,128]{2,1,0:T(8,128)S(1)}, u32[]{:S(2)}, u32[]{:S(2)}) collective-permute-start(f32[28,16,128]{2,1,0:T(8,128)S(1)} %pack2.1.ext), channel_id=1, source_target_pairs={{0,1},{1,2},{2,3},{3,4},{4,5},{5,6},{6,7},{7,0},{8,9},{9,10},{10,1... | collective-permute-start | bytes 688136 | tf_op jit(solution)/shard_map/ppermute | solution.py:573
  66.6 3.7 %collective-permute-done.11.yhi = f32[28,16,128]{2,1,0:T(8,128)S(1)} collective-permute-done((f32[28,16,128]{2,1,0:T(8,128)S(1)}, f32[28,16,128]{2,1,0:T(8,128)S(1)}, u32[]{:S(2)}, u32[]{:S(2)}) %collective-permute-start.11) | collective-permute-done | bytes 229408 | tf_op jit(solution)/shard_map/ppermute | solution.py:573
  70.3 0.0 collective-permute-done.10.ylo
  70.3 14.9 %way_up.1 = (f32[32,32,256]{2,1,0:T(8,128)}, f32[32,32,256]{2,1,0:T(8,128)}) custom-call(f32[28,16,128]{2,1,0:T(8,128)S(1)} %pack2.1.ext, f32[28,16,128]{2,1,0:T(8,128)S(1)} %collective-permute-done.10.ylo, f32[28,16,128]{2,1,0:T(8,128)S(1)} %collective-permute-done.11.yhi, f32[28,32,128]{2,1,0:T(8,128)S(1)} %get-tuple-element.36.s1, ...), custom_call_target="tpu_custom_call" | custom-call | tf_op jit(solution)/shard_map/way_up/pallas_call | solution.py:554
  (4 shorter events, 0.1 us)
Async XLA Ops:
  0.6 16.8 %copy-start.1 = (f32[32,32,256]{2,1,0:T(8,128)S(1)}, f32[32,32,256]{2,1,0:T(8,128)}, u32[]{:S(2)}) copy-start(f32[32,32,256]{2,1,0:T(8,128)} %s_in.1) | copy-start | bytes 3145732
  0.6 16.8 %copy-start = (s32[32,32,256]{2,1,0:T(8,128)S(1)}, s32[32,32,256]{2,1,0:T(8,128)}, u32[]{:S(2)}) copy-start(s32[32,32,256]{2,1,0:T(8,128)} %f_in.1) | copy-start | bytes 3145732
  2.8 14.6 %collective-permute-start = (f32[9,32,256]{2,1,0:T(8,128)S(1)}, f32[9,32,256]{2,1,0:T(8,128)S(1)}, u32[]{:S(2)}, u32[]{:S(2)}) collective-permute-start(f32[9,32,256]{2,1,0:T(8,128)S(1)} %pad_maximum_fusion), channel_id=1, source_target_pairs={{0,8},{8,16},{16,24},{24,32},{32,40},{40,48},{48,56},{56,64},{64,7... | collective-permute-start | bytes 884744 | tf_op jit(solution)/shard_map/ppermute | solution.py:573
  4.6 12.8 %collective-permute-start.1 = (f32[9,32,256]{2,1,0:T(8,128)S(1)}, f32[9,32,256]{2,1,0:T(8,128)S(1)}, u32[]{:S(2)}, u32[]{:S(2)}) collective-permute-start(f32[9,32,256]{2,1,0:T(8,128)S(1)} %pad_maximum_fusion.1), channel_id=1, source_target_pairs={{0,248},{8,0},{16,8},{24,16},{32,24},{40,32},{48,40},{56,48},{64,5... | collective-permute-start | bytes 884744 | tf_op jit(solution)/shard_map/ppermute | solution.py:573
  19.2 5.3 %collective-permute-start.2 = (f32[42,8,256]{2,1,0:T(8,128)S(1)}, f32[42,8,256]{2,1,0:T(8,128)S(1)}, u32[]{:S(2)}, u32[]{:S(2)}) collective-permute-start(f32[42,8,256]{2,1,0:T(8,128)S(1)} %get-tuple-element.25), channel_id=1, source_target_pairs={{0,1},{1,2},{2,3},{3,4},{4,5},{5,6},{6,7},{7,0},{8,9},{9,10},{10,1... | collective-permute-start | bytes 1032200 | tf_op jit(solution)/shard_map/ppermute | solution.py:573
  20.3 7.9 %collective-permute-start.3 = (f32[42,8,256]{2,1,0:T(8,128)S(1)}, f32[42,8,256]{2,1,0:T(8,128)S(1)}, u32[]{:S(2)}, u32[]{:S(2)}) collective-permute-start(f32[42,8,256]{2,1,0:T(8,128)S(1)} %get-tuple-element.26), channel_id=1, source_target_pairs={{0,7},{1,0},{2,1},{3,2},{4,3},{5,4},{6,5},{7,6},{8,15},{9,8},{10,9... | collective-permute-start | bytes 1032200 | tf_op jit(solution)/shard_map/ppermute | solution.py:573
  38.8 7.2 %collective-permute-start.4 = (f32[11,16,128]{2,1,0:T(8,128)S(1)}, f32[11,16,128]{2,1,0:T(8,128)S(1)}, u32[]{:S(2)}, u32[]{:S(2)}) collective-permute-start(f32[11,16,128]{2,1,0:T(8,128)S(1)} %get-tuple-element.29), channel_id=1, source_target_pairs={{0,8},{8,16},{16,24},{24,32},{32,40},{40,48},{48,56},{56,64},{64,7... | collective-permute-start | bytes 270344 | tf_op jit(solution)/shard_map/ppermute | solution.py:573
  38.9 7.1 %collective-permute-start.5 = (f32[11,16,128]{2,1,0:T(8,128)S(1)}, f32[11,16,128]{2,1,0:T(8,128)S(1)}, u32[]{:S(2)}, u32[]{:S(2)}) collective-permute-start(f32[11,16,128]{2,1,0:T(8,128)S(1)} %get-tuple-element.30), channel_id=1, source_target_pairs={{0,248},{8,0},{16,8},{24,16},{32,24},{40,32},{48,40},{56,48},{64,5... | collective-permute-start | bytes 270344 | tf_op jit(solution)/shard_map/ppermute | solution.py:573
  46.0 4.3 %collective-permute-start.6 = (f32[28,16,128]{2,1,0:T(8,128)S(1)}, f32[28,16,128]{2,1,0:T(8,128)S(1)}, u32[]{:S(2)}, u32[]{:S(2)}) collective-permute-start(f32[28,16,128]{2,1,0:T(8,128)S(1)} %get-tuple-element.31), channel_id=1, source_target_pairs={{0,1},{1,2},{2,3},{3,4},{4,5},{5,6},{6,7},{7,0},{8,9},{9,10},{10,1... | collective-permute-start | bytes 688136 | tf_op jit(solution)/shard_map/ppermute | solution.py:573
  47.4 6.7 %collective-permute-start.7 = (f32[28,16,128]{2,1,0:T(8,128)S(1)}, f32[28,16,128]{2,1,0:T(8,128)S(1)}, u32[]{:S(2)}, u32[]{:S(2)}) collective-permute-start(f32[28,16,128]{2,1,0:T(8,128)S(1)} %get-tuple-element.32), channel_id=1, source_target_pairs={{0,7},{1,0},{2,1},{3,2},{4,3},{5,4},{6,5},{7,6},{8,15},{9,8},{10,9... | collective-permute-start | bytes 688136 | tf_op jit(solution)/shard_map/ppermute | solution.py:573
  56.8 6.7 %collective-permute-start.8 = (f32[10,16,128]{2,1,0:T(8,128)S(1)}, f32[10,16,128]{2,1,0:T(8,128)S(1)}, u32[]{:S(2)}, u32[]{:S(2)}) collective-permute-start(f32[10,16,128]{2,1,0:T(8,128)S(1)} %get-tuple-element.34), channel_id=1, source_target_pairs={{0,8},{8,16},{16,24},{24,32},{32,40},{40,48},{48,56},{56,64},{64,7... | collective-permute-start | bytes 245768 | tf_op jit(solution)/shard_map/ppermute | solution.py:573
  56.8 6.7 %collective-permute-start.9 = (f32[10,16,128]{2,1,0:T(8,128)S(1)}, f32[10,16,128]{2,1,0:T(8,128)S(1)}, u32[]{:S(2)}, u32[]{:S(2)}) collective-permute-start(f32[10,16,128]{2,1,0:T(8,128)S(1)} %get-tuple-element.35), channel_id=1, source_target_pairs={{0,248},{8,0},{16,8},{24,16},{32,24},{40,32},{48,40},{56,48},{64,5... | collective-permute-start | bytes 245768 | tf_op jit(solution)/shard_map/ppermute | solution.py:573
  63.6 6.7 %collective-permute-start.11 = (f32[28,16,128]{2,1,0:T(8,128)S(1)}, f32[28,16,128]{2,1,0:T(8,128)S(1)}, u32[]{:S(2)}, u32[]{:S(2)}) collective-permute-start(f32[28,16,128]{2,1,0:T(8,128)S(1)} %pack2.1.ext), channel_id=1, source_target_pairs={{0,7},{1,0},{2,1},{3,2},{4,3},{5,4},{6,5},{7,6},{8,15},{9,8},{10,9... | collective-permute-start | bytes 688136 | tf_op jit(solution)/shard_map/ppermute | solution.py:573
  63.6 6.6 %collective-permute-start.10 = (f32[28,16,128]{2,1,0:T(8,128)S(1)}, f32[28,16,128]{2,1,0:T(8,128)S(1)}, u32[]{:S(2)}, u32[]{:S(2)}) collective-permute-start(f32[28,16,128]{2,1,0:T(8,128)S(1)} %pack2.1.ext), channel_id=1, source_target_pairs={{0,1},{1,2},{2,3},{3,4},{4,5},{5,6},{6,7},{7,0},{8,9},{9,10},{10,1... | collective-permute-start | bytes 688136 | tf_op jit(solution)/shard_map/ppermute | solution.py:573

commit v2 on v1

v2 whole, which is shorter than its diff:
```python
import jax
import jax.numpy as jnp
from jax import lax
from jax.experimental import pallas as pl
from jax.experimental.pallas import tpu as pltpu
from jax.sharding import PartitionSpec as P

OMEGA = 0.8
KEEP = 0.2
WATER = 0.001
MIXED = 2.0 * WATER / (1.0 + WATER)
OUT = 0.25
F32 = jnp.float32
MIB = 1024 * 1024


def up_y(a):
    return pltpu.roll(a, a.shape[-2] - 1, a.ndim - 2)


def dn_y(a):
    return pltpu.roll(a, 1, a.ndim - 2)


def up_z(a):
    return pltpu.roll(a, a.shape[-1] - 1, a.ndim - 1)


def dn_z(a):
    return pltpu.roll(a, 1, a.ndim - 1)


def iota(shape, dim):
    return lax.broadcasted_iota(jnp.int32, shape, dim)


def ring(row, cut, rows):
    return jnp.where(row < cut, row, row - rows)


def restrict_weight(offset):
    near = (offset == 0) | (offset == 1)
    far = (offset == -1) | (offset == 2)
    return jnp.where(near, 0.375, jnp.where(far, 0.125, 0.0)).astype(F32)


def pair_weight(offset):
    return jnp.where((offset == 0) | (offset == 1), 1.0, 0.0).astype(F32)


def dot(a, b):
    return jnp.dot(a, b, precision=lax.Precision.HIGHEST, preferred_element_type=F32)


def face_code(a, b):
    s = a + b
    return jnp.where(s < 0.75, 1.0, jnp.where(s < 1.1, MIXED, WATER)).astype(F32)


def face_mean(a, b):
    product = a * b
    return jnp.where(product > 0.0, 2.0 * product / (a + b), jnp.maximum(a, b))


def blocks(lo, hi, size, work):
    count, rest = divmod(hi - lo, size)
    if count == 1:
        work(lo, size)
    elif count:

        def body(i, carry):
            work(lo + i * size, size)
            return carry

        lax.fori_loop(0, count, body, 0)
    if rest:
        work(hi - rest, rest)


def planes(lo, hi, size, plane, refs):
    def work(j, n):
        results = [plane(j + i) for i in range(n)]
        for i, values in enumerate(results):
            for ref, value in zip(refs, values):
                ref[j + i] = value

    blocks(lo, hi, size, work)


def weights_at(m_low, m, m_high, face, outside, full):
    lane = iota(m.shape, m.ndim - 1)
    last = m.shape[-1] - 1
    wx, wx_low = face(m, m_high), face(m_low, m)
    wy = face(m, up_y(m))
    m_up = up_z(m)
    if full:
        m_up = jnp.where(lane == last, outside, m_up)
    wz = face(m, m_up)
    wz_low = dn_z(wz)
    if full:
        wz_low = jnp.where(lane == 0, face(m, jnp.full_like(m, outside)), wz_low)
    d = (wx + wx_low) + (wy + dn_y(wy)) + (wz + wz_low)
    q = jnp.where(m != outside, OMEGA / d, 0.0)
    if full:
        wz = jnp.where(lane == last, 0.0, wz)
    return wx, wy, wz, q


def weights_pass(lo, hi, size, m_ref, w, s_ref, p_ref, face, outside, full):
    w[0][lo - 1] = face(m_ref[lo - 1], m_ref[lo])

    def plane(j):
        wx, wy, wz, q = weights_at(m_ref[j - 1], m_ref[j], m_ref[j + 1], face, outside, full)
        return wx, wy, wz, q, q * s_ref[j]

    planes(lo, hi, size, plane, (*w, p_ref))


def flow(j, p, p_ref, w):
    wx_ref, wy_ref, wz_ref = w[:3]
    wy, wz = wy_ref[j], wz_ref[j]
    along_x = wx_ref[j] * p_ref[j + 1] + wx_ref[j - 1] * p_ref[j - 1]
    along_y = wy * up_y(p) + dn_y(wy * p)
    along_z = wz * up_z(p) + dn_z(wz * p)
    return along_x + along_y + along_z


def sweep(lo, hi, size, p_ref, out_ref, s_ref, w):
    def plane(j):
        p = p_ref[j]
        return (KEEP * p + w[3][j] * (s_ref[j] + flow(j, p, p_ref, w)),)

    planes(lo, hi, size, plane, (out_ref,))


def remainder(lo, hi, size, p_ref, out_ref, s_ref, w):
    def plane(j):
        p, q = p_ref[j], w[3][j]
        r = s_ref[j] + flow(j, p, p_ref, w) - (OMEGA / q) * p
        return (jnp.where(q > 0.0, r, 0.0),)

    planes(lo, hi, size, plane, (out_ref,))


def restrict_x(r_ref, j):
    return (r_ref[j] + r_ref[j + 3]) * 0.125 + (r_ref[j + 1] + r_ref[j + 2]) * 0.375


def edge(axis):
    i = lax.axis_index(axis)
    return i == 0, i == lax.axis_size(axis) - 1


def blank(flag, value, other):
    return jnp.where(flag, other, value)


X0 = 5
N0 = 32 + 2 * X0
N1 = 28
N2 = 28
N3 = 12
BIG = (N0, 40, 256)
VM = pl.BlockSpec(memory_space=pltpu.VMEM)


def call(kernel, name, out_shape, scratch, limit, *operands, aliases=None, out_specs=None):
    return pl.pallas_call(
        kernel,
        in_specs=[VM] * len(operands),
        out_specs=[VM] * len(out_shape) if out_specs is None else out_specs,
        out_shape=out_shape,
        scratch_shapes=scratch,
        input_output_aliases=aliases or {},
        compiler_params=pltpu.CompilerParams(vmem_limit_bytes=limit * MIB),
        name=name,
    )(*operands)


def kept(*shape):
    return pltpu.VMEM(shape, F32)


def send_rows_kernel(s_in, f_in, dn_ref, upw_ref):
    above = iota((8, 256), 0) < 4

    def work(j, n):
        here = pl.ds(j, n)
        dn_ref[here] = jnp.where(above, s_in[here, :8], pltpu.roll(f_in[here, :8].astype(F32), 4, 1))
        upw_ref[here] = jnp.where(above, pltpu.roll(f_in[here, 24:].astype(F32), 4, 1), s_in[here, 24:])

    blocks(0, 32, 8, work)


def halo_rows(lo, hi):
    low_y, high_y = edge("gy")
    above = iota((8, 256), 0) < 4
    outer = (above & high_y) | (~above & low_y)
    source = jnp.where(outer, 0.0, jnp.where(above, hi, lo))
    code = jnp.where(outer, OUT, pltpu.roll(jnp.where(above, lo, hi), 4, lo.ndim - 2))
    return source, code


def send_planes_kernel(s_in, f_in, ylo, yhi, dn_ref, upw_ref):
    for first, out_ref, skip in ((0, dn_ref, 0), (28, upw_ref, 1)):
        block = slice(first, first + 4)
        source, code = halo_rows(ylo[block], yhi[block])
        out_ref[:3, :32] = s_in[first + skip : first + skip + 3]
        out_ref[:3, 32:] = source[skip : skip + 3]
        out_ref[3:, :32] = f_in[block].astype(F32)
        out_ref[3:, 32:] = code


def water_to_mobility(n):
    return 0.25 * ((8.0 - n) * 0.125 + n * (0.125 * WATER))


def rows_to_16():
    fine_y = ring(iota((16, 40), 1), 36, 40)
    return fine_y - 2 * iota((16, 40), 0)


def lanes_to_128():
    return iota((256, 128), 0) - 2 * iota((256, 128), 1)


def inner0_kernel(
    s_in, f_in, ylo, yhi,
    s_ref, c_ref, wx, wy, wz, q_ref, p1, p2, r_ref, src1, mob1,
    t_ref,
):
    def own_planes(j, n):
        here, there = pl.ds(j, n), pl.ds(j + X0, n)
        source, code = halo_rows(ylo[here], yhi[here])
        s_ref[there, :32] = s_in[here]
        s_ref[there, 32:] = source
        c_ref[there, :32] = f_in[here].astype(F32)
        c_ref[there, 32:] = code

    blocks(0, 32, 4, own_planes)
    w = (wx, wy, wz, q_ref)
    weights_pass(6, 36, 6, c_ref, w, s_ref, p1, face_code, OUT, True)
    sweep(7, 35, 7, p1, p2, s_ref, w)
    remainder(8, 34, 6, p2, r_ref, s_ref, w)

    ry, rz = restrict_weight(rows_to_16()), restrict_weight(lanes_to_128())
    my, mz = pair_weight(rows_to_16()), pair_weight(lanes_to_128())
    for k in range(2, 14):
        t_ref[k * 16 : k * 16 + 16] = dot(ry, restrict_x(r_ref, 2 * k + 4))
    coarse = dot(t_ref[32:224], rz)
    for k in range(2, 14):
        src1[k] = coarse[k * 16 - 32 : k * 16 - 16]
    for k in range(16):
        t_ref[k * 16 : k * 16 + 16] = dot(my, c_ref[2 * k + X0] + c_ref[2 * k + X0 + 1])
    mobility = water_to_mobility(dot(t_ref[...], mz))
    for k in range(16):
        mob1[k] = mobility[k * 16 : k * 16 + 16]


def inner0(source, phase, ylo, yhi):
    return call(
        inner0_kernel, "inner0", [kept(*BIG)] * 9 + [kept(16, 16, 128)] * 2,
        [kept(256, 256)], 4, source, phase, ylo, yhi,
    )


def lay_rows(out, first, rows):
    for k in range(4):
        out[first + k] = rows[k // 2 * 16 : k // 2 * 16 + 16, k % 2 * 128 : k % 2 * 128 + 128]


def outer0_kernel(
    xlo, xhi, mob1, s_0, c_0, wx_0, wy_0, wz_0, q_0, p1_0, p2_0, r_0, src1_0,
    s_ref, c_ref, wx, wy, wz, q_ref, p1, p2, r_ref, src1, dn1, upw1, rows_dn, rows_up,
    t_ref,
):
    low_x, high_x = edge("gx")
    s_ref[2:5] = blank(low_x, xlo[:3], 0.0)
    c_ref[1:5] = blank(low_x, xlo[3:], OUT)
    s_ref[37:40] = blank(high_x, xhi[:3], 0.0)
    c_ref[37:41] = blank(high_x, xhi[3:], OUT)
    w = (wx, wy, wz, q_ref)
    for lo in (2, 36):
        weights_pass(lo, lo + 4, 4, c_ref, w, s_ref, p1, face_code, OUT, True)
    for lo in (3, 35):
        sweep(lo, lo + 4, 4, p1, p2, s_ref, w)
    for lo in (4, 34):
        remainder(lo, lo + 4, 4, p2, r_ref, s_ref, w)
    ry, rz = restrict_weight(rows_to_16()), restrict_weight(lanes_to_128())
    edges = (0, 1, 14, 15)
    for i, k in enumerate(edges):
        t_ref[i * 16 : i * 16 + 16] = dot(ry, restrict_x(r_ref, 2 * k + 4))
    coarse = dot(t_ref[...], rz)
    for i, k in enumerate(edges):
        src1[k] = coarse[i * 16 : i * 16 + 16]
    dn1[:5] = src1[:5]
    dn1[5:11] = mob1[:6]
    lay_rows(dn1, 11, p2[X0 + 2, :32])
    upw1[:5] = src1[11:]
    upw1[5:11] = mob1[10:]
    lay_rows(upw1, 11, p2[X0 + 29, :32])
    for k in range(32):
        rows_dn[k : k + 1] = p2[X0 + k, 2:3]
        rows_up[k : k + 1] = p2[X0 + k, 29:30]


def outer0(xlo, xhi, mob1, state):
    return call(
        outer0_kernel, "outer0",
        [kept(*BIG)] * 9 + [kept(16, 16, 128)] + [kept(15, 16, 128)] * 2 + [kept(32, 256)] * 2,
        [kept(64, 256)], 4, xlo, xhi, mob1, *state, aliases={3 + k: k for k in range(10)},
    )


def pack1_kernel(src, mob, xlo, xhi, rows_dn, rows_up, dn_ref, upw_ref):
    low_x, high_x = edge("gx")
    for rows, out, p_rows in ((slice(0, 8), dn_ref, rows_dn), (slice(8, 16), upw_ref, rows_up)):
        out[0, :8] = jnp.zeros((8, 128), F32)
        out[N1 - 1, :8] = jnp.zeros((8, 128), F32)
        out[1:6, :8] = blank(low_x, xlo[:5, rows], 0.0)
        out[0:6, 8:] = blank(low_x, xlo[5:11, rows], 0.0)
        out[6:22, :8] = src[:, rows]
        out[6:22, 8:] = mob[:, rows]
        out[22:27, :8] = blank(high_x, xhi[:5, rows], 0.0)
        out[22:28, 8:] = blank(high_x, xhi[5:11, rows], 0.0)
        lay_rows(out, N1, p_rows[...])


def pack1(*operands):
    return call(pack1_kernel, "pack1", [kept(N1 + 4, 16, 128)] * 2, [], 4, *operands)


def down1_kernel(
    src, mob, xlo, xhi, ylo, yhi,
    own2, dn2, upw2, s_ref, wx, wy, wz, q_ref, p2,
    m_ref, p1, r_ref, t_ref, pk_ref,
):
    low_x, high_x = edge("gx")
    low_y, high_y = edge("gy")
    zero = jnp.zeros((32, 128), F32)
    s_ref[0] = zero
    s_ref[N1 - 1] = zero
    s_ref[1:6, :16] = blank(low_x, xlo[:5], 0.0)
    m_ref[0:6, :16] = blank(low_x, xlo[5:11], 0.0)
    s_ref[6:22, :16] = src[...]
    m_ref[6:22, :16] = mob[...]
    s_ref[22:27, :16] = blank(high_x, xhi[:5], 0.0)
    m_ref[22:28, :16] = blank(high_x, xhi[5:11], 0.0)
    s_ref[:, 16:24] = blank(high_y, yhi[:N1, :8], 0.0)
    m_ref[:, 16:24] = blank(high_y, yhi[:N1, 8:], 0.0)
    s_ref[:, 24:] = blank(low_y, ylo[:N1, :8], 0.0)
    m_ref[:, 24:] = blank(low_y, ylo[:N1, 8:], 0.0)
    w = (wx, wy, wz, q_ref)

    weights_pass(1, N1 - 1, 13, m_ref, w, s_ref, p1, face_mean, 0.0, True)
    sweep(2, N1 - 2, 12, p1, p2, s_ref, w)
    remainder(3, N1 - 3, 11, p2, r_ref, s_ref, w)

    lane_in, lane_out = iota((128, 128), 0), iota((128, 128), 1)
    rz = jnp.where(lane_out < 64, restrict_weight(lane_in - 2 * lane_out), 0.0)
    mz = pair_weight(lane_in - 2 * (lane_out - 64))
    row_out = iota((16, 32), 0)
    coarse_y = ring(row_out, 12, 16)
    held = (coarse_y >= -2) & (coarse_y <= 9)
    fine_y = ring(iota((16, 32), 1), 24, 32)
    ry = jnp.where(held, restrict_weight(fine_y - 2 * coarse_y), 0.0)
    my = jnp.where(held, pair_weight(fine_y - 2 * coarse_y), 0.0)
    zero16 = jnp.zeros((16, 128), F32)
    for k in range(10):
        t_ref[k * 32 : k * 32 + 32] = restrict_x(r_ref, 2 * k + 3)
    coarse = dot(t_ref[:320], rz)
    for k in range(12):
        t_ref[k * 32 : k * 32 + 32] = (m_ref[2 * k + 2] + m_ref[2 * k + 3]) * (0.25 * 0.125)
    mean = dot(t_ref[...], mz)
    for k in range(12):
        value = dot(my, mean[k * 32 : k * 32 + 32])
        if 1 <= k <= 10:
            value = value + dot(ry, coarse[(k - 1) * 32 : k * 32])
        pk_ref[k] = value
    own2[...] = pk_ref[2:10]
    dn2[...] = pk_ref[2:12]
    upw2[...] = pk_ref[0:10]


def down1(*operands):
    return call(
        down1_kernel, "down1", [kept(k, 16, 128) for k in (8, 10, 10)] + [kept(N1, 32, 128)] * 6,
        [kept(N1, 32, 128)] * 3 + [kept(384, 128), kept(12, 16, 128)], 6, *operands,
    )


def pack2_kernel(own, xlo, xhi, out):
    low_x, high_x = edge("gx")
    out[:10] = blank(low_x, xlo[...], 0.0)
    out[10:18] = own[...]
    out[18:] = blank(high_x, xhi[...], 0.0)


def pack2(*operands):
    return call(pack2_kernel, "pack2", [kept(N2, 16, 128)], [], 4, *operands)[0]


def up_kernel(
    ext, ylo, yhi, s1, wx1, wy1, wz1, q1, down1_ref,
    wx0, wy0, wz0, q0, s0, down0_ref, plane_lo, plane_hi, rows_lo, rows_hi,
    scaled, residual,
    pa0, pb0,
    pa1, pb1,
    s2, m2, wx2, wy2, wz2, q2, pa2, pb2, r2,
    s3, m3, wx3, wy3, wz3, q3, pa3, pb3,
    t_ref, u_ref, v_ref, out_a, out_b, row_ref, sems,
):
    low_y, high_y = edge("gy")

    lane8, sub8 = iota((8, 128), 1), iota((8, 128), 0)

    def unpack(j, carry):
        def put(rows, packed):
            s2[j, rows] = packed
            m2[j, rows] = jnp.where(lane8 < 64, pltpu.roll(packed, 64, 1), 0.0)

        hi = blank(high_y, yhi[j], 0.0)
        lo = blank(low_y, ylo[j], 0.0)
        put(slice(0, 8), ext[j, :8])
        put(slice(8, 16), hi[:8])
        put(slice(16, 24), jnp.where(sub8 < 4, hi[8:], lo[8:]))
        put(slice(24, 32), lo[:8])
        return carry

    lax.fori_loop(0, N2, unpack, 0)
    w2 = (wx2, wy2, wz2, q2)

    weights_pass(1, N2 - 1, 13, m2, w2, s2, pa2, face_mean, 0.0, False)
    sweep(2, N2 - 2, 12, pa2, pb2, s2, w2)
    remainder(3, N2 - 3, 11, pb2, r2, s2, w2)

    lane_in, lane_out = iota((128, 128), 0), iota((128, 128), 1)
    down_z = lane_in - 2 * lane_out
    inner = (lane_in < 64) & (lane_out < 32)
    rz = jnp.where(inner, restrict_weight(down_z), 0.0)
    mz = jnp.where(inner, pair_weight(down_z), 0.0)
    coarse_y = ring(iota((16, 32), 0), 8, 16)
    fine_y = ring(iota((16, 32), 1), 20, 32)
    ry = restrict_weight(fine_y - 2 * coarse_y)
    my = pair_weight(fine_y - 2 * coarse_y)
    for k in range(10):
        t_ref[k * 32 : k * 32 + 32] = restrict_x(r2, 2 * k + 3)
    coarse = dot(t_ref[:320], rz)
    for k in range(12):
        t_ref[k * 32 : k * 32 + 32] = (m2[2 * k + 2] + m2[2 * k + 3]) * (0.25 * 0.125)
    mean = dot(t_ref[:384], mz)
    for k in range(12):
        m3[k] = dot(my, mean[k * 32 : k * 32 + 32])
        if 1 <= k <= 10:
            s3[k] = dot(ry, coarse[(k - 1) * 32 : k * 32])
    w3 = (wx3, wy3, wz3, q3)

    weights_pass(1, N3 - 1, 10, m3, w3, s3, pa3, face_mean, 0.0, False)
    sweep(2, N3 - 2, 8, pa3, pb3, s3, w3)

    pz = pair_weight(lane_out - 2 * lane_in)
    pz = jnp.where(lane_in < 32, pz, 0.0)
    py = pair_weight(ring(iota((32, 16), 0), 20, 32) - 2 * ring(iota((32, 16), 1), 8, 16))
    for k in range(8):
        t_ref[k * 32 : k * 32 + 32] = dot(py, pb3[k + 2])
    u_ref[:256] = dot(t_ref[:256], pz)
    for k in range(8):
        rise = u_ref[k * 32 : k * 32 + 32]
        pb2[2 * k + 6] = pb2[2 * k + 6] + rise
        pb2[2 * k + 7] = pb2[2 * k + 7] + rise
    sweep(7, 21, 7, pb2, pa2, s2, w2)
    sweep(8, 20, 12, pa2, pb2, s2, w2)

    pz = pair_weight(lane_out - 2 * lane_in)
    py = pair_weight(ring(iota((32, 32), 0), 24, 32) - 2 * ring(iota((32, 32), 1), 20, 32))
    for k in range(12):
        t_ref[k * 32 : k * 32 + 32] = dot(py, pb2[k + 8])
    u_ref[:384] = dot(t_ref[:384], pz)
    for k in range(12):
        rise = u_ref[k * 32 : k * 32 + 32]
        pa1[2 * k + 2] = down1_ref[2 * k + 2] + rise
        pa1[2 * k + 3] = down1_ref[2 * k + 3] + rise
    w1 = (wx1, wy1, wz1, q1)
    sweep(3, 25, 11, pa1, pb1, s1, w1)
    sweep(4, 24, 10, pb1, pa1, s1, w1)

    pz = pair_weight(iota((128, 256), 1) - 2 * iota((128, 256), 0))
    py = pair_weight(ring(iota((40, 32), 0), 36, 40) - 2 * ring(iota((40, 32), 1), 24, 32))
    for k in range(20):
        t_ref[k * 40 : k * 40 + 40] = dot(py, pa1[k + 4])
    v_ref[...] = dot(t_ref[...], pz)

    def rise0(k, n):
        for i in range(n):
            rise = v_ref[pl.ds(pl.multiple_of((k + i) * 40, 8), 40)]
            for j in (2 * (k + i) + 1, 2 * (k + i) + 2):
                pa0[j] = down0_ref[j] + rise

    low_x, high_x = edge("gx")
    row8 = iota((8, 256), 0)

    def plane_of(message, first):
        tiles = [message[first + k] for k in range(4)]
        return jnp.concatenate(
            [jnp.concatenate(tiles[:2], 1), jnp.concatenate(tiles[2:], 1), jnp.zeros((8, 256), F32)], 0
        )

    pa0[2] = v_ref[:40] + blank(low_x, plane_of(plane_lo, 11), 0.0)
    pa0[N0 - 3] = v_ref[760:] + blank(high_x, plane_of(plane_hi, 11), 0.0)
    for k in range(4):
        h, z = k // 2 * 16, k % 2 * 128
        row_ref[0, h : h + 16, z : z + 128] = blank(high_y, rows_hi[N1 + k], 0.0)
        row_ref[1, h : h + 16, z : z + 128] = blank(low_y, rows_lo[N1 + k], 0.0)
    for j in (3, 4, 37, 38):
        k = (j - 1) // 2
        pa0[j] = down0_ref[j] + v_ref[k * 40 : k * 40 + 40]

    def rise0(k, n):
        for i in range(n):
            rise = v_ref[pl.ds(pl.multiple_of((k + i) * 40, 8), 40)]
            for j in (2 * (k + i) + 1, 2 * (k + i) + 2):
                pa0[j, :32] = down0_ref[j, :32] + rise[:32]
                above = row_ref[0, pl.ds(j - X0, 1)]
                below = row_ref[1, pl.ds(j - X0, 1)]
                halo = jnp.where(row8 == 2, above, jnp.where(row8 == 5, below, down0_ref[j, 32:]))
                pa0[j, 32:] = halo + rise[32:]

    blocks(2, 18, 2, rise0)
    w0 = (wx0, wy0, wz0, q0)
    sweep(3, N0 - 3, 6, pa0, pb0, s0, w0)
    sweep(4, N0 - 4, 8, pb0, pa0, s0, w0)

    def out_copies(k, j):
        here = pl.ds(j, 8)
        return (
            pltpu.make_async_copy(out_a.at[here], scaled.at[here], sems.at[0, k]),
            pltpu.make_async_copy(out_b.at[here], residual.at[here], sems.at[1, k]),
        )

    def last(k, carry):
        j = k * 8
        results = []
        for i in range(8):
            p = pa0[j + i + X0]
            dp = (OMEGA / q0[j + i + X0]) * p
            results.append((dp[:32], (s0[j + i + X0] + flow(j + i + X0, p, pa0, w0) - dp)[:32]))
        for i, (a, b) in enumerate(results):
            out_a[j + i] = a
            out_b[j + i] = b
        for copy in out_copies(k, j):
            copy.start()
        return carry

    lax.fori_loop(0, 4, last, 0)
    for k in range(4):
        for copy in out_copies(k, k * 8):
            copy.wait()


def way_up(*operands):
    shape = jax.ShapeDtypeStruct((32, 32, 256), F32)
    buf = lambda count, *shape: [kept(*shape)] * count
    scratch = (
        buf(2, *BIG)
        + buf(2, N1, 32, 128)
        + buf(9, N2, 32, 128)
        + buf(8, N3, 16, 128)
        + buf(1, 800, 128)
        + buf(1, 384, 128)
        + buf(1, 800, 256)
        + buf(2, 32, 32, 256)
        + buf(1, 2, 32, 256)
        + [pltpu.SemaphoreType.DMA((2, 4))]
    )
    hbm = pl.BlockSpec(memory_space=pl.ANY)
    return call(up_kernel, "way_up", [shape] * 2, scratch, 20, *operands, out_specs=[hbm] * 2)


def shift(a, axis, step):
    count = lax.axis_size(axis)
    return lax.ppermute(a, axis, [(i, (i + step) % count) for i in range(count)])


def both(to_low, to_high, axis):
    return shift(to_high, axis, 1), shift(to_low, axis, -1)


def shards(source, phase):
    msg = [kept(32, 8, 256)] * 2
    ylo, yhi = both(*call(send_rows_kernel, "send_rows", msg, [], 4, source, phase), "gy")
    msg = [kept(7, 40, 256)] * 2
    dn0, up0 = call(send_planes_kernel, "send_planes", msg, [], 4, source, phase, ylo, yhi)
    xlo, xhi = both(dn0, up0, "gx")
    *state, mob1 = inner0(source, phase, ylo, yhi)
    s0, _, wx0, wy0, wz0, q0, _, p0, _, src1, dn1, up1, rows_dn, rows_up = outer0(xlo, xhi, mob1, state)
    xlo1, xhi1 = both(dn1, up1, "gx")
    ylo1, yhi1 = both(*pack1(src1, mob1, xlo1, xhi1, rows_dn, rows_up), "gy")
    own2, dn2, up2, *level1 = down1(src1, mob1, xlo1, xhi1, ylo1, yhi1)
    xlo, xhi = both(dn2, up2, "gx")
    ext = pack2(own2, xlo, xhi)
    ylo, yhi = both(ext, ext, "gy")
    level0 = (wx0, wy0, wz0, q0, s0, p0, xlo1, xhi1, ylo1, yhi1)
    return tuple(way_up(ext, ylo, yhi, *level1, *level0))


def solution(mesh):
    spec = P("gx", "gy", None)
    return jax.shard_map(shards, mesh=mesh, in_specs=(spec, spec), out_specs=(spec, spec), check_vma=False)
```

time: 86 us -> 73.7 us (0.86)
  Pallas kernels: 30.2 us -> 23 us
  waiting for transfers between devices: 28.4 us -> 23.4 us
  local copies, waits for them, and re-layouts: 1.14 us -> 2.44 us
  other arithmetic: 1.06 us -> 0 us
    pallas_call x6 -> x8, Pallas kernels: 30.2 us -> 23 us  [call(): pl.pallas_call(kernel, in_specs=[VM] * len(operands), out_specs=[VM] * le...]
    ppermute x12, waiting for transfers between devices: 28.4 us -> 23.4 us  [shift(): lax.ppermute(a, axis, [(i, (i + step) % count) for i in range(count)])]
    unnamed x4, local copies, waits for them, and re-layouts: 0.01 us -> 2.44 us
    slice x1 -> x0, local copies, waits for them, and re-layouts: 1.13 us -> none  [shards(): to_low = jnp.concatenate([source[:4], phase[:5].astype(F32)])]
    convert_element_type x1 -> x0, other arithmetic: 1.02 us -> none  [shards(): to_low = jnp.concatenate([source[:4], phase[:5].astype(F32)])]
  transfers between devices with their start and end apart: 12 -> 12, of which waited for: 8 -> 8; matrix products, arithmetic and copies ran while one was open for 0% -> 0% of each run, Pallas kernels for 0% -> 8%
where the time goes in v2:
time: 73.7 us; the launch traced here: 72.8 us
  waiting for transfers between devices  23.4 us (32%)
  Pallas kernels  23 us (31%)
  starting transfers between devices  23 us (31%)
  local copies, waits for them, and re-layouts  2.44 us (3%)
  between operations  0.86 us (1%)
    ppermute x12, waiting for transfers between devices, shift(): lax.ppermute(a, axis, [(i, (i + step) % count) for i in range(count)])  23.4 us
    pallas_call x8, Pallas kernels, call(): pl.pallas_call(kernel, in_specs=[VM] * len(operands), out_specs=[VM] * le...  23 us
    ppermute x12, starting transfers between devices, shift(): lax.ppermute(a, axis, [(i, (i + step) % count) for i in range(count)])  23 us
    unnamed x4, local copies, waits for them, and re-layouts  2.44 us
  transfers between devices with their start and end apart: 12, of which 8 were waited for; matrix products, arithmetic and copies ran while one was open for 0% of the time, Pallas kernels for 8%

profile of v2, /device:TPU:25, one launch (start us, length us, event | category | flops | bytes accessed | tf_op | source)
XLA Modules:
  0.0 72.8 jit_solution(12424871924235502348)
XLA Ops:
  0.6 0.0 copy-start
  0.6 1.2 %copy-done = f32[32,32,256]{2,1,0:T(8,128)S(1)} copy-done((f32[32,32,256]{2,1,0:T(8,128)S(1)}, f32[32,32,256]{2,1,0:T(8,128)}, u32[]{:S(2)}) %copy-start) | copy-done | bytes 1048600
  1.9 0.0 copy-start.1
  1.9 1.2 %copy-done.1 = s32[32,32,256]{2,1,0:T(8,128)S(1)} copy-done((s32[32,32,256]{2,1,0:T(8,128)S(1)}, s32[32,32,256]{2,1,0:T(8,128)}, u32[]{:S(2)}) %copy-start.1) | copy-done | bytes 1048600
  3.1 0.1 send_rows.1
  3.2 2.3 %collective-permute-start = (f32[32,8,256]{2,1,0:T(8,128)S(1)}, f32[32,8,256]{2,1,0:T(8,128)S(1)}, u32[]{:S(2)}, u32[]{:S(2)}) collective-permute-start(f32[32,8,256]{2,1,0:T(8,128)S(1)} %get-tuple-element.39), channel_id=1, source_target_pairs={{0,1},{1,2},{2,3},{3,4},{4,5},{5,6},{6,7},{7,0},{8,9},{9,10},{10,1... | collective-permute-start | bytes 786440 | tf_op jit(solution)/shard_map/ppermute | solution.py:581
  5.4 0.0 collective-permute-start.1
  5.4 3.3 %collective-permute-done.ylo = f32[32,8,256]{2,1,0:T(8,128)S(1)} collective-permute-done((f32[32,8,256]{2,1,0:T(8,128)S(1)}, f32[32,8,256]{2,1,0:T(8,128)S(1)}, u32[]{:S(2)}, u32[]{:S(2)}) %collective-permute-start) | collective-permute-done | bytes 262176 | tf_op jit(solution)/shard_map/ppermute | solution.py:581
  8.7 3.7 %collective-permute-done.1.yhi = f32[32,8,256]{2,1,0:T(8,128)S(1)} collective-permute-done((f32[32,8,256]{2,1,0:T(8,128)S(1)}, f32[32,8,256]{2,1,0:T(8,128)S(1)}, u32[]{:S(2)}, u32[]{:S(2)}) %collective-permute-start.1) | collective-permute-done | bytes 262176 | tf_op jit(solution)/shard_map/ppermute | solution.py:581
  12.5 0.1 collective-permute-start.2
  12.6 6.1 %collective-permute-start.3 = (f32[7,40,256]{2,1,0:T(8,128)S(1)}, f32[7,40,256]{2,1,0:T(8,128)S(1)}, u32[]{:S(2)}, u32[]{:S(2)}) collective-permute-start(f32[7,40,256]{2,1,0:T(8,128)S(1)} %get-tuple-element.42), channel_id=1, source_target_pairs={{0,248},{8,0},{16,8},{24,16},{32,24},{40,32},{48,40},{56,48},{64,5... | collective-permute-start | bytes 860168 | tf_op jit(solution)/shard_map/ppermute | solution.py:581
  18.7 5.5 %inner0.1 = (f32[42,40,256]{2,1,0:T(8,128)S(1)}, f32[42,40,256]{2,1,0:T(8,128)S(1)}, f32[42,40,256]{2,1,0:T(8,128)S(1)}, f32[42,40,256]{2,1,0:T(8,128)S(1)}, f32...) custom-call(f32[32,32,256]{2,1,0:T(8,128)S(1)} %copy-done, ...), custom_call_target="tpu_custom_call" | custom-call | tf_op jit(solution)/shard_map/inner0/pallas_call | solution.py:168
  24.2 0.6 collective-permute-done.2.xlo
  24.8 0.0 collective-permute-done.3.xhi
  24.8 1.5 %outer0.1 = (f32[42,40,256]{2,1,0:T(8,128)S(1)}, f32[42,40,256]{2,1,0:T(8,128)S(1)}, f32[42,40,256]{2,1,0:T(8,128)S(1)}, f32[42,40,256]{2,1,0:T(8,128)S(1)}, f32...) custom-call(f32[7,40,256]{2,1,0:T(8,128)S(1)} %collective-permute-do, ...), custom_call_target="tpu_custom_call", output_to_operand_aliasing={{0}: (3, {}), {1}: (4, {}), {2}: (5, {}), {3}: (6, {}), {4}... | custom-call | tf_op jit(solution)/shard_map/outer0/pallas_call | solution.py:168
  26.3 0.1 collective-permute-start.4
  26.4 5.2 %collective-permute-start.5 = (f32[15,16,128]{2,1,0:T(8,128)S(1)}, f32[15,16,128]{2,1,0:T(8,128)S(1)}, u32[]{:S(2)}, u32[]{:S(2)}) collective-permute-start(f32[15,16,128]{2,1,0:T(8,128)S(1)} %get-tuple-element.56), channel_id=1, source_target_pairs={{0,248},{8,0},{16,8},{24,16},{32,24},{40,32},{48,40},{56,48},{64,5... | collective-permute-start | bytes 368648 | tf_op jit(solution)/shard_map/ppermute | solution.py:581
  31.6 3.5 %collective-permute-done.4.xlo.plane_lo = f32[15,16,128]{2,1,0:T(8,128)S(1)} collective-permute-done((f32[15,16,128]{2,1,0:T(8,128)S(1)}, f32[15,16,128]{2,1,0:T(8,128)S(1)}, u32[]{:S(2)}, u32[]{:S(2)}) %collective-permute-start.4) | collective-permute-done | bytes 122912 | tf_op jit(solution)/shard_map/ppermute | solution.py:581
  35.2 0.0 collective-permute-done.5.xhi.plane_hi
  35.2 1.2 %collective-permute-start.6 = (f32[32,16,128]{2,1,0:T(8,128)S(1)}, f32[32,16,128]{2,1,0:T(8,128)S(1)}, u32[]{:S(2)}, u32[]{:S(2)}) collective-permute-start(f32[32,16,128]{2,1,0:T(8,128)S(1)} %get-tuple-element.59), channel_id=1, source_target_pairs={{0,1},{1,2},{2,3},{3,4},{4,5},{5,6},{6,7},{7,0},{8,9},{9,10},{10,1... | collective-permute-start | bytes 786440 | tf_op jit(solution)/shard_map/ppermute | solution.py:581
  36.4 0.0 collective-permute-start.7
  36.4 3.3 %collective-permute-done.6.ylo.rows_lo = f32[32,16,128]{2,1,0:T(8,128)S(1)} collective-permute-done((f32[32,16,128]{2,1,0:T(8,128)S(1)}, f32[32,16,128]{2,1,0:T(8,128)S(1)}, u32[]{:S(2)}, u32[]{:S(2)}) %collective-permute-start.6) | collective-permute-done | bytes 262176 | tf_op jit(solution)/shard_map/ppermute | solution.py:581
  39.7 3.7 %collective-permute-done.7.yhi.rows_hi = f32[32,16,128]{2,1,0:T(8,128)S(1)} collective-permute-done((f32[32,16,128]{2,1,0:T(8,128)S(1)}, f32[32,16,128]{2,1,0:T(8,128)S(1)}, u32[]{:S(2)}, u32[]{:S(2)}) %collective-permute-start.7) | collective-permute-done | bytes 262176 | tf_op jit(solution)/shard_map/ppermute | solution.py:581
  43.4 2.7 %down1.1 = (f32[8,16,128]{2,1,0:T(8,128)S(1)}, f32[10,16,128]{2,1,0:T(8,128)S(1)}, f32[10,16,128]{2,1,0:T(8,128)S(1)}, f32[28,32,128]{2,1,0:T(8,128)S(1)}, f32[2...) custom-call(f32[16,16,128]{2,1,0:T(8,128)S(1)} %get-tuple-element.54, ...), custom_call_target="tpu_custom_call" | custom-call | tf_op jit(solution)/shard_map/down1/pallas_call | solution.py:168
  46.1 0.0 collective-permute-start.8
  46.1 5.1 %collective-permute-start.9 = (f32[10,16,128]{2,1,0:T(8,128)S(1)}, f32[10,16,128]{2,1,0:T(8,128)S(1)}, u32[]{:S(2)}, u32[]{:S(2)}) collective-permute-start(f32[10,16,128]{2,1,0:T(8,128)S(1)} %get-tuple-element.63), channel_id=1, source_target_pairs={{0,248},{8,0},{16,8},{24,16},{32,24},{40,32},{48,40},{56,48},{64,5... | collective-permute-start | bytes 245768 | tf_op jit(solution)/shard_map/ppermute | solution.py:581
  51.2 1.6 %collective-permute-done.8.xlo = f32[10,16,128]{2,1,0:T(8,128)S(1)} collective-permute-done((f32[10,16,128]{2,1,0:T(8,128)S(1)}, f32[10,16,128]{2,1,0:T(8,128)S(1)}, u32[]{:S(2)}, u32[]{:S(2)}) %collective-permute-start.8) | collective-permute-done | bytes 81952 | tf_op jit(solution)/shard_map/ppermute | solution.py:581
  52.8 0.0 collective-permute-done.9.xhi
  52.8 0.0 collective-permute-start.11
  52.8 2.9 %collective-permute-start.10 = (f32[28,16,128]{2,1,0:T(8,128)S(1)}, f32[28,16,128]{2,1,0:T(8,128)S(1)}, u32[]{:S(2)}, u32[]{:S(2)}) collective-permute-start(f32[28,16,128]{2,1,0:T(8,128)S(1)} %pack2.1.ext), channel_id=1, source_target_pairs={{0,1},{1,2},{2,3},{3,4},{4,5},{5,6},{6,7},{7,0},{8,9},{9,10},{10,1... | collective-permute-start | bytes 688136 | tf_op jit(solution)/shard_map/ppermute | solution.py:581
  55.8 3.7 %collective-permute-done.11.yhi = f32[28,16,128]{2,1,0:T(8,128)S(1)} collective-permute-done((f32[28,16,128]{2,1,0:T(8,128)S(1)}, f32[28,16,128]{2,1,0:T(8,128)S(1)}, u32[]{:S(2)}, u32[]{:S(2)}) %collective-permute-start.11) | collective-permute-done | bytes 229408 | tf_op jit(solution)/shard_map/ppermute | solution.py:581
  59.5 0.0 collective-permute-done.10.ylo
  59.5 13.1 %way_up.1 = (f32[32,32,256]{2,1,0:T(8,128)}, f32[32,32,256]{2,1,0:T(8,128)}) custom-call(f32[28,16,128]{2,1,0:T(8,128)S(1)} %pack2.1.ext, f32[28,16,128]{2,1,0:T(8,128)S(1)} %collective-permute-done.10.ylo, f32[28,16,128]{2,1,0:T(8,128)S(1)} %collective-permute-done.11.yhi, f32[28,32,128]{2,1,0:T(8,128)S(1)} %get-tuple-element.64.s1, ...), custom_call_target="tpu_custom_call" | custom-call | tf_op jit(solution)/shard_map/way_up/pallas_call | solution.py:168
  (3 shorter events, 0.1 us)
Async XLA Ops:
  0.6 1.2 %copy-start = (f32[32,32,256]{2,1,0:T(8,128)S(1)}, f32[32,32,256]{2,1,0:T(8,128)}, u32[]{:S(2)}) copy-start(f32[32,32,256]{2,1,0:T(8,128)} %s_in.5) | copy-start | bytes 3145732
  1.9 1.2 %copy-start.1 = (s32[32,32,256]{2,1,0:T(8,128)S(1)}, s32[32,32,256]{2,1,0:T(8,128)}, u32[]{:S(2)}) copy-start(s32[32,32,256]{2,1,0:T(8,128)} %f_in.5) | copy-start | bytes 3145732
  3.2 5.6 %collective-permute-start = (f32[32,8,256]{2,1,0:T(8,128)S(1)}, f32[32,8,256]{2,1,0:T(8,128)S(1)}, u32[]{:S(2)}, u32[]{:S(2)}) collective-permute-start(f32[32,8,256]{2,1,0:T(8,128)S(1)} %get-tuple-element.39), channel_id=1, source_target_pairs={{0,1},{1,2},{2,3},{3,4},{4,5},{5,6},{6,7},{7,0},{8,9},{9,10},{10,1... | collective-permute-start | bytes 786440 | tf_op jit(solution)/shard_map/ppermute | solution.py:581
  5.4 7.0 %collective-permute-start.1 = (f32[32,8,256]{2,1,0:T(8,128)S(1)}, f32[32,8,256]{2,1,0:T(8,128)S(1)}, u32[]{:S(2)}, u32[]{:S(2)}) collective-permute-start(f32[32,8,256]{2,1,0:T(8,128)S(1)} %get-tuple-element.40), channel_id=1, source_target_pairs={{0,7},{1,0},{2,1},{3,2},{4,3},{5,4},{6,5},{7,6},{8,15},{9,8},{10,9... | collective-permute-start | bytes 786440 | tf_op jit(solution)/shard_map/ppermute | solution.py:581
  12.5 12.4 %collective-permute-start.2 = (f32[7,40,256]{2,1,0:T(8,128)S(1)}, f32[7,40,256]{2,1,0:T(8,128)S(1)}, u32[]{:S(2)}, u32[]{:S(2)}) collective-permute-start(f32[7,40,256]{2,1,0:T(8,128)S(1)} %get-tuple-element.41), channel_id=1, source_target_pairs={{0,8},{8,16},{16,24},{24,32},{32,40},{40,48},{48,56},{56,64},{64,7... | collective-permute-start | bytes 860168 | tf_op jit(solution)/shard_map/ppermute | solution.py:581
  12.6 12.3 %collective-permute-start.3 = (f32[7,40,256]{2,1,0:T(8,128)S(1)}, f32[7,40,256]{2,1,0:T(8,128)S(1)}, u32[]{:S(2)}, u32[]{:S(2)}) collective-permute-start(f32[7,40,256]{2,1,0:T(8,128)S(1)} %get-tuple-element.42), channel_id=1, source_target_pairs={{0,248},{8,0},{16,8},{24,16},{32,24},{40,32},{48,40},{56,48},{64,5... | collective-permute-start | bytes 860168 | tf_op jit(solution)/shard_map/ppermute | solution.py:581
  26.3 8.8 %collective-permute-start.4 = (f32[15,16,128]{2,1,0:T(8,128)S(1)}, f32[15,16,128]{2,1,0:T(8,128)S(1)}, u32[]{:S(2)}, u32[]{:S(2)}) collective-permute-start(f32[15,16,128]{2,1,0:T(8,128)S(1)} %get-tuple-element.55), channel_id=1, source_target_pairs={{0,8},{8,16},{16,24},{24,32},{32,40},{40,48},{48,56},{56,64},{64,7... | collective-permute-start | bytes 368648 | tf_op jit(solution)/shard_map/ppermute | solution.py:581
  26.4 8.8 %collective-permute-start.5 = (f32[15,16,128]{2,1,0:T(8,128)S(1)}, f32[15,16,128]{2,1,0:T(8,128)S(1)}, u32[]{:S(2)}, u32[]{:S(2)}) collective-permute-start(f32[15,16,128]{2,1,0:T(8,128)S(1)} %get-tuple-element.56), channel_id=1, source_target_pairs={{0,248},{8,0},{16,8},{24,16},{32,24},{40,32},{48,40},{56,48},{64,5... | collective-permute-start | bytes 368648 | tf_op jit(solution)/shard_map/ppermute | solution.py:581
  35.2 4.5 %collective-permute-start.6 = (f32[32,16,128]{2,1,0:T(8,128)S(1)}, f32[32,16,128]{2,1,0:T(8,128)S(1)}, u32[]{:S(2)}, u32[]{:S(2)}) collective-permute-start(f32[32,16,128]{2,1,0:T(8,128)S(1)} %get-tuple-element.59), channel_id=1, source_target_pairs={{0,1},{1,2},{2,3},{3,4},{4,5},{5,6},{6,7},{7,0},{8,9},{9,10},{10,1... | collective-permute-start | bytes 786440 | tf_op jit(solution)/shard_map/ppermute | solution.py:581
  36.4 7.0 %collective-permute-start.7 = (f32[32,16,128]{2,1,0:T(8,128)S(1)}, f32[32,16,128]{2,1,0:T(8,128)S(1)}, u32[]{:S(2)}, u32[]{:S(2)}) collective-permute-start(f32[32,16,128]{2,1,0:T(8,128)S(1)} %get-tuple-element.60), channel_id=1, source_target_pairs={{0,7},{1,0},{2,1},{3,2},{4,3},{5,4},{6,5},{7,6},{8,15},{9,8},{10,9... | collective-permute-start | bytes 786440 | tf_op jit(solution)/shard_map/ppermute | solution.py:581
  46.1 6.7 %collective-permute-start.8 = (f32[10,16,128]{2,1,0:T(8,128)S(1)}, f32[10,16,128]{2,1,0:T(8,128)S(1)}, u32[]{:S(2)}, u32[]{:S(2)}) collective-permute-start(f32[10,16,128]{2,1,0:T(8,128)S(1)} %get-tuple-element.62), channel_id=1, source_target_pairs={{0,8},{8,16},{16,24},{24,32},{32,40},{40,48},{48,56},{56,64},{64,7... | collective-permute-start | bytes 245768 | tf_op jit(solution)/shard_map/ppermute | solution.py:581
  46.1 6.7 %collective-permute-start.9 = (f32[10,16,128]{2,1,0:T(8,128)S(1)}, f32[10,16,128]{2,1,0:T(8,128)S(1)}, u32[]{:S(2)}, u32[]{:S(2)}) collective-permute-start(f32[10,16,128]{2,1,0:T(8,128)S(1)} %get-tuple-element.63), channel_id=1, source_target_pairs={{0,248},{8,0},{16,8},{24,16},{32,24},{40,32},{48,40},{56,48},{64,5... | collective-permute-start | bytes 245768 | tf_op jit(solution)/shard_map/ppermute | solution.py:581
  52.8 6.7 %collective-permute-start.11 = (f32[28,16,128]{2,1,0:T(8,128)S(1)}, f32[28,16,128]{2,1,0:T(8,128)S(1)}, u32[]{:S(2)}, u32[]{:S(2)}) collective-permute-start(f32[28,16,128]{2,1,0:T(8,128)S(1)} %pack2.1.ext), channel_id=1, source_target_pairs={{0,7},{1,0},{2,1},{3,2},{4,3},{5,4},{6,5},{7,6},{8,15},{9,8},{10,9... | collective-permute-start | bytes 688136 | tf_op jit(solution)/shard_map/ppermute | solution.py:581
  52.8 6.6 %collective-permute-start.10 = (f32[28,16,128]{2,1,0:T(8,128)S(1)}, f32[28,16,128]{2,1,0:T(8,128)S(1)}, u32[]{:S(2)}, u32[]{:S(2)}) collective-permute-start(f32[28,16,128]{2,1,0:T(8,128)S(1)} %pack2.1.ext), channel_id=1, source_target_pairs={{0,1},{1,2},{2,3},{3,4},{4,5},{5,6},{6,7},{7,0},{8,9},{9,10},{10,1... | collective-permute-start | bytes 688136 | tf_op jit(solution)/shard_map/ppermute | solution.py:581

commit v3 on v2

--- a/solution.py
+++ b/solution.py
@@ -142,6 +142,39 @@
     planes(lo, hi, size, plane, (out_ref,))
 
 
+def halving(valid):
+    lane_in, lane_out = iota((256, 128), 0), iota((256, 128), 1)
+    down = jnp.where((lane_in < 128) & (lane_out < valid), restrict_weight(lane_in - 2 * lane_out), 0.0)
+    return down + jnp.where(lane_in >= 128, pair_weight(lane_in - 2 * lane_out), 0.0)
+
+
+def halve_rows(t):
+    above = up_y(t)
+    near, far = t + above, dn_y(t) + up_y(above)
+    return jnp.where(iota(t.shape, 1) < 64, near * 0.375 + far * 0.125, near)
+
+
+def every_other(ref, first, count):
+    return ref[pl.ds(first, count, stride=2)]
+
+
+def twice(ref, first, value):
+    count = value.shape[0]
+    ref[pl.ds(first, count, stride=2)] = value
+    ref[pl.ds(first + 1, count, stride=2)] = value
+
+
+def halve(count, r_ref, m_ref, t_ref, u_ref, valid):
+    for k in range(count):
+        rows = slice(k * 32, k * 32 + 32)
+        t_ref[rows, :128] = restrict_x(r_ref, 2 * k + 1) if 1 <= k < count - 1 else jnp.zeros((32, 128), F32)
+        t_ref[rows, 128:] = (m_ref[2 * k + 2] + m_ref[2 * k + 3]) * (0.25 * 0.125)
+    packed = dot(t_ref[...], halving(valid))
+    for k in range(count):
+        u_ref[k * 32 : k * 32 + 32] = halve_rows(packed[k * 32 : k * 32 + 32])
+    return [every_other(u_ref, k * 32, 16) for k in range(count)]
+
+
 def restrict_x(r_ref, j):
     return (r_ref[j] + r_ref[j + 3]) * 0.125 + (r_ref[j + 1] + r_ref[j + 2]) * 0.375
 
@@ -164,10 +197,10 @@
 VM = pl.BlockSpec(memory_space=pltpu.VMEM)
 
 
-def call(kernel, name, out_shape, scratch, limit, *operands, aliases=None, out_specs=None):
+def call(kernel, name, out_shape, scratch, limit, *operands, aliases=None, in_specs=None, out_specs=None):
     return pl.pallas_call(
         kernel,
-        in_specs=[VM] * len(operands),
+        in_specs=[VM] * len(operands) if in_specs is None else in_specs,
         out_specs=[VM] * len(out_shape) if out_specs is None else out_specs,
         out_shape=out_shape,
         scratch_shapes=scratch,
@@ -181,15 +214,32 @@
     return pltpu.VMEM(shape, F32)
 
 
-def send_rows_kernel(s_in, f_in, dn_ref, upw_ref):
+def send_rows_kernel(s_hbm, f_hbm, dn_ref, upw_ref, s_lo, s_hi, f_lo, f_hi, sems):
+    parts = ((s_hbm, 0, s_lo), (f_hbm, 0, f_lo), (s_hbm, 24, s_hi), (f_hbm, 24, f_hi))
+    copies = [
+        pltpu.make_async_copy(ref.at[:, pl.ds(first, 8)], part, sems.at[k])
+        for k, (ref, first, part) in enumerate(parts)
+    ]
+    for copy in copies:
+        copy.start()
+    for copy in copies:
+        copy.wait()
     above = iota((8, 256), 0) < 4
 
     def work(j, n):
         here = pl.ds(j, n)
-        dn_ref[here] = jnp.where(above, s_in[here, :8], pltpu.roll(f_in[here, :8].astype(F32), 4, 1))
-        upw_ref[here] = jnp.where(above, pltpu.roll(f_in[here, 24:].astype(F32), 4, 1), s_in[here, 24:])
+        dn_ref[here] = jnp.where(above, s_lo[here], pltpu.roll(f_lo[here].astype(F32), 4, 1))
+        upw_ref[here] = jnp.where(above, pltpu.roll(f_hi[here].astype(F32), 4, 1), s_hi[here])
 
     blocks(0, 32, 8, work)
+
+
+def send_rows(source, phase):
+    part = (32, 8, 256)
+    scratch = [kept(*part)] * 2 + [pltpu.VMEM(part, jnp.int32)] * 2 + [pltpu.SemaphoreType.DMA((4,))]
+    hbm = [pl.BlockSpec(memory_space=pltpu.HBM)] * 2
+    operands = [pltpu.with_memory_space_constraint(x, pltpu.HBM) for x in (source, phase)]
+    return call(send_rows_kernel, "send_rows", [kept(*part)] * 2, scratch, 4, *operands, in_specs=hbm)
 
 
 def halo_rows(lo, hi):
@@ -333,7 +383,7 @@
 def down1_kernel(
     src, mob, xlo, xhi, ylo, yhi,
     own2, dn2, upw2, s_ref, wx, wy, wz, q_ref, p2,
-    m_ref, p1, r_ref, t_ref, pk_ref,
+    m_ref, p1, r_ref, t_ref, u_ref, pk_ref,
 ):
     low_x, high_x = edge("gx")
     low_y, high_y = edge("gy")
@@ -356,27 +406,8 @@
     sweep(2, N1 - 2, 12, p1, p2, s_ref, w)
     remainder(3, N1 - 3, 11, p2, r_ref, s_ref, w)
 
-    lane_in, lane_out = iota((128, 128), 0), iota((128, 128), 1)
-    rz = jnp.where(lane_out < 64, restrict_weight(lane_in - 2 * lane_out), 0.0)
-    mz = pair_weight(lane_in - 2 * (lane_out - 64))
-    row_out = iota((16, 32), 0)
-    coarse_y = ring(row_out, 12, 16)
-    held = (coarse_y >= -2) & (coarse_y <= 9)
-    fine_y = ring(iota((16, 32), 1), 24, 32)
-    ry = jnp.where(held, restrict_weight(fine_y - 2 * coarse_y), 0.0)
-    my = jnp.where(held, pair_weight(fine_y - 2 * coarse_y), 0.0)
-    zero16 = jnp.zeros((16, 128), F32)
-    for k in range(10):
-        t_ref[k * 32 : k * 32 + 32] = restrict_x(r_ref, 2 * k + 3)
-    coarse = dot(t_ref[:320], rz)
-    for k in range(12):
-        t_ref[k * 32 : k * 32 + 32] = (m_ref[2 * k + 2] + m_ref[2 * k + 3]) * (0.25 * 0.125)
-    mean = dot(t_ref[...], mz)
-    for k in range(12):
-        value = dot(my, mean[k * 32 : k * 32 + 32])
-        if 1 <= k <= 10:
-            value = value + dot(ry, coarse[(k - 1) * 32 : k * 32])
-        pk_ref[k] = value
+    for k, packed in enumerate(halve(12, r_ref, m_ref, t_ref, u_ref, 64)):
+        pk_ref[k] = packed
     own2[...] = pk_ref[2:10]
     dn2[...] = pk_ref[2:12]
     upw2[...] = pk_ref[0:10]
@@ -385,19 +416,34 @@
 def down1(*operands):
     return call(
         down1_kernel, "down1", [kept(k, 16, 128) for k in (8, 10, 10)] + [kept(N1, 32, 128)] * 6,
-        [kept(N1, 32, 128)] * 3 + [kept(384, 128), kept(12, 16, 128)], 6, *operands,
+        [kept(N1, 32, 128)] * 3 + [kept(384, 256), kept(384, 128), kept(12, 16, 128)], 6, *operands,
     )
 
 
-def pack2_kernel(own, xlo, xhi, out):
+def pack2_kernel(own, xlo, xhi, dn_ref, upw_ref):
     low_x, high_x = edge("gx")
-    out[:10] = blank(low_x, xlo[...], 0.0)
-    out[10:18] = own[...]
-    out[18:] = blank(high_x, xhi[...], 0.0)
+    row = iota((8, 128), 0)
+    for a in range(N2 // 4):
+        two_dn = two_up = jnp.zeros((8, 128), F32)
+        for b in range(4):
+            j = 4 * a + b
+            if j < 10:
+                plane = blank(low_x, xlo[j], 0.0)
+            elif j < 18:
+                plane = own[j - 10]
+            else:
+                plane = blank(high_x, xhi[j - 18], 0.0)
+            dn_ref[j] = plane[:8]
+            upw_ref[j] = plane[:8]
+            here = (row == 2 * b) | (row == 2 * b + 1)
+            two_dn = jnp.where(here, pltpu.roll(plane[8:], 2 * b, 0) if b else plane[8:], two_dn)
+            two_up = jnp.where(here, pltpu.roll(plane[8:], 2 * b + 2, 0) if b < 3 else plane[8:], two_up)
+        dn_ref[N2 + a] = two_dn
+        upw_ref[N2 + a] = two_up
 
 
 def pack2(*operands):
-    return call(pack2_kernel, "pack2", [kept(N2, 16, 128)], [], 4, *operands)[0]
+    return call(pack2_kernel, "pack2", [kept(N2 + N2 // 4, 8, 128)] * 2, [], 4, *operands)
 
 
 def up_kernel(
@@ -408,93 +454,81 @@
     pa1, pb1,
     s2, m2, wx2, wy2, wz2, q2, pa2, pb2, r2,
     s3, m3, wx3, wy3, wz3, q3, pa3, pb3,
-    t_ref, u_ref, v_ref, out_a, out_b, row_ref, sems,
+    t_ref, u_ref, v_ref, rise_lo, rise_hi, out_a, out_b, row_ref, sems,
 ):
     low_y, high_y = edge("gy")
 
     lane8, sub8 = iota((8, 128), 1), iota((8, 128), 0)
 
-    def unpack(j, carry):
-        def put(rows, packed):
-            s2[j, rows] = packed
-            m2[j, rows] = jnp.where(lane8 < 64, pltpu.roll(packed, 64, 1), 0.0)
-
-        hi = blank(high_y, yhi[j], 0.0)
-        lo = blank(low_y, ylo[j], 0.0)
-        put(slice(0, 8), ext[j, :8])
-        put(slice(8, 16), hi[:8])
-        put(slice(16, 24), jnp.where(sub8 < 4, hi[8:], lo[8:]))
-        put(slice(24, 32), lo[:8])
-        return carry
-
-    lax.fori_loop(0, N2, unpack, 0)
+    def put(j, rows, packed):
+        s2[j, rows] = packed
+        m2[j, rows] = jnp.where(lane8 < 64, pltpu.roll(packed, 64, 1), 0.0)
+
+    for j in range(N2):
+        a, b = divmod(j, 4)
+        hi, lo = yhi[N2 + a], ylo[N2 + a]
+        hi = pltpu.roll(hi, 8 - 2 * b, 0) if b else hi
+        lo = pltpu.roll(lo, 6 - 2 * b, 0) if b < 3 else lo
+        put(j, slice(0, 8), ext[j])
+        put(j, slice(8, 16), blank(high_y, yhi[j], 0.0))
+        put(j, slice(16, 24), jnp.where((sub8 < 4) & ~high_y, hi, jnp.where((sub8 >= 4) & ~low_y, lo, 0.0)))
+        put(j, slice(24, 32), blank(low_y, ylo[j], 0.0))
+
     w2 = (wx2, wy2, wz2, q2)
 
     weights_pass(1, N2 - 1, 13, m2, w2, s2, pa2, face_mean, 0.0, False)
     sweep(2, N2 - 2, 12, pa2, pb2, s2, w2)
     remainder(3, N2 - 3, 11, pb2, r2, s2, w2)
 
-    lane_in, lane_out = iota((128, 128), 0), iota((128, 128), 1)
-    down_z = lane_in - 2 * lane_out
-    inner = (lane_in < 64) & (lane_out < 32)
-    rz = jnp.where(inner, restrict_weight(down_z), 0.0)
-    mz = jnp.where(inner, pair_weight(down_z), 0.0)
-    coarse_y = ring(iota((16, 32), 0), 8, 16)
-    fine_y = ring(iota((16, 32), 1), 20, 32)
-    ry = restrict_weight(fine_y - 2 * coarse_y)
-    my = pair_weight(fine_y - 2 * coarse_y)
-    for k in range(10):
-        t_ref[k * 32 : k * 32 + 32] = restrict_x(r2, 2 * k + 3)
-    coarse = dot(t_ref[:320], rz)
-    for k in range(12):
-        t_ref[k * 32 : k * 32 + 32] = (m2[2 * k + 2] + m2[2 * k + 3]) * (0.25 * 0.125)
-    mean = dot(t_ref[:384], mz)
-    for k in range(12):
-        m3[k] = dot(my, mean[k * 32 : k * 32 + 32])
-        if 1 <= k <= 10:
-            s3[k] = dot(ry, coarse[(k - 1) * 32 : k * 32])
+    lane16 = iota((16, 128), 1)
+    for k, packed in enumerate(halve(12, r2, m2, t_ref, u_ref, 32)):
+        s3[k] = packed
+        m3[k] = jnp.where(lane16 < 64, pltpu.roll(packed, 64, 1), 0.0)
     w3 = (wx3, wy3, wz3, q3)
 
     weights_pass(1, N3 - 1, 10, m3, w3, s3, pa3, face_mean, 0.0, False)
     sweep(2, N3 - 2, 8, pa3, pb3, s3, w3)
 
-    pz = pair_weight(lane_out - 2 * lane_in)
-    pz = jnp.where(lane_in < 32, pz, 0.0)
-    py = pair_weight(ring(iota((32, 16), 0), 20, 32) - 2 * ring(iota((32, 16), 1), 8, 16))
+    lane_in, lane_out = iota((128, 128), 0), iota((128, 128), 1)
+    double = pair_weight(lane_out - 2 * lane_in)
     for k in range(8):
-        t_ref[k * 32 : k * 32 + 32] = dot(py, pb3[k + 2])
-    u_ref[:256] = dot(t_ref[:256], pz)
+        v_ref[k * 16 : k * 16 + 16] = pb3[k + 2]
+    rise = dot(v_ref[:128], jnp.where(lane_in < 32, double, 0.0))
     for k in range(8):
-        rise = u_ref[k * 32 : k * 32 + 32]
-        pb2[2 * k + 6] = pb2[2 * k + 6] + rise
-        pb2[2 * k + 7] = pb2[2 * k + 7] + rise
+        twice(u_ref, k * 32, rise[k * 16 : k * 16 + 16])
+    for k in range(8):
+        for j in (2 * k + 6, 2 * k + 7):
+            pb2[j] = pb2[j] + u_ref[k * 32 : k * 32 + 32]
     sweep(7, 21, 7, pb2, pa2, s2, w2)
     sweep(8, 20, 12, pa2, pb2, s2, w2)
 
-    pz = pair_weight(lane_out - 2 * lane_in)
-    py = pair_weight(ring(iota((32, 32), 0), 24, 32) - 2 * ring(iota((32, 32), 1), 20, 32))
     for k in range(12):
-        t_ref[k * 32 : k * 32 + 32] = dot(py, pb2[k + 8])
-    u_ref[:384] = dot(t_ref[:384], pz)
+        v_ref[k * 16 : k * 16 + 8] = pb2[k + 8, :8]
+        v_ref[k * 16 + 8 : k * 16 + 16] = jnp.where(sub8 < 4, pb2[k + 8, 8:16], pb2[k + 8, 24:])
+    rise = dot(v_ref[:192], double)
     for k in range(12):
-        rise = u_ref[k * 32 : k * 32 + 32]
-        pa1[2 * k + 2] = down1_ref[2 * k + 2] + rise
-        pa1[2 * k + 3] = down1_ref[2 * k + 3] + rise
+        twice(u_ref, k * 32, rise[k * 16 : k * 16 + 16])
+    for k in range(12):
+        for j in (2 * k + 2, 2 * k + 3):
+            pa1[j] = down1_ref[j] + u_ref[k * 32 : k * 32 + 32]
     w1 = (wx1, wy1, wz1, q1)
     sweep(3, 25, 11, pa1, pb1, s1, w1)
     sweep(4, 24, 10, pb1, pa1, s1, w1)
 
-    pz = pair_weight(iota((128, 256), 1) - 2 * iota((128, 256), 0))
-    py = pair_weight(ring(iota((40, 32), 0), 36, 40) - 2 * ring(iota((40, 32), 1), 24, 32))
     for k in range(20):
-        t_ref[k * 40 : k * 40 + 40] = dot(py, pa1[k + 4])
-    v_ref[...] = dot(t_ref[...], pz)
-
-    def rise0(k, n):
-        for i in range(n):
-            rise = v_ref[pl.ds(pl.multiple_of((k + i) * 40, 8), 40)]
-            for j in (2 * (k + i) + 1, 2 * (k + i) + 2):
-                pa0[j] = down0_ref[j] + rise
+        v_ref[k * 24 : k * 24 + 16] = pa1[k + 4, :16]
+        v_ref[k * 24 + 16 : k * 24 + 24] = jnp.where(
+            sub8 < 2, pa1[k + 4, 16:24], pltpu.roll(pa1[k + 4, 24:], 4, 0)
+        )
+    for z, out in ((0, rise_lo), (128, rise_hi)):
+        double = pair_weight(lane_out + z - 2 * lane_in)
+        rise = dot(v_ref[...], double)
+        for k in range(20):
+            twice(out, k * 48, rise[k * 24 : k * 24 + 24])
+
+    def rise_at(k):
+        here = pl.ds(k * 48 if isinstance(k, int) else pl.multiple_of(k * 48, 8), 40)
+        return jnp.concatenate([rise_lo[here], rise_hi[here]], 1)
 
     low_x, high_x = edge("gx")
     row8 = iota((8, 256), 0)
@@ -505,19 +539,18 @@
             [jnp.concatenate(tiles[:2], 1), jnp.concatenate(tiles[2:], 1), jnp.zeros((8, 256), F32)], 0
         )
 
-    pa0[2] = v_ref[:40] + blank(low_x, plane_of(plane_lo, 11), 0.0)
-    pa0[N0 - 3] = v_ref[760:] + blank(high_x, plane_of(plane_hi, 11), 0.0)
+    pa0[2] = rise_at(0) + blank(low_x, plane_of(plane_lo, 11), 0.0)
+    pa0[N0 - 3] = rise_at(19) + blank(high_x, plane_of(plane_hi, 11), 0.0)
     for k in range(4):
         h, z = k // 2 * 16, k % 2 * 128
         row_ref[0, h : h + 16, z : z + 128] = blank(high_y, rows_hi[N1 + k], 0.0)
         row_ref[1, h : h + 16, z : z + 128] = blank(low_y, rows_lo[N1 + k], 0.0)
     for j in (3, 4, 37, 38):
-        k = (j - 1) // 2
-        pa0[j] = down0_ref[j] + v_ref[k * 40 : k * 40 + 40]
+        pa0[j] = down0_ref[j] + rise_at((j - 1) // 2)
 
     def rise0(k, n):
         for i in range(n):
-            rise = v_ref[pl.ds(pl.multiple_of((k + i) * 40, 8), 40)]
+            rise = rise_at(k + i)
             for j in (2 * (k + i) + 1, 2 * (k + i) + 2):
                 pa0[j, :32] = down0_ref[j, :32] + rise[:32]
                 above = row_ref[0, pl.ds(j - X0, 1)]
@@ -565,9 +598,10 @@
         + buf(2, N1, 32, 128)
         + buf(9, N2, 32, 128)
         + buf(8, N3, 16, 128)
-        + buf(1, 800, 128)
+        + buf(1, 384, 256)
         + buf(1, 384, 128)
-        + buf(1, 800, 256)
+        + buf(1, 480, 128)
+        + buf(2, 960, 128)
         + buf(2, 32, 32, 256)
         + buf(1, 2, 32, 256)
         + [pltpu.SemaphoreType.DMA((2, 4))]
@@ -586,8 +620,7 @@
 
 
 def shards(source, phase):
-    msg = [kept(32, 8, 256)] * 2
-    ylo, yhi = both(*call(send_rows_kernel, "send_rows", msg, [], 4, source, phase), "gy")
+    ylo, yhi = both(*send_rows(source, phase), "gy")
     msg = [kept(7, 40, 256)] * 2
     dn0, up0 = call(send_planes_kernel, "send_planes", msg, [], 4, source, phase, ylo, yhi)
     xlo, xhi = both(dn0, up0, "gx")
@@ -597,8 +630,8 @@
     ylo1, yhi1 = both(*pack1(src1, mob1, xlo1, xhi1, rows_dn, rows_up), "gy")
     own2, dn2, up2, *level1 = down1(src1, mob1, xlo1, xhi1, ylo1, yhi1)
     xlo, xhi = both(dn2, up2, "gx")
-    ext = pack2(own2, xlo, xhi)
-    ylo, yhi = both(ext, ext, "gy")
+    ext, ext_up = pack2(own2, xlo, xhi)
+    ylo, yhi = both(ext, ext_up, "gy")
     level0 = (wx0, wy0, wz0, q0, s0, p0, xlo1, xhi1, ylo1, yhi1)
     return tuple(way_up(ext, ylo, yhi, *level1, *level0))
 

time: 73.7 us -> 68.6 us (0.931); the launches traced: 72.8 us -> 68.5 us
  local copies, waits for them, and re-layouts: 2.44 us -> 0.01 us
  Pallas kernels: 23 us -> 21.2 us
  waiting for transfers between devices: 23.4 us -> 25.1 us
  starting transfers between devices: 23 us -> 21.3 us
    unnamed x4, local copies, waits for them, and re-layouts: 2.44 us -> 0.01 us
    pallas_call x8, Pallas kernels: 23 us -> 21.2 us  [call(): pl.pallas_call(kernel, in_specs=[VM] * len(operands) if in_specs is None...]
    ppermute x12, starting transfers between devices: 23 us -> 21.3 us  [shift(): lax.ppermute(a, axis, [(i, (i + step) % count) for i in range(count)])]
    ppermute x12, waiting for transfers between devices: 23.4 us -> 25.1 us  [shift(): lax.ppermute(a, axis, [(i, (i + step) % count) for i in range(count)])]
  transfers between devices with their start and end apart: 12 -> 12, of which waited for: 8 -> 9; matrix products, arithmetic and copies ran while one was open for 0% -> 0% of each run, Pallas kernels for 8% -> 9%
where the time goes in v3:
time: 68.6 us; the launch traced here: 68.5 us
  waiting for transfers between devices  25.1 us (37%)
  starting transfers between devices  21.3 us (31%)
  Pallas kernels  21.2 us (31%)
  between operations  0.87 us (1%)
    ppermute x12, waiting for transfers between devices, shift(): lax.ppermute(a, axis, [(i, (i + step) % count) for i in range(count)])  25.1 us
    ppermute x12, starting transfers between devices, shift(): lax.ppermute(a, axis, [(i, (i + step) % count) for i in range(count)])  21.3 us
    pallas_call x8, Pallas kernels, call(): pl.pallas_call(kernel, in_specs=[VM] * len(operands) if in_specs is None...  21.2 us
  transfers between devices with their start and end apart: 12, of which 9 were waited for; matrix products, arithmetic and copies ran while one was open for 0% of the time, Pallas kernels for 9%

profile of v3, /device:TPU:25, one launch (start us, length us, event | category | flops | bytes accessed | tf_op | source)
XLA Modules:
  0.0 68.5 jit_solution(13681841852075183718)
XLA Ops:
  0.6 0.0 copy-start.1
  0.6 0.0 copy-start
  0.6 1.4 %send_rows.1 = (f32[32,8,256]{2,1,0:T(8,128)S(1)}, f32[32,8,256]{2,1,0:T(8,128)S(1)}) custom-call(f32[32,32,256]{2,1,0:T(8,128)} %s_in.3, s32[32,32,256]{2,1,0:T(8,128)} %f_in.3), custom_call_target="tpu_custom_call" | custom-call | tf_op jit(solution)/shard_map/send_rows/pallas_call | solution.py:201
  2.1 2.3 %collective-permute-start = (f32[32,8,256]{2,1,0:T(8,128)S(1)}, f32[32,8,256]{2,1,0:T(8,128)S(1)}, u32[]{:S(2)}, u32[]{:S(2)}) collective-permute-start(f32[32,8,256]{2,1,0:T(8,128)S(1)} %get-tuple-element.41), channel_id=1, source_target_pairs={{0,1},{1,2},{2,3},{3,4},{4,5},{5,6},{6,7},{7,0},{8,9},{9,10},{10,1... | collective-permute-start | bytes 786440 | tf_op jit(solution)/shard_map/ppermute | solution.py:615
  4.3 0.0 collective-permute-start.1
  4.4 3.3 %collective-permute-done.ylo = f32[32,8,256]{2,1,0:T(8,128)S(1)} collective-permute-done((f32[32,8,256]{2,1,0:T(8,128)S(1)}, f32[32,8,256]{2,1,0:T(8,128)S(1)}, u32[]{:S(2)}, u32[]{:S(2)}) %collective-permute-start) | collective-permute-done | bytes 262176 | tf_op jit(solution)/shard_map/ppermute | solution.py:615
  7.7 3.7 %collective-permute-done.1.yhi = f32[32,8,256]{2,1,0:T(8,128)S(1)} collective-permute-done((f32[32,8,256]{2,1,0:T(8,128)S(1)}, f32[32,8,256]{2,1,0:T(8,128)S(1)}, u32[]{:S(2)}, u32[]{:S(2)}) %collective-permute-start.1) | collective-permute-done | bytes 262176 | tf_op jit(solution)/shard_map/ppermute | solution.py:615
  11.4 0.0 copy-done.1
  11.4 0.0 copy-done
  11.4 0.1 collective-permute-start.2
  11.5 6.1 %collective-permute-start.3 = (f32[7,40,256]{2,1,0:T(8,128)S(1)}, f32[7,40,256]{2,1,0:T(8,128)S(1)}, u32[]{:S(2)}, u32[]{:S(2)}) collective-permute-start(f32[7,40,256]{2,1,0:T(8,128)S(1)} %get-tuple-element.44), channel_id=1, source_target_pairs={{0,248},{8,0},{16,8},{24,16},{32,24},{40,32},{48,40},{56,48},{64,5... | collective-permute-start | bytes 860168 | tf_op jit(solution)/shard_map/ppermute | solution.py:615
  17.6 5.9 %inner0.1 = (f32[42,40,256]{2,1,0:T(8,128)S(1)}, f32[42,40,256]{2,1,0:T(8,128)S(1)}, f32[42,40,256]{2,1,0:T(8,128)S(1)}, f32[42,40,256]{2,1,0:T(8,128)S(1)}, f32...) custom-call(f32[32,32,256]{2,1,0:T(8,128)S(1)} %copy-done, ...), custom_call_target="tpu_custom_call" | custom-call | tf_op jit(solution)/shard_map/inner0/pallas_call | solution.py:201
  23.5 0.3 collective-permute-done.2.xlo
  23.8 0.0 collective-permute-done.3.xhi
  23.8 1.6 %outer0.1 = (f32[42,40,256]{2,1,0:T(8,128)S(1)}, f32[42,40,256]{2,1,0:T(8,128)S(1)}, f32[42,40,256]{2,1,0:T(8,128)S(1)}, f32[42,40,256]{2,1,0:T(8,128)S(1)}, f32...) custom-call(f32[7,40,256]{2,1,0:T(8,128)S(1)} %collective-permute-do, ...), custom_call_target="tpu_custom_call", output_to_operand_aliasing={{0}: (3, {}), {1}: (4, {}), {2}: (5, {}), {3}: (6, {}), {4}... | custom-call | tf_op jit(solution)/shard_map/outer0/pallas_call | solution.py:201
  25.4 0.1 collective-permute-start.4
  25.5 5.2 %collective-permute-start.5 = (f32[15,16,128]{2,1,0:T(8,128)S(1)}, f32[15,16,128]{2,1,0:T(8,128)S(1)}, u32[]{:S(2)}, u32[]{:S(2)}) collective-permute-start(f32[15,16,128]{2,1,0:T(8,128)S(1)} %get-tuple-element.58), channel_id=1, source_target_pairs={{0,248},{8,0},{16,8},{24,16},{32,24},{40,32},{48,40},{56,48},{64,5... | collective-permute-start | bytes 368648 | tf_op jit(solution)/shard_map/ppermute | solution.py:615
  30.7 3.5 %collective-permute-done.4.xlo.plane_lo = f32[15,16,128]{2,1,0:T(8,128)S(1)} collective-permute-done((f32[15,16,128]{2,1,0:T(8,128)S(1)}, f32[15,16,128]{2,1,0:T(8,128)S(1)}, u32[]{:S(2)}, u32[]{:S(2)}) %collective-permute-start.4) | collective-permute-done | bytes 122912 | tf_op jit(solution)/shard_map/ppermute | solution.py:615
  34.2 0.0 collective-permute-done.5.xhi.plane_hi
  34.3 1.2 %collective-permute-start.6 = (f32[32,16,128]{2,1,0:T(8,128)S(1)}, f32[32,16,128]{2,1,0:T(8,128)S(1)}, u32[]{:S(2)}, u32[]{:S(2)}) collective-permute-start(f32[32,16,128]{2,1,0:T(8,128)S(1)} %get-tuple-element.61), channel_id=1, source_target_pairs={{0,1},{1,2},{2,3},{3,4},{4,5},{5,6},{6,7},{7,0},{8,9},{9,10},{10,1... | collective-permute-start | bytes 786440 | tf_op jit(solution)/shard_map/ppermute | solution.py:615
  35.5 0.0 collective-permute-start.7
  35.5 3.3 %collective-permute-done.6.ylo.rows_lo = f32[32,16,128]{2,1,0:T(8,128)S(1)} collective-permute-done((f32[32,16,128]{2,1,0:T(8,128)S(1)}, f32[32,16,128]{2,1,0:T(8,128)S(1)}, u32[]{:S(2)}, u32[]{:S(2)}) %collective-permute-start.6) | collective-permute-done | bytes 262176 | tf_op jit(solution)/shard_map/ppermute | solution.py:615
  38.8 3.7 %collective-permute-done.7.yhi.rows_hi = f32[32,16,128]{2,1,0:T(8,128)S(1)} collective-permute-done((f32[32,16,128]{2,1,0:T(8,128)S(1)}, f32[32,16,128]{2,1,0:T(8,128)S(1)}, u32[]{:S(2)}, u32[]{:S(2)}) %collective-permute-start.7) | collective-permute-done | bytes 262176 | tf_op jit(solution)/shard_map/ppermute | solution.py:615
  42.5 2.2 %down1.1 = (f32[8,16,128]{2,1,0:T(8,128)S(1)}, f32[10,16,128]{2,1,0:T(8,128)S(1)}, f32[10,16,128]{2,1,0:T(8,128)S(1)}, f32[28,32,128]{2,1,0:T(8,128)S(1)}, f32[2...) custom-call(f32[16,16,128]{2,1,0:T(8,128)S(1)} %get-tuple-element.56, ...), custom_call_target="tpu_custom_call" | custom-call | tf_op jit(solution)/shard_map/down1/pallas_call | solution.py:201
  44.6 0.1 collective-permute-start.8
  44.7 5.1 %collective-permute-start.9 = (f32[10,16,128]{2,1,0:T(8,128)S(1)}, f32[10,16,128]{2,1,0:T(8,128)S(1)}, u32[]{:S(2)}, u32[]{:S(2)}) collective-permute-start(f32[10,16,128]{2,1,0:T(8,128)S(1)} %get-tuple-element.65), channel_id=1, source_target_pairs={{0,248},{8,0},{16,8},{24,16},{32,24},{40,32},{48,40},{56,48},{64,5... | collective-permute-start | bytes 245768 | tf_op jit(solution)/shard_map/ppermute | solution.py:615
  49.8 1.6 %collective-permute-done.8.xlo = f32[10,16,128]{2,1,0:T(8,128)S(1)} collective-permute-done((f32[10,16,128]{2,1,0:T(8,128)S(1)}, f32[10,16,128]{2,1,0:T(8,128)S(1)}, u32[]{:S(2)}, u32[]{:S(2)}) %collective-permute-start.8) | collective-permute-done | bytes 81952 | tf_op jit(solution)/shard_map/ppermute | solution.py:615
  51.4 0.0 collective-permute-done.9.xhi
  51.4 1.2 %collective-permute-start.10 = (f32[35,8,128]{2,1,0:T(8,128)S(1)}, f32[35,8,128]{2,1,0:T(8,128)S(1)}, u32[]{:S(2)}, u32[]{:S(2)}) collective-permute-start(f32[35,8,128]{2,1,0:T(8,128)S(1)} %get-tuple-element.67), channel_id=1, source_target_pairs={{0,1},{1,2},{2,3},{3,4},{4,5},{5,6},{6,7},{7,0},{8,9},{9,10},{10,1... | collective-permute-start | bytes 430088 | tf_op jit(solution)/shard_map/ppermute | solution.py:615
  52.6 0.0 collective-permute-start.11
  52.6 2.1 %collective-permute-done.10.ylo = f32[35,8,128]{2,1,0:T(8,128)S(1)} collective-permute-done((f32[35,8,128]{2,1,0:T(8,128)S(1)}, f32[35,8,128]{2,1,0:T(8,128)S(1)}, u32[]{:S(2)}, u32[]{:S(2)}) %collective-permute-start.10) | collective-permute-done | bytes 143392 | tf_op jit(solution)/shard_map/ppermute | solution.py:615
  54.7 3.7 %collective-permute-done.11.yhi = f32[35,8,128]{2,1,0:T(8,128)S(1)} collective-permute-done((f32[35,8,128]{2,1,0:T(8,128)S(1)}, f32[35,8,128]{2,1,0:T(8,128)S(1)}, u32[]{:S(2)}, u32[]{:S(2)}) %collective-permute-start.11) | collective-permute-done | bytes 143392 | tf_op jit(solution)/shard_map/ppermute | solution.py:615
  58.3 10.0 %way_up.1 = (f32[32,32,256]{2,1,0:T(8,128)}, f32[32,32,256]{2,1,0:T(8,128)}) custom-call(f32[35,8,128]{2,1,0:T(8,128)S(1)} %get-tuple-element.66.ext, f32[35,8,128]{2,1,0:T(8,128)S(1)} %collective-permute-done.10.ylo, f32[35,8,128]{2,1,0:T(8,128)S(1)} %collective-permute-done.11.yhi, f32[28,32,128]{2,1,0:T(8,128)S(1)} %get-tuple-element.68.s1, ...), custom_call_target="tpu_custom_call" | custom-call | tf_op jit(solution)/shard_map/way_up/pallas_call | solution.py:201
  (3 shorter events, 0.1 us)
Async XLA Ops:
  0.6 10.7 %copy-start.1 = (s32[32,32,256]{2,1,0:T(8,128)S(1)}, s32[32,32,256]{2,1,0:T(8,128)}, u32[]{:S(2)}) copy-start(s32[32,32,256]{2,1,0:T(8,128)} %f_in.3) | copy-start | bytes 3145732
  0.6 10.7 %copy-start = (f32[32,32,256]{2,1,0:T(8,128)S(1)}, f32[32,32,256]{2,1,0:T(8,128)}, u32[]{:S(2)}) copy-start(f32[32,32,256]{2,1,0:T(8,128)} %s_in.3) | copy-start | bytes 3145732
  2.1 5.6 %collective-permute-start = (f32[32,8,256]{2,1,0:T(8,128)S(1)}, f32[32,8,256]{2,1,0:T(8,128)S(1)}, u32[]{:S(2)}, u32[]{:S(2)}) collective-permute-start(f32[32,8,256]{2,1,0:T(8,128)S(1)} %get-tuple-element.41), channel_id=1, source_target_pairs={{0,1},{1,2},{2,3},{3,4},{4,5},{5,6},{6,7},{7,0},{8,9},{9,10},{10,1... | collective-permute-start | bytes 786440 | tf_op jit(solution)/shard_map/ppermute | solution.py:615
  4.3 7.0 %collective-permute-start.1 = (f32[32,8,256]{2,1,0:T(8,128)S(1)}, f32[32,8,256]{2,1,0:T(8,128)S(1)}, u32[]{:S(2)}, u32[]{:S(2)}) collective-permute-start(f32[32,8,256]{2,1,0:T(8,128)S(1)} %get-tuple-element.42), channel_id=1, source_target_pairs={{0,7},{1,0},{2,1},{3,2},{4,3},{5,4},{6,5},{7,6},{8,15},{9,8},{10,9... | collective-permute-start | bytes 786440 | tf_op jit(solution)/shard_map/ppermute | solution.py:615
  11.4 12.4 %collective-permute-start.2 = (f32[7,40,256]{2,1,0:T(8,128)S(1)}, f32[7,40,256]{2,1,0:T(8,128)S(1)}, u32[]{:S(2)}, u32[]{:S(2)}) collective-permute-start(f32[7,40,256]{2,1,0:T(8,128)S(1)} %get-tuple-element.43), channel_id=1, source_target_pairs={{0,8},{8,16},{16,24},{24,32},{32,40},{40,48},{48,56},{56,64},{64,7... | collective-permute-start | bytes 860168 | tf_op jit(solution)/shard_map/ppermute | solution.py:615
  11.5 12.3 %collective-permute-start.3 = (f32[7,40,256]{2,1,0:T(8,128)S(1)}, f32[7,40,256]{2,1,0:T(8,128)S(1)}, u32[]{:S(2)}, u32[]{:S(2)}) collective-permute-start(f32[7,40,256]{2,1,0:T(8,128)S(1)} %get-tuple-element.44), channel_id=1, source_target_pairs={{0,248},{8,0},{16,8},{24,16},{32,24},{40,32},{48,40},{56,48},{64,5... | collective-permute-start | bytes 860168 | tf_op jit(solution)/shard_map/ppermute | solution.py:615
  25.4 8.8 %collective-permute-start.4 = (f32[15,16,128]{2,1,0:T(8,128)S(1)}, f32[15,16,128]{2,1,0:T(8,128)S(1)}, u32[]{:S(2)}, u32[]{:S(2)}) collective-permute-start(f32[15,16,128]{2,1,0:T(8,128)S(1)} %get-tuple-element.57), channel_id=1, source_target_pairs={{0,8},{8,16},{16,24},{24,32},{32,40},{40,48},{48,56},{56,64},{64,7... | collective-permute-start | bytes 368648 | tf_op jit(solution)/shard_map/ppermute | solution.py:615
  25.5 8.7 %collective-permute-start.5 = (f32[15,16,128]{2,1,0:T(8,128)S(1)}, f32[15,16,128]{2,1,0:T(8,128)S(1)}, u32[]{:S(2)}, u32[]{:S(2)}) collective-permute-start(f32[15,16,128]{2,1,0:T(8,128)S(1)} %get-tuple-element.58), channel_id=1, source_target_pairs={{0,248},{8,0},{16,8},{24,16},{32,24},{40,32},{48,40},{56,48},{64,5... | collective-permute-start | bytes 368648 | tf_op jit(solution)/shard_map/ppermute | solution.py:615
  34.3 4.5 %collective-permute-start.6 = (f32[32,16,128]{2,1,0:T(8,128)S(1)}, f32[32,16,128]{2,1,0:T(8,128)S(1)}, u32[]{:S(2)}, u32[]{:S(2)}) collective-permute-start(f32[32,16,128]{2,1,0:T(8,128)S(1)} %get-tuple-element.61), channel_id=1, source_target_pairs={{0,1},{1,2},{2,3},{3,4},{4,5},{5,6},{6,7},{7,0},{8,9},{9,10},{10,1... | collective-permute-start | bytes 786440 | tf_op jit(solution)/shard_map/ppermute | solution.py:615
  35.5 7.0 %collective-permute-start.7 = (f32[32,16,128]{2,1,0:T(8,128)S(1)}, f32[32,16,128]{2,1,0:T(8,128)S(1)}, u32[]{:S(2)}, u32[]{:S(2)}) collective-permute-start(f32[32,16,128]{2,1,0:T(8,128)S(1)} %get-tuple-element.62), channel_id=1, source_target_pairs={{0,7},{1,0},{2,1},{3,2},{4,3},{5,4},{6,5},{7,6},{8,15},{9,8},{10,9... | collective-permute-start | bytes 786440 | tf_op jit(solution)/shard_map/ppermute | solution.py:615
  44.6 6.7 %collective-permute-start.8 = (f32[10,16,128]{2,1,0:T(8,128)S(1)}, f32[10,16,128]{2,1,0:T(8,128)S(1)}, u32[]{:S(2)}, u32[]{:S(2)}) collective-permute-start(f32[10,16,128]{2,1,0:T(8,128)S(1)} %get-tuple-element.64), channel_id=1, source_target_pairs={{0,8},{8,16},{16,24},{24,32},{32,40},{40,48},{48,56},{56,64},{64,7... | collective-permute-start | bytes 245768 | tf_op jit(solution)/shard_map/ppermute | solution.py:615
  44.7 6.6 %collective-permute-start.9 = (f32[10,16,128]{2,1,0:T(8,128)S(1)}, f32[10,16,128]{2,1,0:T(8,128)S(1)}, u32[]{:S(2)}, u32[]{:S(2)}) collective-permute-start(f32[10,16,128]{2,1,0:T(8,128)S(1)} %get-tuple-element.65), channel_id=1, source_target_pairs={{0,248},{8,0},{16,8},{24,16},{32,24},{40,32},{48,40},{56,48},{64,5... | collective-permute-start | bytes 245768 | tf_op jit(solution)/shard_map/ppermute | solution.py:615
  51.4 3.2 %collective-permute-start.10 = (f32[35,8,128]{2,1,0:T(8,128)S(1)}, f32[35,8,128]{2,1,0:T(8,128)S(1)}, u32[]{:S(2)}, u32[]{:S(2)}) collective-permute-start(f32[35,8,128]{2,1,0:T(8,128)S(1)} %get-tuple-element.67), channel_id=1, source_target_pairs={{0,1},{1,2},{2,3},{3,4},{4,5},{5,6},{6,7},{7,0},{8,9},{9,10},{10,1... | collective-permute-start | bytes 430088 | tf_op jit(solution)/shard_map/ppermute | solution.py:615
  52.6 5.7 %collective-permute-start.11 = (f32[35,8,128]{2,1,0:T(8,128)S(1)}, f32[35,8,128]{2,1,0:T(8,128)S(1)}, u32[]{:S(2)}, u32[]{:S(2)}) collective-permute-start(f32[35,8,128]{2,1,0:T(8,128)S(1)} %get-tuple-element.66.ext), channel_id=1, source_target_pairs={{0,7},{1,0},{2,1},{3,2},{4,3},{5,4},{6,5},{7,6},{8,15},{9,8},{10,9... | collective-permute-start | bytes 430088 | tf_op jit(solution)/shard_map/ppermute | solution.py:615

commit v4 on v3

--- a/solution.py
+++ b/solution.py
@@ -48,7 +48,18 @@
     return jnp.where((offset == 0) | (offset == 1), 1.0, 0.0).astype(F32)
 
 
-def dot(a, b):
+def dot(a, b, exact=False):
+    high, b = a.astype(jnp.bfloat16), b.astype(jnp.bfloat16)
+    if exact:
+        return jnp.dot(high, b, preferred_element_type=F32)
+    low = (a - high.astype(F32)).astype(jnp.bfloat16)
+    if a.shape[1] == 128:
+        both = jnp.concatenate([high, low], 1)
+        return jnp.dot(both, jnp.concatenate([b, b], 0), preferred_element_type=F32)
+    return jnp.dot(high, b, preferred_element_type=F32) + jnp.dot(low, b, preferred_element_type=F32)
+
+
+def full_dot(a, b):
     return jnp.dot(a, b, precision=lax.Precision.HIGHEST, preferred_element_type=F32)
 
 
@@ -85,6 +96,13 @@
                 ref[j + i] = value
 
     blocks(lo, hi, size, work)
+
+
+def planes_at(js, plane, refs):
+    results = [plane(j) for j in js]
+    for j, values in zip(js, results):
+        for ref, value in zip(refs, values):
+            ref[j] = value
 
 
 def weights_at(m_low, m, m_high, face, outside, full):
@@ -106,14 +124,17 @@
     return wx, wy, wz, q
 
 
-def weights_pass(lo, hi, size, m_ref, w, s_ref, p_ref, face, outside, full):
-    w[0][lo - 1] = face(m_ref[lo - 1], m_ref[lo])
-
+def weights_plane(m_ref, s_ref, face, outside, full):
     def plane(j):
         wx, wy, wz, q = weights_at(m_ref[j - 1], m_ref[j], m_ref[j + 1], face, outside, full)
         return wx, wy, wz, q, q * s_ref[j]
 
-    planes(lo, hi, size, plane, (*w, p_ref))
+    return plane
+
+
+def weights_pass(lo, hi, size, m_ref, w, s_ref, p_ref, face, outside, full):
+    w[0][lo - 1] = face(m_ref[lo - 1], m_ref[lo])
+    planes(lo, hi, size, weights_plane(m_ref, s_ref, face, outside, full), (*w, p_ref))
 
 
 def flow(j, p, p_ref, w):
@@ -125,21 +146,29 @@
     return along_x + along_y + along_z
 
 
-def sweep(lo, hi, size, p_ref, out_ref, s_ref, w):
+def sweep_plane(p_ref, s_ref, w):
     def plane(j):
         p = p_ref[j]
         return (KEEP * p + w[3][j] * (s_ref[j] + flow(j, p, p_ref, w)),)
 
-    planes(lo, hi, size, plane, (out_ref,))
-
-
-def remainder(lo, hi, size, p_ref, out_ref, s_ref, w):
+    return plane
+
+
+def sweep(lo, hi, size, p_ref, out_ref, s_ref, w):
+    planes(lo, hi, size, sweep_plane(p_ref, s_ref, w), (out_ref,))
+
+
+def remainder_plane(p_ref, s_ref, w):
     def plane(j):
         p, q = p_ref[j], w[3][j]
         r = s_ref[j] + flow(j, p, p_ref, w) - (OMEGA / q) * p
         return (jnp.where(q > 0.0, r, 0.0),)
 
-    planes(lo, hi, size, plane, (out_ref,))
+    return plane
+
+
+def remainder(lo, hi, size, p_ref, out_ref, s_ref, w):
+    planes(lo, hi, size, remainder_plane(p_ref, s_ref, w), (out_ref,))
 
 
 def halving(valid):
@@ -164,12 +193,12 @@
     ref[pl.ds(first + 1, count, stride=2)] = value
 
 
-def halve(count, r_ref, m_ref, t_ref, u_ref, valid):
+def halve(count, r_ref, m_ref, t_ref, u_ref, valid, product):
     for k in range(count):
         rows = slice(k * 32, k * 32 + 32)
         t_ref[rows, :128] = restrict_x(r_ref, 2 * k + 1) if 1 <= k < count - 1 else jnp.zeros((32, 128), F32)
         t_ref[rows, 128:] = (m_ref[2 * k + 2] + m_ref[2 * k + 3]) * (0.25 * 0.125)
-    packed = dot(t_ref[...], halving(valid))
+    packed = product(t_ref[...], halving(valid))
     for k in range(count):
         u_ref[k * 32 : k * 32 + 32] = halve_rows(packed[k * 32 : k * 32 + 32])
     return [every_other(u_ref, k * 32, 16) for k in range(count)]
@@ -242,6 +271,26 @@
     return call(send_rows_kernel, "send_rows", [kept(*part)] * 2, scratch, 4, *operands, in_specs=hbm)
 
 
+def load_kernel(s_hbm, f_hbm, sent, s_ref, f_ref, sems):
+    del sent
+    copies = [
+        pltpu.make_async_copy(a, b, sems.at[k]) for k, (a, b) in enumerate(((s_hbm, s_ref), (f_hbm, f_ref)))
+    ]
+    for copy in copies:
+        copy.start()
+    for copy in copies:
+        copy.wait()
+
+
+def load(source, phase, sent):
+    any_space = pl.BlockSpec(memory_space=pl.ANY)
+    hbm = [pl.BlockSpec(memory_space=pltpu.HBM)] * 2
+    operands = [pltpu.with_memory_space_constraint(x, pltpu.HBM) for x in (source, phase)]
+    out = [kept(32, 32, 256), pltpu.VMEM((32, 32, 256), jnp.int32)]
+    scratch = [pltpu.SemaphoreType.DMA((2,))]
+    return call(load_kernel, "load", out, scratch, 4, *operands, sent, in_specs=[*hbm, any_space])
+
+
 def halo_rows(lo, hi):
     low_y, high_y = edge("gy")
     above = iota((8, 256), 0) < 4
@@ -265,19 +314,26 @@
     return 0.25 * ((8.0 - n) * 0.125 + n * (0.125 * WATER))
 
 
-def rows_to_16():
-    fine_y = ring(iota((16, 40), 1), 36, 40)
-    return fine_y - 2 * iota((16, 40), 0)
-
-
 def lanes_to_128():
     return iota((256, 128), 0) - 2 * iota((256, 128), 1)
+
+
+def halve0(ks, r_ref, src1, t_ref, u_ref):
+    for i, k in enumerate(ks):
+        t_ref[i * 40 : i * 40 + 40] = restrict_x(r_ref, 2 * k + 4)
+    coarse = dot(t_ref[: len(ks) * 40], restrict_weight(lanes_to_128()))
+    for i in range(len(ks)):
+        t = coarse[i * 40 : i * 40 + 40]
+        above = up_y(t)
+        u_ref[i * 40 : i * 40 + 40] = (t + above) * 0.375 + (dn_y(t) + up_y(above)) * 0.125
+    for i, k in enumerate(ks):
+        src1[k] = every_other(u_ref, i * 40, 16)
 
 
 def inner0_kernel(
     s_in, f_in, ylo, yhi,
     s_ref, c_ref, wx, wy, wz, q_ref, p1, p2, r_ref, src1, mob1,
-    t_ref,
+    t_ref, u_ref,
 ):
     def own_planes(j, n):
         here, there = pl.ds(j, n), pl.ds(j + X0, n)
@@ -289,28 +345,25 @@
 
     blocks(0, 32, 4, own_planes)
     w = (wx, wy, wz, q_ref)
-    weights_pass(6, 36, 6, c_ref, w, s_ref, p1, face_code, OUT, True)
-    sweep(7, 35, 7, p1, p2, s_ref, w)
-    remainder(8, 34, 6, p2, r_ref, s_ref, w)
-
-    ry, rz = restrict_weight(rows_to_16()), restrict_weight(lanes_to_128())
-    my, mz = pair_weight(rows_to_16()), pair_weight(lanes_to_128())
-    for k in range(2, 14):
-        t_ref[k * 16 : k * 16 + 16] = dot(ry, restrict_x(r_ref, 2 * k + 4))
-    coarse = dot(t_ref[32:224], rz)
-    for k in range(2, 14):
-        src1[k] = coarse[k * 16 - 32 : k * 16 - 16]
+    weights_pass(6, 36, 10, c_ref, w, s_ref, p1, face_code, OUT, True)
+    sweep(7, 35, 14, p1, p2, s_ref, w)
+    remainder(8, 34, 13, p2, r_ref, s_ref, w)
+
+    halve0(range(2, 14), r_ref, src1, t_ref, u_ref)
     for k in range(16):
-        t_ref[k * 16 : k * 16 + 16] = dot(my, c_ref[2 * k + X0] + c_ref[2 * k + X0 + 1])
-    mobility = water_to_mobility(dot(t_ref[...], mz))
+        t_ref[k * 40 : k * 40 + 40] = c_ref[2 * k + X0] + c_ref[2 * k + X0 + 1]
+    water = dot(t_ref[...], pair_weight(lanes_to_128()), exact=True)
     for k in range(16):
-        mob1[k] = mobility[k * 16 : k * 16 + 16]
+        t = water[k * 40 : k * 40 + 40]
+        u_ref[k * 40 : k * 40 + 40] = t + up_y(t)
+    for k in range(16):
+        mob1[k] = water_to_mobility(every_other(u_ref, k * 40, 16))
 
 
 def inner0(source, phase, ylo, yhi):
     return call(
         inner0_kernel, "inner0", [kept(*BIG)] * 9 + [kept(16, 16, 128)] * 2,
-        [kept(256, 256)], 4, source, phase, ylo, yhi,
+        [kept(640, 256), kept(640, 128)], 4, source, phase, ylo, yhi,
     )
 
 
@@ -322,7 +375,7 @@
 def outer0_kernel(
     xlo, xhi, mob1, s_0, c_0, wx_0, wy_0, wz_0, q_0, p1_0, p2_0, r_0, src1_0,
     s_ref, c_ref, wx, wy, wz, q_ref, p1, p2, r_ref, src1, dn1, upw1, rows_dn, rows_up,
-    t_ref,
+    t_ref, u_ref,
 ):
     low_x, high_x = edge("gx")
     s_ref[2:5] = blank(low_x, xlo[:3], 0.0)
@@ -330,19 +383,12 @@
     s_ref[37:40] = blank(high_x, xhi[:3], 0.0)
     c_ref[37:41] = blank(high_x, xhi[3:], OUT)
     w = (wx, wy, wz, q_ref)
-    for lo in (2, 36):
-        weights_pass(lo, lo + 4, 4, c_ref, w, s_ref, p1, face_code, OUT, True)
-    for lo in (3, 35):
-        sweep(lo, lo + 4, 4, p1, p2, s_ref, w)
-    for lo in (4, 34):
-        remainder(lo, lo + 4, 4, p2, r_ref, s_ref, w)
-    ry, rz = restrict_weight(rows_to_16()), restrict_weight(lanes_to_128())
-    edges = (0, 1, 14, 15)
-    for i, k in enumerate(edges):
-        t_ref[i * 16 : i * 16 + 16] = dot(ry, restrict_x(r_ref, 2 * k + 4))
-    coarse = dot(t_ref[...], rz)
-    for i, k in enumerate(edges):
-        src1[k] = coarse[i * 16 : i * 16 + 16]
+    wx[1] = face_code(c_ref[1], c_ref[2])
+    wx[35] = face_code(c_ref[35], c_ref[36])
+    planes_at((2, 3, 4, 5, 36, 37, 38, 39), weights_plane(c_ref, s_ref, face_code, OUT, True), (*w, p1))
+    planes_at((3, 4, 5, 6, 35, 36, 37, 38), sweep_plane(p1, s_ref, w), (p2,))
+    planes_at((4, 5, 6, 7, 34, 35, 36, 37), remainder_plane(p2, s_ref, w), (r_ref,))
+    halve0((0, 1, 14, 15), r_ref, src1, t_ref, u_ref)
     dn1[:5] = src1[:5]
     dn1[5:11] = mob1[:6]
     lay_rows(dn1, 11, p2[X0 + 2, :32])
@@ -358,7 +404,7 @@
     return call(
         outer0_kernel, "outer0",
         [kept(*BIG)] * 9 + [kept(16, 16, 128)] + [kept(15, 16, 128)] * 2 + [kept(32, 256)] * 2,
-        [kept(64, 256)], 4, xlo, xhi, mob1, *state, aliases={3 + k: k for k in range(10)},
+        [kept(160, 256), kept(160, 128)], 4, xlo, xhi, mob1, *state, aliases={3 + k: k for k in range(10)},
     )
 
 
@@ -402,11 +448,11 @@
     m_ref[:, 24:] = blank(low_y, ylo[:N1, 8:], 0.0)
     w = (wx, wy, wz, q_ref)
 
-    weights_pass(1, N1 - 1, 13, m_ref, w, s_ref, p1, face_mean, 0.0, True)
-    sweep(2, N1 - 2, 12, p1, p2, s_ref, w)
-    remainder(3, N1 - 3, 11, p2, r_ref, s_ref, w)
-
-    for k, packed in enumerate(halve(12, r_ref, m_ref, t_ref, u_ref, 64)):
+    weights_pass(1, N1 - 1, 26, m_ref, w, s_ref, p1, face_mean, 0.0, True)
+    sweep(2, N1 - 2, 24, p1, p2, s_ref, w)
+    remainder(3, N1 - 3, 22, p2, r_ref, s_ref, w)
+
+    for k, packed in enumerate(halve(12, r_ref, m_ref, t_ref, u_ref, 64, full_dot)):
         pk_ref[k] = packed
     own2[...] = pk_ref[2:10]
     dn2[...] = pk_ref[2:12]
@@ -476,12 +522,12 @@
 
     w2 = (wx2, wy2, wz2, q2)
 
-    weights_pass(1, N2 - 1, 13, m2, w2, s2, pa2, face_mean, 0.0, False)
-    sweep(2, N2 - 2, 12, pa2, pb2, s2, w2)
-    remainder(3, N2 - 3, 11, pb2, r2, s2, w2)
+    weights_pass(1, N2 - 1, 26, m2, w2, s2, pa2, face_mean, 0.0, False)
+    sweep(2, N2 - 2, 24, pa2, pb2, s2, w2)
+    remainder(3, N2 - 3, 22, pb2, r2, s2, w2)
 
     lane16 = iota((16, 128), 1)
-    for k, packed in enumerate(halve(12, r2, m2, t_ref, u_ref, 32)):
+    for k, packed in enumerate(halve(12, r2, m2, t_ref, u_ref, 32, dot)):
         s3[k] = packed
         m3[k] = jnp.where(lane16 < 64, pltpu.roll(packed, 64, 1), 0.0)
     w3 = (wx3, wy3, wz3, q3)
@@ -499,7 +545,7 @@
     for k in range(8):
         for j in (2 * k + 6, 2 * k + 7):
             pb2[j] = pb2[j] + u_ref[k * 32 : k * 32 + 32]
-    sweep(7, 21, 7, pb2, pa2, s2, w2)
+    sweep(7, 21, 14, pb2, pa2, s2, w2)
     sweep(8, 20, 12, pa2, pb2, s2, w2)
 
     for k in range(12):
@@ -512,8 +558,8 @@
         for j in (2 * k + 2, 2 * k + 3):
             pa1[j] = down1_ref[j] + u_ref[k * 32 : k * 32 + 32]
     w1 = (wx1, wy1, wz1, q1)
-    sweep(3, 25, 11, pa1, pb1, s1, w1)
-    sweep(4, 24, 10, pb1, pa1, s1, w1)
+    sweep(3, 25, 22, pa1, pb1, s1, w1)
+    sweep(4, 24, 20, pb1, pa1, s1, w1)
 
     for k in range(20):
         v_ref[k * 24 : k * 24 + 16] = pa1[k + 4, :16]
@@ -560,8 +606,8 @@
 
     blocks(2, 18, 2, rise0)
     w0 = (wx0, wy0, wz0, q0)
-    sweep(3, N0 - 3, 6, pa0, pb0, s0, w0)
-    sweep(4, N0 - 4, 8, pb0, pa0, s0, w0)
+    sweep(3, N0 - 3, 12, pa0, pb0, s0, w0)
+    sweep(4, N0 - 4, 17, pb0, pa0, s0, w0)
 
     def out_copies(k, j):
         here = pl.ds(j, 8)
@@ -620,7 +666,9 @@
 
 
 def shards(source, phase):
-    ylo, yhi = both(*send_rows(source, phase), "gy")
+    dn0, up0 = send_rows(source, phase)
+    ylo, yhi = both(dn0, up0, "gy")
+    source, phase = load(source, phase, dn0)
     msg = [kept(7, 40, 256)] * 2
     dn0, up0 = call(send_planes_kernel, "send_planes", msg, [], 4, source, phase, ylo, yhi)
     xlo, xhi = both(dn0, up0, "gx")

time: 68.6 us -> 65.8 us (0.959)
  Pallas kernels: 21.2 us -> 18.9 us
    pallas_call x8 -> x9, Pallas kernels: 21.2 us -> 18.9 us  [call(): pl.pallas_call(kernel, in_specs=[VM] * len(operands) if in_specs is None...]
  transfers between devices with their start and end apart: 12 -> 12, of which waited for: 9 -> 9; matrix products, arithmetic and copies ran while one was open for 0% -> 0% of each run, Pallas kernels for 9% -> 10%
where the time goes in v4:
time: 65.8 us; the launch traced here: 65.6 us
  waiting for transfers between devices  24.6 us (37%)
  starting transfers between devices  21.3 us (32%)
  Pallas kernels  18.9 us (29%)
  between operations  0.87 us (1%)
    ppermute x12, waiting for transfers between devices, shift(): lax.ppermute(a, axis, [(i, (i + step) % count) for i in range(count)])  24.6 us
    ppermute x12, starting transfers between devices, shift(): lax.ppermute(a, axis, [(i, (i + step) % count) for i in range(count)])  21.3 us
    pallas_call x9, Pallas kernels, call(): pl.pallas_call(kernel, in_specs=[VM] * len(operands) if in_specs is None...  18.9 us
  transfers between devices with their start and end apart: 12, of which 9 were waited for; matrix products, arithmetic and copies ran while one was open for 0% of the time, Pallas kernels for 10%

profile of v4, /device:TPU:25, one launch (start us, length us, event | category | flops | bytes accessed | tf_op | source)
XLA Modules:
  0.0 65.6 jit_solution(12213595732798269892)
XLA Ops:
  0.6 1.3 %send_rows.1 = (f32[32,8,256]{2,1,0:T(8,128)S(1)}, f32[32,8,256]{2,1,0:T(8,128)S(1)}) custom-call(f32[32,32,256]{2,1,0:T(8,128)} %s_hbm.3, s32[32,32,256]{2,1,0:T(8,128)} %f_hbm.3), custom_call_target="tpu_custom_call" | custom-call | tf_op jit(solution)/shard_map/send_rows/pallas_call | solution.py:230
  1.9 2.3 %collective-permute-start = (f32[32,8,256]{2,1,0:T(8,128)S(1)}, f32[32,8,256]{2,1,0:T(8,128)S(1)}, u32[]{:S(2)}, u32[]{:S(2)}) collective-permute-start(f32[32,8,256]{2,1,0:T(8,128)S(1)} %get-tuple-element.46), channel_id=1, source_target_pairs={{0,1},{1,2},{2,3},{3,4},{4,5},{5,6},{6,7},{7,0},{8,9},{9,10},{10,1... | collective-permute-start | bytes 786440 | tf_op jit(solution)/shard_map/ppermute | solution.py:661
  4.2 0.0 collective-permute-start.1
  4.2 1.6 %load.1 = (f32[32,32,256]{2,1,0:T(8,128)S(1)}, s32[32,32,256]{2,1,0:T(8,128)S(1)}) custom-call(f32[32,32,256]{2,1,0:T(8,128)} %s_hbm.3, s32[32,32,256]{2,1,0:T(8,128)} %f_hbm.3, f32[32,8,256]{2,1,0:T(8,128)S(1)} %get-tuple-element.43.sent), custom_call_target="tpu_custom_call" | custom-call | tf_op jit(solution)/shard_map/load/pallas_call | solution.py:230
  5.8 1.7 %collective-permute-done.ylo = f32[32,8,256]{2,1,0:T(8,128)S(1)} collective-permute-done((f32[32,8,256]{2,1,0:T(8,128)S(1)}, f32[32,8,256]{2,1,0:T(8,128)S(1)}, u32[]{:S(2)}, u32[]{:S(2)}) %collective-permute-start) | collective-permute-done | bytes 262176 | tf_op jit(solution)/shard_map/ppermute | solution.py:661
  7.5 3.7 %collective-permute-done.1.yhi = f32[32,8,256]{2,1,0:T(8,128)S(1)} collective-permute-done((f32[32,8,256]{2,1,0:T(8,128)S(1)}, f32[32,8,256]{2,1,0:T(8,128)S(1)}, u32[]{:S(2)}, u32[]{:S(2)}) %collective-permute-start.1) | collective-permute-done | bytes 262176 | tf_op jit(solution)/shard_map/ppermute | solution.py:661
  11.2 0.1 collective-permute-start.2
  11.3 6.1 %collective-permute-start.3 = (f32[7,40,256]{2,1,0:T(8,128)S(1)}, f32[7,40,256]{2,1,0:T(8,128)S(1)}, u32[]{:S(2)}, u32[]{:S(2)}) collective-permute-start(f32[7,40,256]{2,1,0:T(8,128)S(1)} %get-tuple-element.48), channel_id=1, source_target_pairs={{0,248},{8,0},{16,8},{24,16},{32,24},{40,32},{48,40},{56,48},{64,5... | collective-permute-start | bytes 860168 | tf_op jit(solution)/shard_map/ppermute | solution.py:661
  17.4 4.9 %inner0.1 = (f32[42,40,256]{2,1,0:T(8,128)S(1)}, f32[42,40,256]{2,1,0:T(8,128)S(1)}, f32[42,40,256]{2,1,0:T(8,128)S(1)}, f32[42,40,256]{2,1,0:T(8,128)S(1)}, f32...) custom-call(f32[32,32,256]{2,1,0:T(8,128)S(1)} %get-tuple-element.44, ...), custom_call_target="tpu_custom_call" | custom-call | tf_op jit(solution)/shard_map/inner0/pallas_call | solution.py:230
  22.3 1.3 %collective-permute-done.2.xlo = f32[7,40,256]{2,1,0:T(8,128)S(1)} collective-permute-done((f32[7,40,256]{2,1,0:T(8,128)S(1)}, f32[7,40,256]{2,1,0:T(8,128)S(1)}, u32[]{:S(2)}, u32[]{:S(2)}) %collective-permute-start.2) | collective-permute-done | bytes 286752 | tf_op jit(solution)/shard_map/ppermute | solution.py:661
  23.6 0.0 collective-permute-done.3.xhi
  23.6 1.5 %outer0.1 = (f32[42,40,256]{2,1,0:T(8,128)S(1)}, f32[42,40,256]{2,1,0:T(8,128)S(1)}, f32[42,40,256]{2,1,0:T(8,128)S(1)}, f32[42,40,256]{2,1,0:T(8,128)S(1)}, f32...) custom-call(f32[7,40,256]{2,1,0:T(8,128)S(1)} %collective-permute-do, ...), custom_call_target="tpu_custom_call", output_to_operand_aliasing={{0}: (3, {}), {1}: (4, {}), {2}: (5, {}), {3}: (6, {}), {4}... | custom-call | tf_op jit(solution)/shard_map/outer0/pallas_call | solution.py:230
  25.1 0.1 collective-permute-start.4
  25.1 5.2 %collective-permute-start.5 = (f32[15,16,128]{2,1,0:T(8,128)S(1)}, f32[15,16,128]{2,1,0:T(8,128)S(1)}, u32[]{:S(2)}, u32[]{:S(2)}) collective-permute-start(f32[15,16,128]{2,1,0:T(8,128)S(1)} %get-tuple-element.62), channel_id=1, source_target_pairs={{0,248},{8,0},{16,8},{24,16},{32,24},{40,32},{48,40},{56,48},{64,5... | collective-permute-start | bytes 368648 | tf_op jit(solution)/shard_map/ppermute | solution.py:661
  30.4 3.5 %collective-permute-done.4.xlo.plane_lo = f32[15,16,128]{2,1,0:T(8,128)S(1)} collective-permute-done((f32[15,16,128]{2,1,0:T(8,128)S(1)}, f32[15,16,128]{2,1,0:T(8,128)S(1)}, u32[]{:S(2)}, u32[]{:S(2)}) %collective-permute-start.4) | collective-permute-done | bytes 122912 | tf_op jit(solution)/shard_map/ppermute | solution.py:661
  33.9 0.0 collective-permute-done.5.xhi.plane_hi
  33.9 1.2 %collective-permute-start.6 = (f32[32,16,128]{2,1,0:T(8,128)S(1)}, f32[32,16,128]{2,1,0:T(8,128)S(1)}, u32[]{:S(2)}, u32[]{:S(2)}) collective-permute-start(f32[32,16,128]{2,1,0:T(8,128)S(1)} %get-tuple-element.65), channel_id=1, source_target_pairs={{0,1},{1,2},{2,3},{3,4},{4,5},{5,6},{6,7},{7,0},{8,9},{9,10},{10,1... | collective-permute-start | bytes 786440 | tf_op jit(solution)/shard_map/ppermute | solution.py:661
  35.2 0.0 collective-permute-start.7
  35.2 3.3 %collective-permute-done.6.ylo.rows_lo = f32[32,16,128]{2,1,0:T(8,128)S(1)} collective-permute-done((f32[32,16,128]{2,1,0:T(8,128)S(1)}, f32[32,16,128]{2,1,0:T(8,128)S(1)}, u32[]{:S(2)}, u32[]{:S(2)}) %collective-permute-start.6) | collective-permute-done | bytes 262176 | tf_op jit(solution)/shard_map/ppermute | solution.py:661
  38.5 3.7 %collective-permute-done.7.yhi.rows_hi = f32[32,16,128]{2,1,0:T(8,128)S(1)} collective-permute-done((f32[32,16,128]{2,1,0:T(8,128)S(1)}, f32[32,16,128]{2,1,0:T(8,128)S(1)}, u32[]{:S(2)}, u32[]{:S(2)}) %collective-permute-start.7) | collective-permute-done | bytes 262176 | tf_op jit(solution)/shard_map/ppermute | solution.py:661
  42.2 1.8 %down1.1 = (f32[8,16,128]{2,1,0:T(8,128)S(1)}, f32[10,16,128]{2,1,0:T(8,128)S(1)}, f32[10,16,128]{2,1,0:T(8,128)S(1)}, f32[28,32,128]{2,1,0:T(8,128)S(1)}, f32[2...) custom-call(f32[16,16,128]{2,1,0:T(8,128)S(1)} %get-tuple-element.60, ...), custom_call_target="tpu_custom_call" | custom-call | tf_op jit(solution)/shard_map/down1/pallas_call | solution.py:230
  44.0 0.1 collective-permute-start.8
  44.1 5.1 %collective-permute-start.9 = (f32[10,16,128]{2,1,0:T(8,128)S(1)}, f32[10,16,128]{2,1,0:T(8,128)S(1)}, u32[]{:S(2)}, u32[]{:S(2)}) collective-permute-start(f32[10,16,128]{2,1,0:T(8,128)S(1)} %get-tuple-element.69), channel_id=1, source_target_pairs={{0,248},{8,0},{16,8},{24,16},{32,24},{40,32},{48,40},{56,48},{64,5... | collective-permute-start | bytes 245768 | tf_op jit(solution)/shard_map/ppermute | solution.py:661
  49.2 1.6 %collective-permute-done.8.xlo = f32[10,16,128]{2,1,0:T(8,128)S(1)} collective-permute-done((f32[10,16,128]{2,1,0:T(8,128)S(1)}, f32[10,16,128]{2,1,0:T(8,128)S(1)}, u32[]{:S(2)}, u32[]{:S(2)}) %collective-permute-start.8) | collective-permute-done | bytes 81952 | tf_op jit(solution)/shard_map/ppermute | solution.py:661
  50.7 0.0 collective-permute-done.9.xhi
  50.8 1.2 %collective-permute-start.10 = (f32[35,8,128]{2,1,0:T(8,128)S(1)}, f32[35,8,128]{2,1,0:T(8,128)S(1)}, u32[]{:S(2)}, u32[]{:S(2)}) collective-permute-start(f32[35,8,128]{2,1,0:T(8,128)S(1)} %get-tuple-element.71), channel_id=1, source_target_pairs={{0,1},{1,2},{2,3},{3,4},{4,5},{5,6},{6,7},{7,0},{8,9},{9,10},{10,1... | collective-permute-start | bytes 430088 | tf_op jit(solution)/shard_map/ppermute | solution.py:661
  52.0 0.0 collective-permute-start.11
  52.0 2.1 %collective-permute-done.10.ylo = f32[35,8,128]{2,1,0:T(8,128)S(1)} collective-permute-done((f32[35,8,128]{2,1,0:T(8,128)S(1)}, f32[35,8,128]{2,1,0:T(8,128)S(1)}, u32[]{:S(2)}, u32[]{:S(2)}) %collective-permute-start.10) | collective-permute-done | bytes 143392 | tf_op jit(solution)/shard_map/ppermute | solution.py:661
  54.0 3.7 %collective-permute-done.11.yhi = f32[35,8,128]{2,1,0:T(8,128)S(1)} collective-permute-done((f32[35,8,128]{2,1,0:T(8,128)S(1)}, f32[35,8,128]{2,1,0:T(8,128)S(1)}, u32[]{:S(2)}, u32[]{:S(2)}) %collective-permute-start.11) | collective-permute-done | bytes 143392 | tf_op jit(solution)/shard_map/ppermute | solution.py:661
  57.7 7.8 %way_up.1 = (f32[32,32,256]{2,1,0:T(8,128)}, f32[32,32,256]{2,1,0:T(8,128)}) custom-call(f32[35,8,128]{2,1,0:T(8,128)S(1)} %get-tuple-element.70.ext, f32[35,8,128]{2,1,0:T(8,128)S(1)} %collective-permute-done.10.ylo, f32[35,8,128]{2,1,0:T(8,128)S(1)} %collective-permute-done.11.yhi, f32[28,32,128]{2,1,0:T(8,128)S(1)} %get-tuple-element.72.s1, ...), custom_call_target="tpu_custom_call" | custom-call | tf_op jit(solution)/shard_map/way_up/pallas_call | solution.py:230
  (3 shorter events, 0.1 us)
Async XLA Ops:
  1.9 5.6 %collective-permute-start = (f32[32,8,256]{2,1,0:T(8,128)S(1)}, f32[32,8,256]{2,1,0:T(8,128)S(1)}, u32[]{:S(2)}, u32[]{:S(2)}) collective-permute-start(f32[32,8,256]{2,1,0:T(8,128)S(1)} %get-tuple-element.46), channel_id=1, source_target_pairs={{0,1},{1,2},{2,3},{3,4},{4,5},{5,6},{6,7},{7,0},{8,9},{9,10},{10,1... | collective-permute-start | bytes 786440 | tf_op jit(solution)/shard_map/ppermute | solution.py:661
  4.2 7.0 %collective-permute-start.1 = (f32[32,8,256]{2,1,0:T(8,128)S(1)}, f32[32,8,256]{2,1,0:T(8,128)S(1)}, u32[]{:S(2)}, u32[]{:S(2)}) collective-permute-start(f32[32,8,256]{2,1,0:T(8,128)S(1)} %get-tuple-element.43.sent), channel_id=1, source_target_pairs={{0,7},{1,0},{2,1},{3,2},{4,3},{5,4},{6,5},{7,6},{8,15},{9,8},{10,9... | collective-permute-start | bytes 786440 | tf_op jit(solution)/shard_map/ppermute | solution.py:661
  11.2 12.4 %collective-permute-start.2 = (f32[7,40,256]{2,1,0:T(8,128)S(1)}, f32[7,40,256]{2,1,0:T(8,128)S(1)}, u32[]{:S(2)}, u32[]{:S(2)}) collective-permute-start(f32[7,40,256]{2,1,0:T(8,128)S(1)} %get-tuple-element.47), channel_id=1, source_target_pairs={{0,8},{8,16},{16,24},{24,32},{32,40},{40,48},{48,56},{56,64},{64,7... | collective-permute-start | bytes 860168 | tf_op jit(solution)/shard_map/ppermute | solution.py:661
  11.3 12.3 %collective-permute-start.3 = (f32[7,40,256]{2,1,0:T(8,128)S(1)}, f32[7,40,256]{2,1,0:T(8,128)S(1)}, u32[]{:S(2)}, u32[]{:S(2)}) collective-permute-start(f32[7,40,256]{2,1,0:T(8,128)S(1)} %get-tuple-element.48), channel_id=1, source_target_pairs={{0,248},{8,0},{16,8},{24,16},{32,24},{40,32},{48,40},{56,48},{64,5... | collective-permute-start | bytes 860168 | tf_op jit(solution)/shard_map/ppermute | solution.py:661
  25.1 8.8 %collective-permute-start.4 = (f32[15,16,128]{2,1,0:T(8,128)S(1)}, f32[15,16,128]{2,1,0:T(8,128)S(1)}, u32[]{:S(2)}, u32[]{:S(2)}) collective-permute-start(f32[15,16,128]{2,1,0:T(8,128)S(1)} %get-tuple-element.61), channel_id=1, source_target_pairs={{0,8},{8,16},{16,24},{24,32},{32,40},{40,48},{48,56},{56,64},{64,7... | collective-permute-start | bytes 368648 | tf_op jit(solution)/shard_map/ppermute | solution.py:661
  25.1 8.8 %collective-permute-start.5 = (f32[15,16,128]{2,1,0:T(8,128)S(1)}, f32[15,16,128]{2,1,0:T(8,128)S(1)}, u32[]{:S(2)}, u32[]{:S(2)}) collective-permute-start(f32[15,16,128]{2,1,0:T(8,128)S(1)} %get-tuple-element.62), channel_id=1, source_target_pairs={{0,248},{8,0},{16,8},{24,16},{32,24},{40,32},{48,40},{56,48},{64,5... | collective-permute-start | bytes 368648 | tf_op jit(solution)/shard_map/ppermute | solution.py:661
  33.9 4.5 %collective-permute-start.6 = (f32[32,16,128]{2,1,0:T(8,128)S(1)}, f32[32,16,128]{2,1,0:T(8,128)S(1)}, u32[]{:S(2)}, u32[]{:S(2)}) collective-permute-start(f32[32,16,128]{2,1,0:T(8,128)S(1)} %get-tuple-element.65), channel_id=1, source_target_pairs={{0,1},{1,2},{2,3},{3,4},{4,5},{5,6},{6,7},{7,0},{8,9},{9,10},{10,1... | collective-permute-start | bytes 786440 | tf_op jit(solution)/shard_map/ppermute | solution.py:661
  35.2 7.0 %collective-permute-start.7 = (f32[32,16,128]{2,1,0:T(8,128)S(1)}, f32[32,16,128]{2,1,0:T(8,128)S(1)}, u32[]{:S(2)}, u32[]{:S(2)}) collective-permute-start(f32[32,16,128]{2,1,0:T(8,128)S(1)} %get-tuple-element.66), channel_id=1, source_target_pairs={{0,7},{1,0},{2,1},{3,2},{4,3},{5,4},{6,5},{7,6},{8,15},{9,8},{10,9... | collective-permute-start | bytes 786440 | tf_op jit(solution)/shard_map/ppermute | solution.py:661
  44.0 6.7 %collective-permute-start.8 = (f32[10,16,128]{2,1,0:T(8,128)S(1)}, f32[10,16,128]{2,1,0:T(8,128)S(1)}, u32[]{:S(2)}, u32[]{:S(2)}) collective-permute-start(f32[10,16,128]{2,1,0:T(8,128)S(1)} %get-tuple-element.68), channel_id=1, source_target_pairs={{0,8},{8,16},{16,24},{24,32},{32,40},{40,48},{48,56},{56,64},{64,7... | collective-permute-start | bytes 245768 | tf_op jit(solution)/shard_map/ppermute | solution.py:661
  44.1 6.6 %collective-permute-start.9 = (f32[10,16,128]{2,1,0:T(8,128)S(1)}, f32[10,16,128]{2,1,0:T(8,128)S(1)}, u32[]{:S(2)}, u32[]{:S(2)}) collective-permute-start(f32[10,16,128]{2,1,0:T(8,128)S(1)} %get-tuple-element.69), channel_id=1, source_target_pairs={{0,248},{8,0},{16,8},{24,16},{32,24},{40,32},{48,40},{56,48},{64,5... | collective-permute-start | bytes 245768 | tf_op jit(solution)/shard_map/ppermute | solution.py:661
  50.8 3.2 %collective-permute-start.10 = (f32[35,8,128]{2,1,0:T(8,128)S(1)}, f32[35,8,128]{2,1,0:T(8,128)S(1)}, u32[]{:S(2)}, u32[]{:S(2)}) collective-permute-start(f32[35,8,128]{2,1,0:T(8,128)S(1)} %get-tuple-element.71), channel_id=1, source_target_pairs={{0,1},{1,2},{2,3},{3,4},{4,5},{5,6},{6,7},{7,0},{8,9},{9,10},{10,1... | collective-permute-start | bytes 430088 | tf_op jit(solution)/shard_map/ppermute | solution.py:661
  52.0 5.7 %collective-permute-start.11 = (f32[35,8,128]{2,1,0:T(8,128)S(1)}, f32[35,8,128]{2,1,0:T(8,128)S(1)}, u32[]{:S(2)}, u32[]{:S(2)}) collective-permute-start(f32[35,8,128]{2,1,0:T(8,128)S(1)} %get-tuple-element.70.ext), channel_id=1, source_target_pairs={{0,7},{1,0},{2,1},{3,2},{4,3},{5,4},{6,5},{7,6},{8,15},{9,8},{10,9... | collective-permute-start | bytes 430088 | tf_op jit(solution)/shard_map/ppermute | solution.py:661

commit v5 on v4

--- a/solution.py
+++ b/solution.py
@@ -149,7 +149,8 @@
 def sweep_plane(p_ref, s_ref, w):
     def plane(j):
         p = p_ref[j]
-        return (KEEP * p + w[3][j] * (s_ref[j] + flow(j, p, p_ref, w)),)
+        total = flow(j, p, p_ref, w)
+        return (KEEP * p + w[3][j] * (total if s_ref is None else s_ref[j] + total),)
 
     return plane
 
@@ -301,13 +302,17 @@
 
 
 def send_planes_kernel(s_in, f_in, ylo, yhi, dn_ref, upw_ref):
-    for first, out_ref, skip in ((0, dn_ref, 0), (28, upw_ref, 1)):
+    for first, out_ref, last, at in ((0, dn_ref, 2, (0, 1, 2)), (28, upw_ref, 1, (None, 0, 1, 2))):
         block = slice(first, first + 4)
-        source, code = halo_rows(ylo[block], yhi[block])
-        out_ref[:3, :32] = s_in[first + skip : first + skip + 3]
-        out_ref[:3, 32:] = source[skip : skip + 3]
-        out_ref[3:, :32] = f_in[block].astype(F32)
-        out_ref[3:, 32:] = code
+        halo_source, halo_code = halo_rows(ylo[block], yhi[block])
+        code = [jnp.concatenate([f_in[first + k].astype(F32), halo_code[k]], 0) for k in range(4)]
+        source = [jnp.concatenate([s_in[first + k], halo_source[k]], 0) for k in range(4)]
+        q = weights_at(code[last - 1], code[last], code[last + 1], face_code, OUT, True)[3]
+        source[last] = q * source[last]
+        for k, place in enumerate(at):
+            if place is not None:
+                out_ref[place] = source[k]
+                out_ref[place + 3] = code[k]
 
 
 def water_to_mobility(n):
@@ -378,14 +383,16 @@
     t_ref, u_ref,
 ):
     low_x, high_x = edge("gx")
-    s_ref[2:5] = blank(low_x, xlo[:3], 0.0)
-    c_ref[1:5] = blank(low_x, xlo[3:], OUT)
-    s_ref[37:40] = blank(high_x, xhi[:3], 0.0)
-    c_ref[37:41] = blank(high_x, xhi[3:], OUT)
+    p1[2] = blank(low_x, xlo[0], 0.0)
+    s_ref[3:5] = blank(low_x, xlo[1:3], 0.0)
+    c_ref[2:5] = blank(low_x, xlo[3:], OUT)
+    s_ref[37:39] = blank(high_x, xhi[:2], 0.0)
+    p1[39] = blank(high_x, xhi[2], 0.0)
+    c_ref[37:40] = blank(high_x, xhi[3:], OUT)
     w = (wx, wy, wz, q_ref)
-    wx[1] = face_code(c_ref[1], c_ref[2])
+    wx[2] = face_code(c_ref[2], c_ref[3])
     wx[35] = face_code(c_ref[35], c_ref[36])
-    planes_at((2, 3, 4, 5, 36, 37, 38, 39), weights_plane(c_ref, s_ref, face_code, OUT, True), (*w, p1))
+    planes_at((3, 4, 5, 36, 37, 38), weights_plane(c_ref, s_ref, face_code, OUT, True), (*w, p1))
     planes_at((3, 4, 5, 6, 35, 36, 37, 38), sweep_plane(p1, s_ref, w), (p2,))
     planes_at((4, 5, 6, 7, 34, 35, 36, 37), remainder_plane(p2, s_ref, w), (r_ref,))
     halve0((0, 1, 14, 15), r_ref, src1, t_ref, u_ref)
@@ -455,13 +462,19 @@
     for k, packed in enumerate(halve(12, r_ref, m_ref, t_ref, u_ref, 64, full_dot)):
         pk_ref[k] = packed
     own2[...] = pk_ref[2:10]
-    dn2[...] = pk_ref[2:12]
-    upw2[...] = pk_ref[0:10]
+    row = iota((8, 128), 0)
+    for out, first in ((dn2, 2), (upw2, 0)):
+        for k in range(10):
+            out[k] = pk_ref[first + k, :8]
+        for k in range(5):
+            a, b = pk_ref[first + 2 * k, 8:], pk_ref[first + 2 * k + 1, 8:]
+            b = jnp.where(row < 4, pltpu.roll(b, 2, 0), pltpu.roll(b, 6, 0))
+            out[10 + k] = jnp.where((row < 2) | (row >= 6), a, b)
 
 
 def down1(*operands):
     return call(
-        down1_kernel, "down1", [kept(k, 16, 128) for k in (8, 10, 10)] + [kept(N1, 32, 128)] * 6,
+        down1_kernel, "down1", [kept(8, 16, 128)] + [kept(15, 8, 128)] * 2 + [kept(N1, 32, 128)] * 6,
         [kept(N1, 32, 128)] * 3 + [kept(384, 256), kept(384, 128), kept(12, 16, 128)], 6, *operands,
     )
 
@@ -473,17 +486,18 @@
         two_dn = two_up = jnp.zeros((8, 128), F32)
         for b in range(4):
             j = 4 * a + b
-            if j < 10:
-                plane = blank(low_x, xlo[j], 0.0)
-            elif j < 18:
-                plane = own[j - 10]
+            if 10 <= j < 18:
+                tile, more = own[j - 10, :8], own[j - 10, 8:]
             else:
-                plane = blank(high_x, xhi[j - 18], 0.0)
-            dn_ref[j] = plane[:8]
-            upw_ref[j] = plane[:8]
+                flag, halo, k = (low_x, xlo, j) if j < 10 else (high_x, xhi, j - 18)
+                tile, more = blank(flag, halo[k], 0.0), blank(flag, halo[10 + k // 2], 0.0)
+                if k % 2:
+                    more = jnp.where(row < 4, pltpu.roll(more, 6, 0), pltpu.roll(more, 2, 0))
+            dn_ref[j] = tile
+            upw_ref[j] = tile
             here = (row == 2 * b) | (row == 2 * b + 1)
-            two_dn = jnp.where(here, pltpu.roll(plane[8:], 2 * b, 0) if b else plane[8:], two_dn)
-            two_up = jnp.where(here, pltpu.roll(plane[8:], 2 * b + 2, 0) if b < 3 else plane[8:], two_up)
+            two_dn = jnp.where(here, pltpu.roll(more, 2 * b, 0) if b else more, two_dn)
+            two_up = jnp.where(here, pltpu.roll(more, 2 * b + 2, 0) if b < 3 else more, two_up)
         dn_ref[N2 + a] = two_dn
         upw_ref[N2 + a] = two_up
 
@@ -492,15 +506,71 @@
     return call(pack2_kernel, "pack2", [kept(N2 + N2 // 4, 8, 128)] * 2, [], 4, *operands)
 
 
+def before_kernel(wx0, wy0, wz0, q0, s0, down0_ref, plane_lo, plane_hi, rows_lo, rows_hi, out_ref, pa0, pb0, row_ref):
+    low_x, high_x = edge("gx")
+    low_y, high_y = edge("gy")
+    row8 = iota((8, 256), 0)
+
+    def plane_of(message, first):
+        tiles = [message[first + k] for k in range(4)]
+        return jnp.concatenate(
+            [jnp.concatenate(tiles[:2], 1), jnp.concatenate(tiles[2:], 1), jnp.zeros((8, 256), F32)], 0
+        )
+
+    pa0[2] = blank(low_x, plane_of(plane_lo, 11), 0.0)
+    pa0[N0 - 3] = blank(high_x, plane_of(plane_hi, 11), 0.0)
+    for k in range(4):
+        h, z = k // 2 * 16, k % 2 * 128
+        row_ref[0, h : h + 16, z : z + 128] = blank(high_y, rows_hi[N1 + k], 0.0)
+        row_ref[1, h : h + 16, z : z + 128] = blank(low_y, rows_lo[N1 + k], 0.0)
+    for j in (3, 4, 37, 38):
+        pa0[j] = down0_ref[j]
+
+    def own_planes(j, n):
+        for i in range(n):
+            above = row_ref[0, pl.ds(j + i, 1)]
+            below = row_ref[1, pl.ds(j + i, 1)]
+            p = down0_ref[j + i + X0]
+            halo = jnp.where(row8 == 2, above, jnp.where(row8 == 5, below, p[32:]))
+            pa0[j + i + X0, :32] = p[:32]
+            pa0[j + i + X0, 32:] = halo
+
+    blocks(0, 32, 8, own_planes)
+    w0 = (wx0, wy0, wz0, q0)
+    sweep(3, N0 - 3, 12, pa0, pb0, s0, w0)
+    sweep(4, N0 - 4, 17, pb0, out_ref, s0, w0)
+
+
+def before(*operands):
+    scratch = [kept(*BIG)] * 2 + [kept(2, 32, 256)]
+    return call(before_kernel, "before", [kept(*BIG)], scratch, 5, *operands)[0]
+
+
+def base_kernel(wx0, wy0, wz0, q0, s0, p_ref, sent, base_s, base_r):
+    del sent
+    w0 = (wx0, wy0, wz0, q0)
+
+    def plane(j):
+        p = p_ref[j + X0]
+        dp = (OMEGA / q0[j + X0]) * p
+        return dp[:32], (s0[j + X0] + flow(j + X0, p, p_ref, w0) - dp)[:32]
+
+    planes(0, 32, 8, plane, (base_s, base_r))
+
+
+def base(*operands):
+    return call(base_kernel, "base", [kept(32, 32, 256)] * 2, [], 4, *operands)
+
+
 def up_kernel(
     ext, ylo, yhi, s1, wx1, wy1, wz1, q1, down1_ref,
-    wx0, wy0, wz0, q0, s0, down0_ref, plane_lo, plane_hi, rows_lo, rows_hi,
+    wx0, wy0, wz0, q0, base_s, base_r,
     scaled, residual,
     pa0, pb0,
     pa1, pb1,
     s2, m2, wx2, wy2, wz2, q2, pa2, pb2, r2,
     s3, m3, wx3, wy3, wz3, q3, pa3, pb3,
-    t_ref, u_ref, v_ref, rise_lo, rise_hi, out_a, out_b, row_ref, sems,
+    t_ref, u_ref, v_ref, rise_lo, rise_hi, out_a, out_b, sems,
 ):
     low_y, high_y = edge("gy")
 
@@ -576,38 +646,25 @@
         here = pl.ds(k * 48 if isinstance(k, int) else pl.multiple_of(k * 48, 8), 40)
         return jnp.concatenate([rise_lo[here], rise_hi[here]], 1)
 
-    low_x, high_x = edge("gx")
-    row8 = iota((8, 256), 0)
-
-    def plane_of(message, first):
-        tiles = [message[first + k] for k in range(4)]
-        return jnp.concatenate(
-            [jnp.concatenate(tiles[:2], 1), jnp.concatenate(tiles[2:], 1), jnp.zeros((8, 256), F32)], 0
-        )
-
-    pa0[2] = rise_at(0) + blank(low_x, plane_of(plane_lo, 11), 0.0)
-    pa0[N0 - 3] = rise_at(19) + blank(high_x, plane_of(plane_hi, 11), 0.0)
-    for k in range(4):
-        h, z = k // 2 * 16, k % 2 * 128
-        row_ref[0, h : h + 16, z : z + 128] = blank(high_y, rows_hi[N1 + k], 0.0)
-        row_ref[1, h : h + 16, z : z + 128] = blank(low_y, rows_lo[N1 + k], 0.0)
-    for j in (3, 4, 37, 38):
-        pa0[j] = down0_ref[j] + rise_at((j - 1) // 2)
-
-    def rise0(k, n):
+    w0 = (wx0, wy0, wz0, q0)
+
+    def first_pairs(k0, n):
+        results = []
         for i in range(n):
-            rise = rise_at(k + i)
-            for j in (2 * (k + i) + 1, 2 * (k + i) + 2):
-                pa0[j, :32] = down0_ref[j, :32] + rise[:32]
-                above = row_ref[0, pl.ds(j - X0, 1)]
-                below = row_ref[1, pl.ds(j - X0, 1)]
-                halo = jnp.where(row8 == 2, above, jnp.where(row8 == 5, below, down0_ref[j, 32:]))
-                pa0[j, 32:] = halo + rise[32:]
-
-    blocks(2, 18, 2, rise0)
-    w0 = (wx0, wy0, wz0, q0)
-    sweep(3, N0 - 3, 12, pa0, pb0, s0, w0)
-    sweep(4, N0 - 4, 17, pb0, pa0, s0, w0)
+            k = k0 + i
+            low, e, high = rise_at(k - 1), rise_at(k), rise_at(k + 1)
+            e_up_y, e_up_z = up_y(e), up_z(e)
+            for j, x_low, x_high in ((2 * k + 1, low, e), (2 * k + 2, e, high)):
+                wy, wz = wy0[j], wz0[j]
+                along_x = wx0[j] * x_high + wx0[j - 1] * x_low
+                along_y = wy * e_up_y + dn_y(wy * e)
+                along_z = wz * e_up_z + dn_z(wz * e)
+                results.append((j, KEEP * e + q0[j] * (along_x + along_y + along_z)))
+        for j, value in results:
+            pb0[j] = value
+
+    blocks(1, 19, 6, first_pairs)
+    sweep(4, N0 - 4, 17, pb0, pa0, None, w0)
 
     def out_copies(k, j):
         here = pl.ds(j, 8)
@@ -622,7 +679,8 @@
         for i in range(8):
             p = pa0[j + i + X0]
             dp = (OMEGA / q0[j + i + X0]) * p
-            results.append((dp[:32], (s0[j + i + X0] + flow(j + i + X0, p, pa0, w0) - dp)[:32]))
+            a = base_s[j + i] + dp[:32]
+            results.append((a, base_r[j + i] + (flow(j + i + X0, p, pa0, w0) - dp)[:32]))
         for i, (a, b) in enumerate(results):
             out_a[j + i] = a
             out_b[j + i] = b
@@ -649,7 +707,6 @@
         + buf(1, 480, 128)
         + buf(2, 960, 128)
         + buf(2, 32, 32, 256)
-        + buf(1, 2, 32, 256)
         + [pltpu.SemaphoreType.DMA((2, 4))]
     )
     hbm = pl.BlockSpec(memory_space=pl.ANY)
@@ -669,7 +726,7 @@
     dn0, up0 = send_rows(source, phase)
     ylo, yhi = both(dn0, up0, "gy")
     source, phase = load(source, phase, dn0)
-    msg = [kept(7, 40, 256)] * 2
+    msg = [kept(6, 40, 256)] * 2
     dn0, up0 = call(send_planes_kernel, "send_planes", msg, [], 4, source, phase, ylo, yhi)
     xlo, xhi = both(dn0, up0, "gx")
     *state, mob1 = inner0(source, phase, ylo, yhi)
@@ -680,8 +737,9 @@
     xlo, xhi = both(dn2, up2, "gx")
     ext, ext_up = pack2(own2, xlo, xhi)
     ylo, yhi = both(ext, ext_up, "gy")
-    level0 = (wx0, wy0, wz0, q0, s0, p0, xlo1, xhi1, ylo1, yhi1)
-    return tuple(way_up(ext, ylo, yhi, *level1, *level0))
+    weights = (wx0, wy0, wz0, q0)
+    p0 = before(*weights, s0, p0, xlo1, xhi1, ylo1, yhi1)
+    return tuple(way_up(ext, ylo, yhi, *level1, *weights, *base(*weights, s0, p0, ext)))
 
 
 def solution(mesh):

time: 65.8 us -> 64.5 us (0.980)
  waiting for transfers between devices: 24.6 us -> 19.5 us
  Pallas kernels: 18.9 us -> 22.7 us
    ppermute x12, waiting for transfers between devices: 24.6 us -> 19.5 us  [shift(): lax.ppermute(a, axis, [(i, (i + step) % count) for i in range(count)])]
    pallas_call x9 -> x11, Pallas kernels: 18.9 us -> 22.7 us  [call(): pl.pallas_call(kernel, in_specs=[VM] * len(operands) if in_specs is None...]
  transfers between devices with their start and end apart: 12 -> 12, of which waited for: 9 -> 8; matrix products, arithmetic and copies ran while one was open for 0% -> 0% of each run, Pallas kernels for 10% -> 16%
where the time goes in v5:
time: 64.5 us; the launch traced here: 64.4 us
  Pallas kernels  22.7 us (35%)
  starting transfers between devices  21.3 us (33%)
  waiting for transfers between devices  19.5 us (30%)
  between operations  0.89 us (1%)
    pallas_call x11, Pallas kernels, call(): pl.pallas_call(kernel, in_specs=[VM] * len(operands) if in_specs is None...  22.7 us
    ppermute x12, starting transfers between devices, shift(): lax.ppermute(a, axis, [(i, (i + step) % count) for i in range(count)])  21.3 us
    ppermute x12, waiting for transfers between devices, shift(): lax.ppermute(a, axis, [(i, (i + step) % count) for i in range(count)])  19.5 us
  transfers between devices with their start and end apart: 12, of which 8 were waited for; matrix products, arithmetic and copies ran while one was open for 0% of the time, Pallas kernels for 16%

profile of v5, /device:TPU:25, one launch (start us, length us, event | category | flops | bytes accessed | tf_op | source)
XLA Modules:
  0.0 64.4 jit_solution(649974398167534121)
XLA Ops:
  0.6 1.3 %send_rows.1 = (f32[32,8,256]{2,1,0:T(8,128)S(1)}, f32[32,8,256]{2,1,0:T(8,128)S(1)}) custom-call(f32[32,32,256]{2,1,0:T(8,128)} %s_hbm.3, s32[32,32,256]{2,1,0:T(8,128)} %f_hbm.3), custom_call_target="tpu_custom_call" | custom-call | tf_op jit(solution)/shard_map/send_rows/pallas_call | solution.py:231
  1.9 2.3 %collective-permute-start = (f32[32,8,256]{2,1,0:T(8,128)S(1)}, f32[32,8,256]{2,1,0:T(8,128)S(1)}, u32[]{:S(2)}, u32[]{:S(2)}) collective-permute-start(f32[32,8,256]{2,1,0:T(8,128)S(1)} %get-tuple-element.48), channel_id=1, source_target_pairs={{0,1},{1,2},{2,3},{3,4},{4,5},{5,6},{6,7},{7,0},{8,9},{9,10},{10,1... | collective-permute-start | bytes 786440 | tf_op jit(solution)/shard_map/ppermute | solution.py:718
  4.2 0.0 collective-permute-start.1
  4.2 1.6 %load.1 = (f32[32,32,256]{2,1,0:T(8,128)S(1)}, s32[32,32,256]{2,1,0:T(8,128)S(1)}) custom-call(f32[32,32,256]{2,1,0:T(8,128)} %s_hbm.3, s32[32,32,256]{2,1,0:T(8,128)} %f_hbm.3, f32[32,8,256]{2,1,0:T(8,128)S(1)} %get-tuple-element.45.sent), custom_call_target="tpu_custom_call" | custom-call | tf_op jit(solution)/shard_map/load/pallas_call | solution.py:231
  5.8 1.7 %collective-permute-done.ylo = f32[32,8,256]{2,1,0:T(8,128)S(1)} collective-permute-done((f32[32,8,256]{2,1,0:T(8,128)S(1)}, f32[32,8,256]{2,1,0:T(8,128)S(1)}, u32[]{:S(2)}, u32[]{:S(2)}) %collective-permute-start) | collective-permute-done | bytes 262176 | tf_op jit(solution)/shard_map/ppermute | solution.py:718
  7.5 3.7 %collective-permute-done.1.yhi = f32[32,8,256]{2,1,0:T(8,128)S(1)} collective-permute-done((f32[32,8,256]{2,1,0:T(8,128)S(1)}, f32[32,8,256]{2,1,0:T(8,128)S(1)}, u32[]{:S(2)}, u32[]{:S(2)}) %collective-permute-start.1) | collective-permute-done | bytes 262176 | tf_op jit(solution)/shard_map/ppermute | solution.py:718
  11.2 0.2 send_planes.1
  11.4 0.1 collective-permute-start.2
  11.5 6.1 %collective-permute-start.3 = (f32[6,40,256]{2,1,0:T(8,128)S(1)}, f32[6,40,256]{2,1,0:T(8,128)S(1)}, u32[]{:S(2)}, u32[]{:S(2)}) collective-permute-start(f32[6,40,256]{2,1,0:T(8,128)S(1)} %get-tuple-element.50), channel_id=1, source_target_pairs={{0,248},{8,0},{16,8},{24,16},{32,24},{40,32},{48,40},{56,48},{64,5... | collective-permute-start | bytes 737288 | tf_op jit(solution)/shard_map/ppermute | solution.py:718
  17.6 4.9 %inner0.1 = (f32[42,40,256]{2,1,0:T(8,128)S(1)}, f32[42,40,256]{2,1,0:T(8,128)S(1)}, f32[42,40,256]{2,1,0:T(8,128)S(1)}, f32[42,40,256]{2,1,0:T(8,128)S(1)}, f32...) custom-call(f32[32,32,256]{2,1,0:T(8,128)S(1)} %get-tuple-element.46, ...), custom_call_target="tpu_custom_call" | custom-call | tf_op jit(solution)/shard_map/inner0/pallas_call | solution.py:231
  22.5 0.3 collective-permute-done.2.xlo
  22.9 0.0 collective-permute-done.3.xhi
  22.9 1.4 %outer0.1 = (f32[42,40,256]{2,1,0:T(8,128)S(1)}, f32[42,40,256]{2,1,0:T(8,128)S(1)}, f32[42,40,256]{2,1,0:T(8,128)S(1)}, f32[42,40,256]{2,1,0:T(8,128)S(1)}, f32...) custom-call(f32[6,40,256]{2,1,0:T(8,128)S(1)} %collective-permute-do, ...), custom_call_target="tpu_custom_call", output_to_operand_aliasing={{0}: (3, {}), {1}: (4, {}), {2}: (5, {}), {3}: (6, {}), {4}... | custom-call | tf_op jit(solution)/shard_map/outer0/pallas_call | solution.py:231
  24.2 0.1 collective-permute-start.4
  24.3 5.2 %collective-permute-start.5 = (f32[15,16,128]{2,1,0:T(8,128)S(1)}, f32[15,16,128]{2,1,0:T(8,128)S(1)}, u32[]{:S(2)}, u32[]{:S(2)}) collective-permute-start(f32[15,16,128]{2,1,0:T(8,128)S(1)} %get-tuple-element.64), channel_id=1, source_target_pairs={{0,248},{8,0},{16,8},{24,16},{32,24},{40,32},{48,40},{56,48},{64,5... | collective-permute-start | bytes 368648 | tf_op jit(solution)/shard_map/ppermute | solution.py:718
  29.6 3.5 %collective-permute-done.4.xlo.plane_lo = f32[15,16,128]{2,1,0:T(8,128)S(1)} collective-permute-done((f32[15,16,128]{2,1,0:T(8,128)S(1)}, f32[15,16,128]{2,1,0:T(8,128)S(1)}, u32[]{:S(2)}, u32[]{:S(2)}) %collective-permute-start.4) | collective-permute-done | bytes 122912 | tf_op jit(solution)/shard_map/ppermute | solution.py:718
  33.1 0.0 collective-permute-done.5.xhi.plane_hi
  33.1 1.2 %collective-permute-start.6 = (f32[32,16,128]{2,1,0:T(8,128)S(1)}, f32[32,16,128]{2,1,0:T(8,128)S(1)}, u32[]{:S(2)}, u32[]{:S(2)}) collective-permute-start(f32[32,16,128]{2,1,0:T(8,128)S(1)} %get-tuple-element.67), channel_id=1, source_target_pairs={{0,1},{1,2},{2,3},{3,4},{4,5},{5,6},{6,7},{7,0},{8,9},{9,10},{10,1... | collective-permute-start | bytes 786440 | tf_op jit(solution)/shard_map/ppermute | solution.py:718
  34.4 0.0 collective-permute-start.7
  34.4 3.3 %collective-permute-done.6.ylo.rows_lo = f32[32,16,128]{2,1,0:T(8,128)S(1)} collective-permute-done((f32[32,16,128]{2,1,0:T(8,128)S(1)}, f32[32,16,128]{2,1,0:T(8,128)S(1)}, u32[]{:S(2)}, u32[]{:S(2)}) %collective-permute-start.6) | collective-permute-done | bytes 262176 | tf_op jit(solution)/shard_map/ppermute | solution.py:718
  37.7 3.7 %collective-permute-done.7.yhi.rows_hi = f32[32,16,128]{2,1,0:T(8,128)S(1)} collective-permute-done((f32[32,16,128]{2,1,0:T(8,128)S(1)}, f32[32,16,128]{2,1,0:T(8,128)S(1)}, u32[]{:S(2)}, u32[]{:S(2)}) %collective-permute-start.7) | collective-permute-done | bytes 262176 | tf_op jit(solution)/shard_map/ppermute | solution.py:718
  41.4 1.9 %down1.1 = (f32[8,16,128]{2,1,0:T(8,128)S(1)}, f32[15,8,128]{2,1,0:T(8,128)S(1)}, f32[15,8,128]{2,1,0:T(8,128)S(1)}, f32[28,32,128]{2,1,0:T(8,128)S(1)}, f32[28,...) custom-call(f32[16,16,128]{2,1,0:T(8,128)S(1)} %get-tuple-element.62, ...), custom_call_target="tpu_custom_call" | custom-call | tf_op jit(solution)/shard_map/down1/pallas_call | solution.py:231
  43.3 0.1 collective-permute-start.8
  43.4 5.1 %collective-permute-start.9 = (f32[15,8,128]{2,1,0:T(8,128)S(1)}, f32[15,8,128]{2,1,0:T(8,128)S(1)}, u32[]{:S(2)}, u32[]{:S(2)}) collective-permute-start(f32[15,8,128]{2,1,0:T(8,128)S(1)} %get-tuple-element.71), channel_id=1, source_target_pairs={{0,248},{8,0},{16,8},{24,16},{32,24},{40,32},{48,40},{56,48},{64,5... | collective-permute-start | bytes 184328 | tf_op jit(solution)/shard_map/ppermute | solution.py:718
  48.4 1.3 %collective-permute-done.8.xlo = f32[15,8,128]{2,1,0:T(8,128)S(1)} collective-permute-done((f32[15,8,128]{2,1,0:T(8,128)S(1)}, f32[15,8,128]{2,1,0:T(8,128)S(1)}, u32[]{:S(2)}, u32[]{:S(2)}) %collective-permute-start.8) | collective-permute-done | bytes 61472 | tf_op jit(solution)/shard_map/ppermute | solution.py:718
  49.8 0.0 collective-permute-done.9.xhi
  49.8 1.1 %collective-permute-start.10 = (f32[35,8,128]{2,1,0:T(8,128)S(1)}, f32[35,8,128]{2,1,0:T(8,128)S(1)}, u32[]{:S(2)}, u32[]{:S(2)}) collective-permute-start(f32[35,8,128]{2,1,0:T(8,128)S(1)} %get-tuple-element.73), channel_id=1, source_target_pairs={{0,1},{1,2},{2,3},{3,4},{4,5},{5,6},{6,7},{7,0},{8,9},{9,10},{10,1... | collective-permute-start | bytes 430088 | tf_op jit(solution)/shard_map/ppermute | solution.py:718
  50.9 0.0 collective-permute-start.11
  50.9 2.9 %before.1.p_ref = f32[42,40,256]{2,1,0:T(8,128)S(1)} custom-call(f32[42,40,256]{2,1,0:T(8,128)S(1)} %get-tuple-element.80.wx0, f32[42,40,256]{2,1,0:T(8,128)S(1)} %get-tuple-element.81.wy0, f32[42,40,256]{2,1,0:T(8,128)S(1)} %get-tuple-element.82.wz0, f32[42,40,256]{2,1,0:T(8,128)S(1)} %get-tuple-element.83.q0, f32[42,40,256]{2,1,0:T(8,128)S(1)} %get-tuple-element.84.s0, ...), custom_call_target="tpu_custom_call" | custom-call | tf_op jit(solution)/shard_map/before/pallas_call | solution.py:231
  53.8 1.0 %base.1 = (f32[32,32,256]{2,1,0:T(8,128)S(1)}, f32[32,32,256]{2,1,0:T(8,128)S(1)}) custom-call(f32[42,40,256]{2,1,0:T(8,128)S(1)} %get-tuple-element.80.wx0, f32[42,40,256]{2,1,0:T(8,128)S(1)} %get-tuple-element.81.wy0, f32[42,40,256]{2,1,0:T(8,128)S(1)} %get-tuple-element.82.wz0, f32[42,40,256]{2,1,0:T(8,128)S(1)} %get-tuple-element.83.q0, ...), custom_call_target="tpu_custom_call" | custom-call | tf_op jit(solution)/shard_map/base/pallas_call | solution.py:231
  54.8 0.0 collective-permute-done.10.ylo
  54.9 1.8 %collective-permute-done.11.yhi = f32[35,8,128]{2,1,0:T(8,128)S(1)} collective-permute-done((f32[35,8,128]{2,1,0:T(8,128)S(1)}, f32[35,8,128]{2,1,0:T(8,128)S(1)}, u32[]{:S(2)}, u32[]{:S(2)}) %collective-permute-start.11) | collective-permute-done | bytes 143392 | tf_op jit(solution)/shard_map/ppermute | solution.py:718
  56.7 7.5 %way_up.1 = (f32[32,32,256]{2,1,0:T(8,128)}, f32[32,32,256]{2,1,0:T(8,128)}) custom-call(f32[35,8,128]{2,1,0:T(8,128)S(1)} %get-tuple-element.72.sent.ext, f32[35,8,128]{2,1,0:T(8,128)S(1)} %collective-permute-done.10.ylo, f32[35,8,128]{2,1,0:T(8,128)S(1)} %collective-permute-done.11.yhi, f32[28,32,128]{2,1,0:T(8,128)S(1)} %get-tuple-element.74.s1, ...), custom_call_target="tpu_custom_call" | custom-call | tf_op jit(solution)/shard_map/way_up/pallas_call | solution.py:231
  (2 shorter events, 0.1 us)
Async XLA Ops:
  1.9 5.6 %collective-permute-start = (f32[32,8,256]{2,1,0:T(8,128)S(1)}, f32[32,8,256]{2,1,0:T(8,128)S(1)}, u32[]{:S(2)}, u32[]{:S(2)}) collective-permute-start(f32[32,8,256]{2,1,0:T(8,128)S(1)} %get-tuple-element.48), channel_id=1, source_target_pairs={{0,1},{1,2},{2,3},{3,4},{4,5},{5,6},{6,7},{7,0},{8,9},{9,10},{10,1... | collective-permute-start | bytes 786440 | tf_op jit(solution)/shard_map/ppermute | solution.py:718
  4.2 7.0 %collective-permute-start.1 = (f32[32,8,256]{2,1,0:T(8,128)S(1)}, f32[32,8,256]{2,1,0:T(8,128)S(1)}, u32[]{:S(2)}, u32[]{:S(2)}) collective-permute-start(f32[32,8,256]{2,1,0:T(8,128)S(1)} %get-tuple-element.45.sent), channel_id=1, source_target_pairs={{0,7},{1,0},{2,1},{3,2},{4,3},{5,4},{6,5},{7,6},{8,15},{9,8},{10,9... | collective-permute-start | bytes 786440 | tf_op jit(solution)/shard_map/ppermute | solution.py:718
  11.4 11.5 %collective-permute-start.2 = (f32[6,40,256]{2,1,0:T(8,128)S(1)}, f32[6,40,256]{2,1,0:T(8,128)S(1)}, u32[]{:S(2)}, u32[]{:S(2)}) collective-permute-start(f32[6,40,256]{2,1,0:T(8,128)S(1)} %get-tuple-element.49), channel_id=1, source_target_pairs={{0,8},{8,16},{16,24},{24,32},{32,40},{40,48},{48,56},{56,64},{64,7... | collective-permute-start | bytes 737288 | tf_op jit(solution)/shard_map/ppermute | solution.py:718
  11.5 11.4 %collective-permute-start.3 = (f32[6,40,256]{2,1,0:T(8,128)S(1)}, f32[6,40,256]{2,1,0:T(8,128)S(1)}, u32[]{:S(2)}, u32[]{:S(2)}) collective-permute-start(f32[6,40,256]{2,1,0:T(8,128)S(1)} %get-tuple-element.50), channel_id=1, source_target_pairs={{0,248},{8,0},{16,8},{24,16},{32,24},{40,32},{48,40},{56,48},{64,5... | collective-permute-start | bytes 737288 | tf_op jit(solution)/shard_map/ppermute | solution.py:718
  24.2 8.8 %collective-permute-start.4 = (f32[15,16,128]{2,1,0:T(8,128)S(1)}, f32[15,16,128]{2,1,0:T(8,128)S(1)}, u32[]{:S(2)}, u32[]{:S(2)}) collective-permute-start(f32[15,16,128]{2,1,0:T(8,128)S(1)} %get-tuple-element.63), channel_id=1, source_target_pairs={{0,8},{8,16},{16,24},{24,32},{32,40},{40,48},{48,56},{56,64},{64,7... | collective-permute-start | bytes 368648 | tf_op jit(solution)/shard_map/ppermute | solution.py:718
  24.3 8.8 %collective-permute-start.5 = (f32[15,16,128]{2,1,0:T(8,128)S(1)}, f32[15,16,128]{2,1,0:T(8,128)S(1)}, u32[]{:S(2)}, u32[]{:S(2)}) collective-permute-start(f32[15,16,128]{2,1,0:T(8,128)S(1)} %get-tuple-element.64), channel_id=1, source_target_pairs={{0,248},{8,0},{16,8},{24,16},{32,24},{40,32},{48,40},{56,48},{64,5... | collective-permute-start | bytes 368648 | tf_op jit(solution)/shard_map/ppermute | solution.py:718
  33.1 4.5 %collective-permute-start.6 = (f32[32,16,128]{2,1,0:T(8,128)S(1)}, f32[32,16,128]{2,1,0:T(8,128)S(1)}, u32[]{:S(2)}, u32[]{:S(2)}) collective-permute-start(f32[32,16,128]{2,1,0:T(8,128)S(1)} %get-tuple-element.67), channel_id=1, source_target_pairs={{0,1},{1,2},{2,3},{3,4},{4,5},{5,6},{6,7},{7,0},{8,9},{9,10},{10,1... | collective-permute-start | bytes 786440 | tf_op jit(solution)/shard_map/ppermute | solution.py:718
  34.4 7.0 %collective-permute-start.7 = (f32[32,16,128]{2,1,0:T(8,128)S(1)}, f32[32,16,128]{2,1,0:T(8,128)S(1)}, u32[]{:S(2)}, u32[]{:S(2)}) collective-permute-start(f32[32,16,128]{2,1,0:T(8,128)S(1)} %get-tuple-element.68), channel_id=1, source_target_pairs={{0,7},{1,0},{2,1},{3,2},{4,3},{5,4},{6,5},{7,6},{8,15},{9,8},{10,9... | collective-permute-start | bytes 786440 | tf_op jit(solution)/shard_map/ppermute | solution.py:718
  43.3 6.5 %collective-permute-start.8 = (f32[15,8,128]{2,1,0:T(8,128)S(1)}, f32[15,8,128]{2,1,0:T(8,128)S(1)}, u32[]{:S(2)}, u32[]{:S(2)}) collective-permute-start(f32[15,8,128]{2,1,0:T(8,128)S(1)} %get-tuple-element.70), channel_id=1, source_target_pairs={{0,8},{8,16},{16,24},{24,32},{32,40},{40,48},{48,56},{56,64},{64,7... | collective-permute-start | bytes 184328 | tf_op jit(solution)/shard_map/ppermute | solution.py:718
  43.4 6.4 %collective-permute-start.9 = (f32[15,8,128]{2,1,0:T(8,128)S(1)}, f32[15,8,128]{2,1,0:T(8,128)S(1)}, u32[]{:S(2)}, u32[]{:S(2)}) collective-permute-start(f32[15,8,128]{2,1,0:T(8,128)S(1)} %get-tuple-element.71), channel_id=1, source_target_pairs={{0,248},{8,0},{16,8},{24,16},{32,24},{40,32},{48,40},{56,48},{64,5... | collective-permute-start | bytes 184328 | tf_op jit(solution)/shard_map/ppermute | solution.py:718
  49.8 5.0 %collective-permute-start.10 = (f32[35,8,128]{2,1,0:T(8,128)S(1)}, f32[35,8,128]{2,1,0:T(8,128)S(1)}, u32[]{:S(2)}, u32[]{:S(2)}) collective-permute-start(f32[35,8,128]{2,1,0:T(8,128)S(1)} %get-tuple-element.73), channel_id=1, source_target_pairs={{0,1},{1,2},{2,3},{3,4},{4,5},{5,6},{6,7},{7,0},{8,9},{9,10},{10,1... | collective-permute-start | bytes 430088 | tf_op jit(solution)/shard_map/ppermute | solution.py:718
  50.9 5.7 %collective-permute-start.11 = (f32[35,8,128]{2,1,0:T(8,128)S(1)}, f32[35,8,128]{2,1,0:T(8,128)S(1)}, u32[]{:S(2)}, u32[]{:S(2)}) collective-permute-start(f32[35,8,128]{2,1,0:T(8,128)S(1)} %get-tuple-element.72.sent.ext), channel_id=1, source_target_pairs={{0,7},{1,0},{2,1},{3,2},{4,3},{5,4},{6,5},{7,6},{8,15},{9,8},{10,9... | collective-permute-start | bytes 430088 | tf_op jit(solution)/shard_map/ppermute | solution.py:718

commit v6 on v5

--- a/solution.py
+++ b/solution.py
@@ -379,7 +379,7 @@
 
 def outer0_kernel(
     xlo, xhi, mob1, s_0, c_0, wx_0, wy_0, wz_0, q_0, p1_0, p2_0, r_0, src1_0,
-    s_ref, c_ref, wx, wy, wz, q_ref, p1, p2, r_ref, src1, dn1, upw1, rows_dn, rows_up,
+    s_ref, c_ref, wx, wy, wz, q_ref, p1, p2, r_ref, src1, dn1, upw1,
     t_ref, u_ref,
 ):
     low_x, high_x = edge("gx")
@@ -398,21 +398,26 @@
     halve0((0, 1, 14, 15), r_ref, src1, t_ref, u_ref)
     dn1[:5] = src1[:5]
     dn1[5:11] = mob1[:6]
-    lay_rows(dn1, 11, p2[X0 + 2, :32])
     upw1[:5] = src1[11:]
     upw1[5:11] = mob1[10:]
-    lay_rows(upw1, 11, p2[X0 + 29, :32])
-    for k in range(32):
-        rows_dn[k : k + 1] = p2[X0 + k, 2:3]
-        rows_up[k : k + 1] = p2[X0 + k, 29:30]
 
 
 def outer0(xlo, xhi, mob1, state):
     return call(
         outer0_kernel, "outer0",
-        [kept(*BIG)] * 9 + [kept(16, 16, 128)] + [kept(15, 16, 128)] * 2 + [kept(32, 256)] * 2,
+        [kept(*BIG)] * 9 + [kept(16, 16, 128)] + [kept(11, 16, 128)] * 2,
         [kept(160, 256), kept(160, 128)], 4, xlo, xhi, mob1, *state, aliases={3 + k: k for k in range(10)},
     )
+
+
+def edge_rows_kernel(p, rows_dn, rows_up):
+    for k in range(32):
+        rows_dn[k : k + 1] = p[X0 + k, 0:1]
+        rows_up[k : k + 1] = p[X0 + k, 31:32]
+
+
+def edge_rows(p2):
+    return call(edge_rows_kernel, "edge_rows", [kept(32, 256)] * 2, [], 4, p2)
 
 
 def pack1_kernel(src, mob, xlo, xhi, rows_dn, rows_up, dn_ref, upw_ref):
@@ -434,7 +439,7 @@
 
 
 def down1_kernel(
-    src, mob, xlo, xhi, ylo, yhi,
+    src, mob, xlo, xhi, ylo, yhi, p0,
     own2, dn2, upw2, s_ref, wx, wy, wz, q_ref, p2,
     m_ref, p1, r_ref, t_ref, u_ref, pk_ref,
 ):
@@ -463,7 +468,10 @@
         pk_ref[k] = packed
     own2[...] = pk_ref[2:10]
     row = iota((8, 128), 0)
-    for out, first in ((dn2, 2), (upw2, 0)):
+    for out, first, plane in ((dn2, 2, X0), (upw2, 0, X0 + 31)):
+        for k in range(8):
+            h, z = k // 2 * 8, k % 2 * 128
+            out[15 + k] = p0[plane, h : h + 8, z : z + 128]
         for k in range(10):
             out[k] = pk_ref[first + k, :8]
         for k in range(5):
@@ -474,7 +482,7 @@
 
 def down1(*operands):
     return call(
-        down1_kernel, "down1", [kept(8, 16, 128)] + [kept(15, 8, 128)] * 2 + [kept(N1, 32, 128)] * 6,
+        down1_kernel, "down1", [kept(8, 16, 128)] + [kept(23, 8, 128)] * 2 + [kept(N1, 32, 128)] * 6,
         [kept(N1, 32, 128)] * 3 + [kept(384, 256), kept(384, 128), kept(12, 16, 128)], 6, *operands,
     )
 
@@ -506,48 +514,41 @@
     return call(pack2_kernel, "pack2", [kept(N2 + N2 // 4, 8, 128)] * 2, [], 4, *operands)
 
 
-def before_kernel(wx0, wy0, wz0, q0, s0, down0_ref, plane_lo, plane_hi, rows_lo, rows_hi, out_ref, pa0, pb0, row_ref):
+def before_kernel(wx0, wy0, wz0, q0, s0, down0_ref, out_ref, pb0):
+    w0 = (wx0, wy0, wz0, q0)
+    sweep(X0 - 1, X0 + 33, 17, down0_ref, pb0, s0, w0)
+    sweep(X0, X0 + 32, 16, pb0, out_ref, s0, w0)
+
+
+def before(*operands):
+    return call(before_kernel, "before", [kept(*BIG)], [kept(*BIG)], 4, *operands)[0]
+
+
+def base_kernel(
+    wx0, wy0, wz0, q0, s0, p_0, plane_lo, plane_hi, rows_lo, rows_hi, sent, base_s, base_r, p_ref, row_ref
+):
+    del p_0, sent
     low_x, high_x = edge("gx")
     low_y, high_y = edge("gy")
     row8 = iota((8, 256), 0)
-
-    def plane_of(message, first):
-        tiles = [message[first + k] for k in range(4)]
-        return jnp.concatenate(
-            [jnp.concatenate(tiles[:2], 1), jnp.concatenate(tiles[2:], 1), jnp.zeros((8, 256), F32)], 0
-        )
-
-    pa0[2] = blank(low_x, plane_of(plane_lo, 11), 0.0)
-    pa0[N0 - 3] = blank(high_x, plane_of(plane_hi, 11), 0.0)
+    for k in range(8):
+        h, z = k // 2 * 8, k % 2 * 128
+        p_ref[X0 - 1, h : h + 8, z : z + 128] = blank(low_x, plane_lo[15 + k], 0.0)
+        p_ref[X0 + 32, h : h + 8, z : z + 128] = blank(high_x, plane_hi[15 + k], 0.0)
     for k in range(4):
         h, z = k // 2 * 16, k % 2 * 128
         row_ref[0, h : h + 16, z : z + 128] = blank(high_y, rows_hi[N1 + k], 0.0)
         row_ref[1, h : h + 16, z : z + 128] = blank(low_y, rows_lo[N1 + k], 0.0)
-    for j in (3, 4, 37, 38):
-        pa0[j] = down0_ref[j]
-
-    def own_planes(j, n):
+
+    def halo(j, n):
         for i in range(n):
             above = row_ref[0, pl.ds(j + i, 1)]
             below = row_ref[1, pl.ds(j + i, 1)]
-            p = down0_ref[j + i + X0]
-            halo = jnp.where(row8 == 2, above, jnp.where(row8 == 5, below, p[32:]))
-            pa0[j + i + X0, :32] = p[:32]
-            pa0[j + i + X0, 32:] = halo
-
-    blocks(0, 32, 8, own_planes)
-    w0 = (wx0, wy0, wz0, q0)
-    sweep(3, N0 - 3, 12, pa0, pb0, s0, w0)
-    sweep(4, N0 - 4, 17, pb0, out_ref, s0, w0)
-
-
-def before(*operands):
-    scratch = [kept(*BIG)] * 2 + [kept(2, 32, 256)]
-    return call(before_kernel, "before", [kept(*BIG)], scratch, 5, *operands)[0]
-
-
-def base_kernel(wx0, wy0, wz0, q0, s0, p_ref, sent, base_s, base_r):
-    del sent
+            p_ref[j + i + X0, 32:] = jnp.where(row8 == 0, above, jnp.where(row8 == 7, below, 0.0))
+
+    blocks(0, 32, 8, halo)
+    p_ref[X0 - 1, 32:] = jnp.zeros((8, 256), F32)
+    p_ref[X0 + 32, 32:] = jnp.zeros((8, 256), F32)
     w0 = (wx0, wy0, wz0, q0)
 
     def plane(j):
@@ -559,7 +560,8 @@
 
 
 def base(*operands):
-    return call(base_kernel, "base", [kept(32, 32, 256)] * 2, [], 4, *operands)
+    out = [kept(32, 32, 256)] * 2 + [kept(*BIG)]
+    return call(base_kernel, "base", out, [kept(2, 32, 256)], 4, *operands, aliases={5: 2})[:2]
 
 
 def up_kernel(
@@ -730,16 +732,17 @@
     dn0, up0 = call(send_planes_kernel, "send_planes", msg, [], 4, source, phase, ylo, yhi)
     xlo, xhi = both(dn0, up0, "gx")
     *state, mob1 = inner0(source, phase, ylo, yhi)
-    s0, _, wx0, wy0, wz0, q0, _, p0, _, src1, dn1, up1, rows_dn, rows_up = outer0(xlo, xhi, mob1, state)
+    s0, _, wx0, wy0, wz0, q0, _, p0, _, src1, dn1, up1 = outer0(xlo, xhi, mob1, state)
+    weights = (wx0, wy0, wz0, q0)
     xlo1, xhi1 = both(dn1, up1, "gx")
-    ylo1, yhi1 = both(*pack1(src1, mob1, xlo1, xhi1, rows_dn, rows_up), "gy")
-    own2, dn2, up2, *level1 = down1(src1, mob1, xlo1, xhi1, ylo1, yhi1)
+    p0 = before(*weights, s0, p0)
+    ylo1, yhi1 = both(*pack1(src1, mob1, xlo1, xhi1, *edge_rows(p0)), "gy")
+    own2, dn2, up2, *level1 = down1(src1, mob1, xlo1, xhi1, ylo1, yhi1, p0)
     xlo, xhi = both(dn2, up2, "gx")
     ext, ext_up = pack2(own2, xlo, xhi)
     ylo, yhi = both(ext, ext_up, "gy")
-    weights = (wx0, wy0, wz0, q0)
-    p0 = before(*weights, s0, p0, xlo1, xhi1, ylo1, yhi1)
-    return tuple(way_up(ext, ylo, yhi, *level1, *weights, *base(*weights, s0, p0, ext)))
+    based = base(*weights, s0, p0, xlo, xhi, ylo1, yhi1, ext)
+    return tuple(way_up(ext, ylo, yhi, *level1, *weights, *based))
 
 
 def solution(mesh):

time: 64.5 us -> 64.1 us (level)
    pallas_call x11 -> x12, Pallas kernels: 22.7 us -> 22.2 us  [call(): pl.pallas_call(kernel, in_specs=[VM] * len(operands) if in_specs is None...]
  transfers between devices with their start and end apart: 12 -> 12, of which waited for: 8 -> 9; matrix products, arithmetic and copies ran while one was open for 0% -> 0% of each run, Pallas kernels for 16% -> 16%
where the time goes in v6:
time: 64.1 us; the launch traced here: 64 us
  Pallas kernels  22.2 us (35%)
  starting transfers between devices  21.4 us (33%)
  waiting for transfers between devices  19.5 us (30%)
  between operations  0.89 us (1%)
    pallas_call x12, Pallas kernels, call(): pl.pallas_call(kernel, in_specs=[VM] * len(operands) if in_specs is None...  22.2 us
    ppermute x12, starting transfers between devices, shift(): lax.ppermute(a, axis, [(i, (i + step) % count) for i in range(count)])  21.4 us
    ppermute x12, waiting for transfers between devices, shift(): lax.ppermute(a, axis, [(i, (i + step) % count) for i in range(count)])  19.5 us
  transfers between devices with their start and end apart: 12, of which 9 were waited for; matrix products, arithmetic and copies ran while one was open for 0% of the time, Pallas kernels for 16%

profile of v6, /device:TPU:25, one launch (start us, length us, event | category | flops | bytes accessed | tf_op | source)
XLA Modules:
  0.0 64.0 jit_solution(17772384947475697221)
XLA Ops:
  0.6 1.3 %send_rows.1 = (f32[32,8,256]{2,1,0:T(8,128)S(1)}, f32[32,8,256]{2,1,0:T(8,128)S(1)}) custom-call(f32[32,32,256]{2,1,0:T(8,128)} %s_hbm.3, s32[32,32,256]{2,1,0:T(8,128)} %f_hbm.3), custom_call_target="tpu_custom_call" | custom-call | tf_op jit(solution)/shard_map/send_rows/pallas_call | solution.py:231
  1.9 2.3 %collective-permute-start = (f32[32,8,256]{2,1,0:T(8,128)S(1)}, f32[32,8,256]{2,1,0:T(8,128)S(1)}, u32[]{:S(2)}, u32[]{:S(2)}) collective-permute-start(f32[32,8,256]{2,1,0:T(8,128)S(1)} %get-tuple-element.48), channel_id=1, source_target_pairs={{0,1},{1,2},{2,3},{3,4},{4,5},{5,6},{6,7},{7,0},{8,9},{9,10},{10,1... | collective-permute-start | bytes 786440 | tf_op jit(solution)/shard_map/ppermute | solution.py:720
  4.2 0.0 collective-permute-start.1
  4.2 1.6 %load.1 = (f32[32,32,256]{2,1,0:T(8,128)S(1)}, s32[32,32,256]{2,1,0:T(8,128)S(1)}) custom-call(f32[32,32,256]{2,1,0:T(8,128)} %s_hbm.3, s32[32,32,256]{2,1,0:T(8,128)} %f_hbm.3, f32[32,8,256]{2,1,0:T(8,128)S(1)} %get-tuple-element.45.sent), custom_call_target="tpu_custom_call" | custom-call | tf_op jit(solution)/shard_map/load/pallas_call | solution.py:231
  5.8 1.7 %collective-permute-done.ylo = f32[32,8,256]{2,1,0:T(8,128)S(1)} collective-permute-done((f32[32,8,256]{2,1,0:T(8,128)S(1)}, f32[32,8,256]{2,1,0:T(8,128)S(1)}, u32[]{:S(2)}, u32[]{:S(2)}) %collective-permute-start) | collective-permute-done | bytes 262176 | tf_op jit(solution)/shard_map/ppermute | solution.py:720
  7.5 3.7 %collective-permute-done.1.yhi = f32[32,8,256]{2,1,0:T(8,128)S(1)} collective-permute-done((f32[32,8,256]{2,1,0:T(8,128)S(1)}, f32[32,8,256]{2,1,0:T(8,128)S(1)}, u32[]{:S(2)}, u32[]{:S(2)}) %collective-permute-start.1) | collective-permute-done | bytes 262176 | tf_op jit(solution)/shard_map/ppermute | solution.py:720
  11.2 0.2 send_planes.1
  11.4 0.1 collective-permute-start.2
  11.5 6.1 %collective-permute-start.3 = (f32[6,40,256]{2,1,0:T(8,128)S(1)}, f32[6,40,256]{2,1,0:T(8,128)S(1)}, u32[]{:S(2)}, u32[]{:S(2)}) collective-permute-start(f32[6,40,256]{2,1,0:T(8,128)S(1)} %get-tuple-element.50), channel_id=1, source_target_pairs={{0,248},{8,0},{16,8},{24,16},{32,24},{40,32},{48,40},{56,48},{64,5... | collective-permute-start | bytes 737288 | tf_op jit(solution)/shard_map/ppermute | solution.py:720
  17.6 4.8 %inner0.1 = (f32[42,40,256]{2,1,0:T(8,128)S(1)}, f32[42,40,256]{2,1,0:T(8,128)S(1)}, f32[42,40,256]{2,1,0:T(8,128)S(1)}, f32[42,40,256]{2,1,0:T(8,128)S(1)}, f32...) custom-call(f32[32,32,256]{2,1,0:T(8,128)S(1)} %get-tuple-element.46, ...), custom_call_target="tpu_custom_call" | custom-call | tf_op jit(solution)/shard_map/inner0/pallas_call | solution.py:231
  22.4 0.4 collective-permute-done.2.xlo
  22.9 0.0 collective-permute-done.3.xhi
  22.9 1.3 %outer0.1 = (f32[42,40,256]{2,1,0:T(8,128)S(1)}, f32[42,40,256]{2,1,0:T(8,128)S(1)}, f32[42,40,256]{2,1,0:T(8,128)S(1)}, f32[42,40,256]{2,1,0:T(8,128)S(1)}, f32...) custom-call(f32[6,40,256]{2,1,0:T(8,128)S(1)} %collective-permute-do, ...), custom_call_target="tpu_custom_call", output_to_operand_aliasing={{0}: (3, {}), {1}: (4, {}), {2}: (5, {}), {3}: (6, {}), {4}... | custom-call | tf_op jit(solution)/shard_map/outer0/pallas_call | solution.py:231
  24.1 0.1 collective-permute-start.4
  24.2 5.2 %collective-permute-start.5 = (f32[11,16,128]{2,1,0:T(8,128)S(1)}, f32[11,16,128]{2,1,0:T(8,128)S(1)}, u32[]{:S(2)}, u32[]{:S(2)}) collective-permute-start(f32[11,16,128]{2,1,0:T(8,128)S(1)} %get-tuple-element.64), channel_id=1, source_target_pairs={{0,248},{8,0},{16,8},{24,16},{32,24},{40,32},{48,40},{56,48},{64,5... | collective-permute-start | bytes 270344 | tf_op jit(solution)/shard_map/ppermute | solution.py:720
  29.5 2.5 %before.1.p.p0.p_0 = f32[42,40,256]{2,1,0:T(8,128)S(1)} custom-call(f32[42,40,256]{2,1,0:T(8,128)S(1)} %get-tuple-element.65.wx0, f32[42,40,256]{2,1,0:T(8,128)S(1)} %get-tuple-element.66.wy0, f32[42,40,256]{2,1,0:T(8,128)S(1)} %get-tuple-element.67.wz0, f32[42,40,256]{2,1,0:T(8,128)S(1)} %get-tuple-element.68.q0, f32[42,40,256]{2,1,0:T(8,128)S(1)} %get-tuple-element.69.s0, ...), custom_call_target="tpu_custom_call" | custom-call | tf_op jit(solution)/shard_map/before/pallas_call | solution.py:231
  32.0 0.3 collective-permute-done.4.xlo
  32.3 0.0 collective-permute-done.5.xhi
  32.3 1.4 %collective-permute-start.6 = (f32[32,16,128]{2,1,0:T(8,128)S(1)}, f32[32,16,128]{2,1,0:T(8,128)S(1)}, u32[]{:S(2)}, u32[]{:S(2)}) collective-permute-start(f32[32,16,128]{2,1,0:T(8,128)S(1)} %get-tuple-element.73), channel_id=1, source_target_pairs={{0,1},{1,2},{2,3},{3,4},{4,5},{5,6},{6,7},{7,0},{8,9},{9,10},{10,1... | collective-permute-start | bytes 786440 | tf_op jit(solution)/shard_map/ppermute | solution.py:720
  33.7 0.0 collective-permute-start.7
  33.7 3.3 %collective-permute-done.6.ylo.rows_lo = f32[32,16,128]{2,1,0:T(8,128)S(1)} collective-permute-done((f32[32,16,128]{2,1,0:T(8,128)S(1)}, f32[32,16,128]{2,1,0:T(8,128)S(1)}, u32[]{:S(2)}, u32[]{:S(2)}) %collective-permute-start.6) | collective-permute-done | bytes 262176 | tf_op jit(solution)/shard_map/ppermute | solution.py:720
  37.0 3.7 %collective-permute-done.7.yhi.rows_hi = f32[32,16,128]{2,1,0:T(8,128)S(1)} collective-permute-done((f32[32,16,128]{2,1,0:T(8,128)S(1)}, f32[32,16,128]{2,1,0:T(8,128)S(1)}, u32[]{:S(2)}, u32[]{:S(2)}) %collective-permute-start.7) | collective-permute-done | bytes 262176 | tf_op jit(solution)/shard_map/ppermute | solution.py:720
  40.7 1.9 %down1.1 = (f32[8,16,128]{2,1,0:T(8,128)S(1)}, f32[23,8,128]{2,1,0:T(8,128)S(1)}, f32[23,8,128]{2,1,0:T(8,128)S(1)}, f32[28,32,128]{2,1,0:T(8,128)S(1)}, f32[28,...) custom-call(f32[16,16,128]{2,1,0:T(8,128)S(1)} %get-tuple-element.62, ...), custom_call_target="tpu_custom_call" | custom-call | tf_op jit(solution)/shard_map/down1/pallas_call | solution.py:231
  42.6 0.1 collective-permute-start.8
  42.7 5.3 %collective-permute-start.9 = (f32[23,8,128]{2,1,0:T(8,128)S(1)}, f32[23,8,128]{2,1,0:T(8,128)S(1)}, u32[]{:S(2)}, u32[]{:S(2)}) collective-permute-start(f32[23,8,128]{2,1,0:T(8,128)S(1)} %get-tuple-element.77), channel_id=1, source_target_pairs={{0,248},{8,0},{16,8},{24,16},{32,24},{40,32},{48,40},{56,48},{64,5... | collective-permute-start | bytes 282632 | tf_op jit(solution)/shard_map/ppermute | solution.py:720
  47.9 1.7 %collective-permute-done.8.xlo.plane_lo = f32[23,8,128]{2,1,0:T(8,128)S(1)} collective-permute-done((f32[23,8,128]{2,1,0:T(8,128)S(1)}, f32[23,8,128]{2,1,0:T(8,128)S(1)}, u32[]{:S(2)}, u32[]{:S(2)}) %collective-permute-start.8) | collective-permute-done | bytes 94240 | tf_op jit(solution)/shard_map/ppermute | solution.py:720
  49.6 0.0 collective-permute-done.9.xhi.plane_hi
  49.7 1.0 %collective-permute-start.10 = (f32[35,8,128]{2,1,0:T(8,128)S(1)}, f32[35,8,128]{2,1,0:T(8,128)S(1)}, u32[]{:S(2)}, u32[]{:S(2)}) collective-permute-start(f32[35,8,128]{2,1,0:T(8,128)S(1)} %get-tuple-element.79), channel_id=1, source_target_pairs={{0,1},{1,2},{2,3},{3,4},{4,5},{5,6},{6,7},{7,0},{8,9},{9,10},{10,1... | collective-permute-start | bytes 430088 | tf_op jit(solution)/shard_map/ppermute | solution.py:720
  50.6 0.0 collective-permute-start.11
  50.6 1.1 %base.1 = (f32[32,32,256]{2,1,0:T(8,128)S(1)}, f32[32,32,256]{2,1,0:T(8,128)S(1)}, f32[42,40,256]{2,1,0:T(8,128)S(1)}) custom-call(f32[42,40,256]{2,1,0:T(8,128)S(1)} %get-tuple-element.65.wx0, f32[42,40,256]{2,1,0:T(8,128)S(1)} %get-tuple-element.66.wy0, f32[42,40,256]{2,1,0:T(8,128)S(1)} %get-tuple-element.67.wz0, ...), custom_call_target="tpu_custom_call", output_to_operand_aliasing={{2}: (5, {})} | custom-call | tf_op jit(solution)/shard_map/base/pallas_call | solution.py:231
  51.7 0.9 %collective-permute-done.10.ylo = f32[35,8,128]{2,1,0:T(8,128)S(1)} collective-permute-done((f32[35,8,128]{2,1,0:T(8,128)S(1)}, f32[35,8,128]{2,1,0:T(8,128)S(1)}, u32[]{:S(2)}, u32[]{:S(2)}) %collective-permute-start.10) | collective-permute-done | bytes 143392 | tf_op jit(solution)/shard_map/ppermute | solution.py:720
  52.7 3.7 %collective-permute-done.11.yhi = f32[35,8,128]{2,1,0:T(8,128)S(1)} collective-permute-done((f32[35,8,128]{2,1,0:T(8,128)S(1)}, f32[35,8,128]{2,1,0:T(8,128)S(1)}, u32[]{:S(2)}, u32[]{:S(2)}) %collective-permute-start.11) | collective-permute-done | bytes 143392 | tf_op jit(solution)/shard_map/ppermute | solution.py:720
  56.4 7.5 %way_up.1 = (f32[32,32,256]{2,1,0:T(8,128)}, f32[32,32,256]{2,1,0:T(8,128)}) custom-call(f32[35,8,128]{2,1,0:T(8,128)S(1)} %get-tuple-element.78.sent.ext, f32[35,8,128]{2,1,0:T(8,128)S(1)} %collective-permute-done.10.ylo, f32[35,8,128]{2,1,0:T(8,128)S(1)} %collective-permute-done.11.yhi, f32[28,32,128]{2,1,0:T(8,128)S(1)} %get-tuple-element.80.s1, ...), custom_call_target="tpu_custom_call" | custom-call | tf_op jit(solution)/shard_map/way_up/pallas_call | solution.py:231
  (3 shorter events, 0.1 us)
Async XLA Ops:
  1.9 5.6 %collective-permute-start = (f32[32,8,256]{2,1,0:T(8,128)S(1)}, f32[32,8,256]{2,1,0:T(8,128)S(1)}, u32[]{:S(2)}, u32[]{:S(2)}) collective-permute-start(f32[32,8,256]{2,1,0:T(8,128)S(1)} %get-tuple-element.48), channel_id=1, source_target_pairs={{0,1},{1,2},{2,3},{3,4},{4,5},{5,6},{6,7},{7,0},{8,9},{9,10},{10,1... | collective-permute-start | bytes 786440 | tf_op jit(solution)/shard_map/ppermute | solution.py:720
  4.2 7.0 %collective-permute-start.1 = (f32[32,8,256]{2,1,0:T(8,128)S(1)}, f32[32,8,256]{2,1,0:T(8,128)S(1)}, u32[]{:S(2)}, u32[]{:S(2)}) collective-permute-start(f32[32,8,256]{2,1,0:T(8,128)S(1)} %get-tuple-element.45.sent), channel_id=1, source_target_pairs={{0,7},{1,0},{2,1},{3,2},{4,3},{5,4},{6,5},{7,6},{8,15},{9,8},{10,9... | collective-permute-start | bytes 786440 | tf_op jit(solution)/shard_map/ppermute | solution.py:720
  11.4 11.5 %collective-permute-start.2 = (f32[6,40,256]{2,1,0:T(8,128)S(1)}, f32[6,40,256]{2,1,0:T(8,128)S(1)}, u32[]{:S(2)}, u32[]{:S(2)}) collective-permute-start(f32[6,40,256]{2,1,0:T(8,128)S(1)} %get-tuple-element.49), channel_id=1, source_target_pairs={{0,8},{8,16},{16,24},{24,32},{32,40},{40,48},{48,56},{56,64},{64,7... | collective-permute-start | bytes 737288 | tf_op jit(solution)/shard_map/ppermute | solution.py:720
  11.5 11.4 %collective-permute-start.3 = (f32[6,40,256]{2,1,0:T(8,128)S(1)}, f32[6,40,256]{2,1,0:T(8,128)S(1)}, u32[]{:S(2)}, u32[]{:S(2)}) collective-permute-start(f32[6,40,256]{2,1,0:T(8,128)S(1)} %get-tuple-element.50), channel_id=1, source_target_pairs={{0,248},{8,0},{16,8},{24,16},{32,24},{40,32},{48,40},{56,48},{64,5... | collective-permute-start | bytes 737288 | tf_op jit(solution)/shard_map/ppermute | solution.py:720
  24.1 8.1 %collective-permute-start.4 = (f32[11,16,128]{2,1,0:T(8,128)S(1)}, f32[11,16,128]{2,1,0:T(8,128)S(1)}, u32[]{:S(2)}, u32[]{:S(2)}) collective-permute-start(f32[11,16,128]{2,1,0:T(8,128)S(1)} %get-tuple-element.63), channel_id=1, source_target_pairs={{0,8},{8,16},{16,24},{24,32},{32,40},{40,48},{48,56},{56,64},{64,7... | collective-permute-start | bytes 270344 | tf_op jit(solution)/shard_map/ppermute | solution.py:720
  24.2 8.0 %collective-permute-start.5 = (f32[11,16,128]{2,1,0:T(8,128)S(1)}, f32[11,16,128]{2,1,0:T(8,128)S(1)}, u32[]{:S(2)}, u32[]{:S(2)}) collective-permute-start(f32[11,16,128]{2,1,0:T(8,128)S(1)} %get-tuple-element.64), channel_id=1, source_target_pairs={{0,248},{8,0},{16,8},{24,16},{32,24},{40,32},{48,40},{56,48},{64,5... | collective-permute-start | bytes 270344 | tf_op jit(solution)/shard_map/ppermute | solution.py:720
  32.3 4.7 %collective-permute-start.6 = (f32[32,16,128]{2,1,0:T(8,128)S(1)}, f32[32,16,128]{2,1,0:T(8,128)S(1)}, u32[]{:S(2)}, u32[]{:S(2)}) collective-permute-start(f32[32,16,128]{2,1,0:T(8,128)S(1)} %get-tuple-element.73), channel_id=1, source_target_pairs={{0,1},{1,2},{2,3},{3,4},{4,5},{5,6},{6,7},{7,0},{8,9},{9,10},{10,1... | collective-permute-start | bytes 786440 | tf_op jit(solution)/shard_map/ppermute | solution.py:720
  33.7 7.0 %collective-permute-start.7 = (f32[32,16,128]{2,1,0:T(8,128)S(1)}, f32[32,16,128]{2,1,0:T(8,128)S(1)}, u32[]{:S(2)}, u32[]{:S(2)}) collective-permute-start(f32[32,16,128]{2,1,0:T(8,128)S(1)} %get-tuple-element.74), channel_id=1, source_target_pairs={{0,7},{1,0},{2,1},{3,2},{4,3},{5,4},{6,5},{7,6},{8,15},{9,8},{10,9... | collective-permute-start | bytes 786440 | tf_op jit(solution)/shard_map/ppermute | solution.py:720
  42.6 7.1 %collective-permute-start.8 = (f32[23,8,128]{2,1,0:T(8,128)S(1)}, f32[23,8,128]{2,1,0:T(8,128)S(1)}, u32[]{:S(2)}, u32[]{:S(2)}) collective-permute-start(f32[23,8,128]{2,1,0:T(8,128)S(1)} %get-tuple-element.76), channel_id=1, source_target_pairs={{0,8},{8,16},{16,24},{24,32},{32,40},{40,48},{48,56},{56,64},{64,7... | collective-permute-start | bytes 282632 | tf_op jit(solution)/shard_map/ppermute | solution.py:720
  42.7 7.0 %collective-permute-start.9 = (f32[23,8,128]{2,1,0:T(8,128)S(1)}, f32[23,8,128]{2,1,0:T(8,128)S(1)}, u32[]{:S(2)}, u32[]{:S(2)}) collective-permute-start(f32[23,8,128]{2,1,0:T(8,128)S(1)} %get-tuple-element.77), channel_id=1, source_target_pairs={{0,248},{8,0},{16,8},{24,16},{32,24},{40,32},{48,40},{56,48},{64,5... | collective-permute-start | bytes 282632 | tf_op jit(solution)/shard_map/ppermute | solution.py:720
  49.7 3.0 %collective-permute-start.10 = (f32[35,8,128]{2,1,0:T(8,128)S(1)}, f32[35,8,128]{2,1,0:T(8,128)S(1)}, u32[]{:S(2)}, u32[]{:S(2)}) collective-permute-start(f32[35,8,128]{2,1,0:T(8,128)S(1)} %get-tuple-element.79), channel_id=1, source_target_pairs={{0,1},{1,2},{2,3},{3,4},{4,5},{5,6},{6,7},{7,0},{8,9},{9,10},{10,1... | collective-permute-start | bytes 430088 | tf_op jit(solution)/shard_map/ppermute | solution.py:720
  50.6 5.7 %collective-permute-start.11 = (f32[35,8,128]{2,1,0:T(8,128)S(1)}, f32[35,8,128]{2,1,0:T(8,128)S(1)}, u32[]{:S(2)}, u32[]{:S(2)}) collective-permute-start(f32[35,8,128]{2,1,0:T(8,128)S(1)} %get-tuple-element.78.sent.ext), channel_id=1, source_target_pairs={{0,7},{1,0},{2,1},{3,2},{4,3},{5,4},{6,5},{7,6},{8,15},{9,8},{10,9... | collective-permute-start | bytes 430088 | tf_op jit(solution)/shard_map/ppermute | solution.py:720

commit v7 on v6

--- a/solution.py
+++ b/solution.py
@@ -301,7 +301,8 @@
     return source, code
 
 
-def send_planes_kernel(s_in, f_in, ylo, yhi, dn_ref, upw_ref):
+def send_planes_kernel(s_in, f_in, ylo, yhi, ahead, dn_ref, upw_ref):
+    del ahead
     for first, out_ref, last, at in ((0, dn_ref, 2, (0, 1, 2)), (28, upw_ref, 1, (None, 0, 1, 2))):
         block = slice(first, first + 4)
         halo_source, halo_code = halo_rows(ylo[block], yhi[block])
@@ -323,6 +324,23 @@
     return iota((256, 128), 0) - 2 * iota((256, 128), 1)
 
 
+def mobility1_kernel(f_in, mob1, t_ref, u_ref):
+    for k in range(16):
+        t_ref[k * 32 : k * 32 + 32] = (f_in[2 * k] + f_in[2 * k + 1]).astype(F32)
+    water = dot(t_ref[...], pair_weight(lanes_to_128()), exact=True)
+    for k in range(16):
+        t = water[k * 32 : k * 32 + 32]
+        u_ref[k * 32 : k * 32 + 32] = t + up_y(t)
+    for k in range(16):
+        mob1[k] = water_to_mobility(every_other(u_ref, k * 32, 16))
+
+
+def mobility1(phase):
+    return call(
+        mobility1_kernel, "mobility1", [kept(16, 16, 128)], [kept(512, 256), kept(512, 128)], 4, phase
+    )[0]
+
+
 def halve0(ks, r_ref, src1, t_ref, u_ref):
     for i, k in enumerate(ks):
         t_ref[i * 40 : i * 40 + 40] = restrict_x(r_ref, 2 * k + 4)
@@ -337,7 +355,7 @@
 
 def inner0_kernel(
     s_in, f_in, ylo, yhi,
-    s_ref, c_ref, wx, wy, wz, q_ref, p1, p2, r_ref, src1, mob1,
+    s_ref, c_ref, wx, wy, wz, q_ref, p1, p2, r_ref, src1,
     t_ref, u_ref,
 ):
     def own_planes(j, n):
@@ -355,20 +373,12 @@
     remainder(8, 34, 13, p2, r_ref, s_ref, w)
 
     halve0(range(2, 14), r_ref, src1, t_ref, u_ref)
-    for k in range(16):
-        t_ref[k * 40 : k * 40 + 40] = c_ref[2 * k + X0] + c_ref[2 * k + X0 + 1]
-    water = dot(t_ref[...], pair_weight(lanes_to_128()), exact=True)
-    for k in range(16):
-        t = water[k * 40 : k * 40 + 40]
-        u_ref[k * 40 : k * 40 + 40] = t + up_y(t)
-    for k in range(16):
-        mob1[k] = water_to_mobility(every_other(u_ref, k * 40, 16))
 
 
 def inner0(source, phase, ylo, yhi):
     return call(
-        inner0_kernel, "inner0", [kept(*BIG)] * 9 + [kept(16, 16, 128)] * 2,
-        [kept(640, 256), kept(640, 128)], 4, source, phase, ylo, yhi,
+        inner0_kernel, "inner0", [kept(*BIG)] * 9 + [kept(16, 16, 128)],
+        [kept(480, 256), kept(480, 128)], 4, source, phase, ylo, yhi,
     )
 
 
@@ -728,10 +738,11 @@
     dn0, up0 = send_rows(source, phase)
     ylo, yhi = both(dn0, up0, "gy")
     source, phase = load(source, phase, dn0)
+    mob1 = mobility1(phase)
     msg = [kept(6, 40, 256)] * 2
-    dn0, up0 = call(send_planes_kernel, "send_planes", msg, [], 4, source, phase, ylo, yhi)
+    dn0, up0 = call(send_planes_kernel, "send_planes", msg, [], 4, source, phase, ylo, yhi, mob1)
     xlo, xhi = both(dn0, up0, "gx")
-    *state, mob1 = inner0(source, phase, ylo, yhi)
+    state = inner0(source, phase, ylo, yhi)
     s0, _, wx0, wy0, wz0, q0, _, p0, _, src1, dn1, up1 = outer0(xlo, xhi, mob1, state)
     weights = (wx0, wy0, wz0, q0)
     xlo1, xhi1 = both(dn1, up1, "gx")

time: 64.1 us -> 64.3 us (level)
    pallas_call x12 -> x13, Pallas kernels: 22.2 us -> 22.4 us  [call(): pl.pallas_call(kernel, in_specs=[VM] * len(operands) if in_specs is None...]
where the time goes in v7:
time: 64.3 us; the launch traced here: 64.2 us
  Pallas kernels  22.4 us (35%)
  starting transfers between devices  21.4 us (33%)
  waiting for transfers between devices  19.4 us (30%)
  between operations  0.89 us (1%)
    pallas_call x13, Pallas kernels, call(): pl.pallas_call(kernel, in_specs=[VM] * len(operands) if in_specs is None...  22.4 us
    ppermute x12, starting transfers between devices, shift(): lax.ppermute(a, axis, [(i, (i + step) % count) for i in range(count)])  21.4 us
    ppermute x12, waiting for transfers between devices, shift(): lax.ppermute(a, axis, [(i, (i + step) % count) for i in range(count)])  19.4 us
  transfers between devices with their start and end apart: 12, of which 9 were waited for; matrix products, arithmetic and copies ran while one was open for 0% of the time, Pallas kernels for 16%

profile of v7, /device:TPU:25, one launch (start us, length us, event | category | flops | bytes accessed | tf_op | source)
XLA Modules:
  0.0 64.2 jit_solution(2635600709257448339)
XLA Ops:
  0.6 1.3 %send_rows.1 = (f32[32,8,256]{2,1,0:T(8,128)S(1)}, f32[32,8,256]{2,1,0:T(8,128)S(1)}) custom-call(f32[32,32,256]{2,1,0:T(8,128)} %s_hbm.3, s32[32,32,256]{2,1,0:T(8,128)} %f_hbm.3), custom_call_target="tpu_custom_call" | custom-call | tf_op jit(solution)/shard_map/send_rows/pallas_call | solution.py:231
  1.9 2.3 %collective-permute-start = (f32[32,8,256]{2,1,0:T(8,128)S(1)}, f32[32,8,256]{2,1,0:T(8,128)S(1)}, u32[]{:S(2)}, u32[]{:S(2)}) collective-permute-start(f32[32,8,256]{2,1,0:T(8,128)S(1)} %get-tuple-element.47), channel_id=1, source_target_pairs={{0,1},{1,2},{2,3},{3,4},{4,5},{5,6},{6,7},{7,0},{8,9},{9,10},{10,1... | collective-permute-start | bytes 786440 | tf_op jit(solution)/shard_map/ppermute | solution.py:730
  4.2 0.0 collective-permute-start.1
  4.2 1.6 %load.1 = (f32[32,32,256]{2,1,0:T(8,128)S(1)}, s32[32,32,256]{2,1,0:T(8,128)S(1)}) custom-call(f32[32,32,256]{2,1,0:T(8,128)} %s_hbm.3, s32[32,32,256]{2,1,0:T(8,128)} %f_hbm.3, f32[32,8,256]{2,1,0:T(8,128)S(1)} %get-tuple-element.44.sent), custom_call_target="tpu_custom_call" | custom-call | tf_op jit(solution)/shard_map/load/pallas_call | solution.py:231
  5.8 0.3 mobility1.1.ahead.mob1.mob
  6.0 1.5 %collective-permute-done.ylo = f32[32,8,256]{2,1,0:T(8,128)S(1)} collective-permute-done((f32[32,8,256]{2,1,0:T(8,128)S(1)}, f32[32,8,256]{2,1,0:T(8,128)S(1)}, u32[]{:S(2)}, u32[]{:S(2)}) %collective-permute-start) | collective-permute-done | bytes 262176 | tf_op jit(solution)/shard_map/ppermute | solution.py:730
  7.5 3.7 %collective-permute-done.1.yhi = f32[32,8,256]{2,1,0:T(8,128)S(1)} collective-permute-done((f32[32,8,256]{2,1,0:T(8,128)S(1)}, f32[32,8,256]{2,1,0:T(8,128)S(1)}, u32[]{:S(2)}, u32[]{:S(2)}) %collective-permute-start.1) | collective-permute-done | bytes 262176 | tf_op jit(solution)/shard_map/ppermute | solution.py:730
  11.2 0.2 send_planes.1
  11.4 0.1 collective-permute-start.2
  11.5 6.1 %collective-permute-start.3 = (f32[6,40,256]{2,1,0:T(8,128)S(1)}, f32[6,40,256]{2,1,0:T(8,128)S(1)}, u32[]{:S(2)}, u32[]{:S(2)}) collective-permute-start(f32[6,40,256]{2,1,0:T(8,128)S(1)} %get-tuple-element.49), channel_id=1, source_target_pairs={{0,248},{8,0},{16,8},{24,16},{32,24},{40,32},{48,40},{56,48},{64,5... | collective-permute-start | bytes 737288 | tf_op jit(solution)/shard_map/ppermute | solution.py:730
  17.6 4.7 %inner0.1 = (f32[42,40,256]{2,1,0:T(8,128)S(1)}, f32[42,40,256]{2,1,0:T(8,128)S(1)}, f32[42,40,256]{2,1,0:T(8,128)S(1)}, f32[42,40,256]{2,1,0:T(8,128)S(1)}, f32...) custom-call(f32[32,32,256]{2,1,0:T(8,128)S(1)} %get-tuple-element.45, ...), custom_call_target="tpu_custom_call" | custom-call | tf_op jit(solution)/shard_map/inner0/pallas_call | solution.py:231
  22.3 0.6 collective-permute-done.2.xlo
  22.9 0.0 collective-permute-done.3.xhi
  22.9 1.3 %outer0.1 = (f32[42,40,256]{2,1,0:T(8,128)S(1)}, f32[42,40,256]{2,1,0:T(8,128)S(1)}, f32[42,40,256]{2,1,0:T(8,128)S(1)}, f32[42,40,256]{2,1,0:T(8,128)S(1)}, f32...) custom-call(f32[6,40,256]{2,1,0:T(8,128)S(1)} %collective-permute-do, ...), custom_call_target="tpu_custom_call", output_to_operand_aliasing={{0}: (3, {}), {1}: (4, {}), {2}: (5, {}), {3}: (6, {}), {4}... | custom-call | tf_op jit(solution)/shard_map/outer0/pallas_call | solution.py:231
  24.1 0.1 collective-permute-start.4
  24.2 5.2 %collective-permute-start.5 = (f32[11,16,128]{2,1,0:T(8,128)S(1)}, f32[11,16,128]{2,1,0:T(8,128)S(1)}, u32[]{:S(2)}, u32[]{:S(2)}) collective-permute-start(f32[11,16,128]{2,1,0:T(8,128)S(1)} %get-tuple-element.62), channel_id=1, source_target_pairs={{0,248},{8,0},{16,8},{24,16},{32,24},{40,32},{48,40},{56,48},{64,5... | collective-permute-start | bytes 270344 | tf_op jit(solution)/shard_map/ppermute | solution.py:730
  29.5 2.5 %before.1.p.p0.p_0 = f32[42,40,256]{2,1,0:T(8,128)S(1)} custom-call(f32[42,40,256]{2,1,0:T(8,128)S(1)} %get-tuple-element.63.wx0, f32[42,40,256]{2,1,0:T(8,128)S(1)} %get-tuple-element.64.wy0, f32[42,40,256]{2,1,0:T(8,128)S(1)} %get-tuple-element.65.wz0, f32[42,40,256]{2,1,0:T(8,128)S(1)} %get-tuple-element.66.q0, f32[42,40,256]{2,1,0:T(8,128)S(1)} %get-tuple-element.67.s0, ...), custom_call_target="tpu_custom_call" | custom-call | tf_op jit(solution)/shard_map/before/pallas_call | solution.py:231
  32.0 0.3 collective-permute-done.4.xlo
  32.3 0.0 collective-permute-done.5.xhi
  32.3 1.4 %collective-permute-start.6 = (f32[32,16,128]{2,1,0:T(8,128)S(1)}, f32[32,16,128]{2,1,0:T(8,128)S(1)}, u32[]{:S(2)}, u32[]{:S(2)}) collective-permute-start(f32[32,16,128]{2,1,0:T(8,128)S(1)} %get-tuple-element.71), channel_id=1, source_target_pairs={{0,1},{1,2},{2,3},{3,4},{4,5},{5,6},{6,7},{7,0},{8,9},{9,10},{10,1... | collective-permute-start | bytes 786440 | tf_op jit(solution)/shard_map/ppermute | solution.py:730
  33.7 0.0 collective-permute-start.7
  33.7 3.3 %collective-permute-done.6.ylo.rows_lo = f32[32,16,128]{2,1,0:T(8,128)S(1)} collective-permute-done((f32[32,16,128]{2,1,0:T(8,128)S(1)}, f32[32,16,128]{2,1,0:T(8,128)S(1)}, u32[]{:S(2)}, u32[]{:S(2)}) %collective-permute-start.6) | collective-permute-done | bytes 262176 | tf_op jit(solution)/shard_map/ppermute | solution.py:730
  37.0 3.7 %collective-permute-done.7.yhi.rows_hi = f32[32,16,128]{2,1,0:T(8,128)S(1)} collective-permute-done((f32[32,16,128]{2,1,0:T(8,128)S(1)}, f32[32,16,128]{2,1,0:T(8,128)S(1)}, u32[]{:S(2)}, u32[]{:S(2)}) %collective-permute-start.7) | collective-permute-done | bytes 262176 | tf_op jit(solution)/shard_map/ppermute | solution.py:730
  40.7 1.9 %down1.1 = (f32[8,16,128]{2,1,0:T(8,128)S(1)}, f32[23,8,128]{2,1,0:T(8,128)S(1)}, f32[23,8,128]{2,1,0:T(8,128)S(1)}, f32[28,32,128]{2,1,0:T(8,128)S(1)}, f32[28,...) custom-call(f32[16,16,128]{2,1,0:T(8,128)S(1)} %get-tuple-element.60, ...), custom_call_target="tpu_custom_call" | custom-call | tf_op jit(solution)/shard_map/down1/pallas_call | solution.py:231
  42.6 0.1 collective-permute-start.8
  42.7 5.3 %collective-permute-start.9 = (f32[23,8,128]{2,1,0:T(8,128)S(1)}, f32[23,8,128]{2,1,0:T(8,128)S(1)}, u32[]{:S(2)}, u32[]{:S(2)}) collective-permute-start(f32[23,8,128]{2,1,0:T(8,128)S(1)} %get-tuple-element.75), channel_id=1, source_target_pairs={{0,248},{8,0},{16,8},{24,16},{32,24},{40,32},{48,40},{56,48},{64,5... | collective-permute-start | bytes 282632 | tf_op jit(solution)/shard_map/ppermute | solution.py:730
  48.0 1.7 %collective-permute-done.8.xlo.plane_lo = f32[23,8,128]{2,1,0:T(8,128)S(1)} collective-permute-done((f32[23,8,128]{2,1,0:T(8,128)S(1)}, f32[23,8,128]{2,1,0:T(8,128)S(1)}, u32[]{:S(2)}, u32[]{:S(2)}) %collective-permute-start.8) | collective-permute-done | bytes 94240 | tf_op jit(solution)/shard_map/ppermute | solution.py:730
  49.7 0.0 collective-permute-done.9.xhi.plane_hi
  49.7 1.0 %collective-permute-start.10 = (f32[35,8,128]{2,1,0:T(8,128)S(1)}, f32[35,8,128]{2,1,0:T(8,128)S(1)}, u32[]{:S(2)}, u32[]{:S(2)}) collective-permute-start(f32[35,8,128]{2,1,0:T(8,128)S(1)} %get-tuple-element.77), channel_id=1, source_target_pairs={{0,1},{1,2},{2,3},{3,4},{4,5},{5,6},{6,7},{7,0},{8,9},{9,10},{10,1... | collective-permute-start | bytes 430088 | tf_op jit(solution)/shard_map/ppermute | solution.py:730
  50.7 0.0 collective-permute-start.11
  50.7 1.1 %base.1 = (f32[32,32,256]{2,1,0:T(8,128)S(1)}, f32[32,32,256]{2,1,0:T(8,128)S(1)}, f32[42,40,256]{2,1,0:T(8,128)S(1)}) custom-call(f32[42,40,256]{2,1,0:T(8,128)S(1)} %get-tuple-element.63.wx0, f32[42,40,256]{2,1,0:T(8,128)S(1)} %get-tuple-element.64.wy0, f32[42,40,256]{2,1,0:T(8,128)S(1)} %get-tuple-element.65.wz0, ...), custom_call_target="tpu_custom_call", output_to_operand_aliasing={{2}: (5, {})} | custom-call | tf_op jit(solution)/shard_map/base/pallas_call | solution.py:231
  51.8 0.9 %collective-permute-done.10.ylo = f32[35,8,128]{2,1,0:T(8,128)S(1)} collective-permute-done((f32[35,8,128]{2,1,0:T(8,128)S(1)}, f32[35,8,128]{2,1,0:T(8,128)S(1)}, u32[]{:S(2)}, u32[]{:S(2)}) %collective-permute-start.10) | collective-permute-done | bytes 143392 | tf_op jit(solution)/shard_map/ppermute | solution.py:730
  52.8 3.7 %collective-permute-done.11.yhi = f32[35,8,128]{2,1,0:T(8,128)S(1)} collective-permute-done((f32[35,8,128]{2,1,0:T(8,128)S(1)}, f32[35,8,128]{2,1,0:T(8,128)S(1)}, u32[]{:S(2)}, u32[]{:S(2)}) %collective-permute-start.11) | collective-permute-done | bytes 143392 | tf_op jit(solution)/shard_map/ppermute | solution.py:730
  56.4 7.6 %way_up.1 = (f32[32,32,256]{2,1,0:T(8,128)}, f32[32,32,256]{2,1,0:T(8,128)}) custom-call(f32[35,8,128]{2,1,0:T(8,128)S(1)} %get-tuple-element.76.sent.ext, f32[35,8,128]{2,1,0:T(8,128)S(1)} %collective-permute-done.10.ylo, f32[35,8,128]{2,1,0:T(8,128)S(1)} %collective-permute-done.11.yhi, f32[28,32,128]{2,1,0:T(8,128)S(1)} %get-tuple-element.78.s1, ...), custom_call_target="tpu_custom_call" | custom-call | tf_op jit(solution)/shard_map/way_up/pallas_call | solution.py:231
  (3 shorter events, 0.1 us)
Async XLA Ops:
  1.9 5.6 %collective-permute-start = (f32[32,8,256]{2,1,0:T(8,128)S(1)}, f32[32,8,256]{2,1,0:T(8,128)S(1)}, u32[]{:S(2)}, u32[]{:S(2)}) collective-permute-start(f32[32,8,256]{2,1,0:T(8,128)S(1)} %get-tuple-element.47), channel_id=1, source_target_pairs={{0,1},{1,2},{2,3},{3,4},{4,5},{5,6},{6,7},{7,0},{8,9},{9,10},{10,1... | collective-permute-start | bytes 786440 | tf_op jit(solution)/shard_map/ppermute | solution.py:730
  4.2 7.0 %collective-permute-start.1 = (f32[32,8,256]{2,1,0:T(8,128)S(1)}, f32[32,8,256]{2,1,0:T(8,128)S(1)}, u32[]{:S(2)}, u32[]{:S(2)}) collective-permute-start(f32[32,8,256]{2,1,0:T(8,128)S(1)} %get-tuple-element.44.sent), channel_id=1, source_target_pairs={{0,7},{1,0},{2,1},{3,2},{4,3},{5,4},{6,5},{7,6},{8,15},{9,8},{10,9... | collective-permute-start | bytes 786440 | tf_op jit(solution)/shard_map/ppermute | solution.py:730
  11.4 11.5 %collective-permute-start.2 = (f32[6,40,256]{2,1,0:T(8,128)S(1)}, f32[6,40,256]{2,1,0:T(8,128)S(1)}, u32[]{:S(2)}, u32[]{:S(2)}) collective-permute-start(f32[6,40,256]{2,1,0:T(8,128)S(1)} %get-tuple-element.48), channel_id=1, source_target_pairs={{0,8},{8,16},{16,24},{24,32},{32,40},{40,48},{48,56},{56,64},{64,7... | collective-permute-start | bytes 737288 | tf_op jit(solution)/shard_map/ppermute | solution.py:730
  11.5 11.4 %collective-permute-start.3 = (f32[6,40,256]{2,1,0:T(8,128)S(1)}, f32[6,40,256]{2,1,0:T(8,128)S(1)}, u32[]{:S(2)}, u32[]{:S(2)}) collective-permute-start(f32[6,40,256]{2,1,0:T(8,128)S(1)} %get-tuple-element.49), channel_id=1, source_target_pairs={{0,248},{8,0},{16,8},{24,16},{32,24},{40,32},{48,40},{56,48},{64,5... | collective-permute-start | bytes 737288 | tf_op jit(solution)/shard_map/ppermute | solution.py:730
  24.1 8.1 %collective-permute-start.4 = (f32[11,16,128]{2,1,0:T(8,128)S(1)}, f32[11,16,128]{2,1,0:T(8,128)S(1)}, u32[]{:S(2)}, u32[]{:S(2)}) collective-permute-start(f32[11,16,128]{2,1,0:T(8,128)S(1)} %get-tuple-element.61), channel_id=1, source_target_pairs={{0,8},{8,16},{16,24},{24,32},{32,40},{40,48},{48,56},{56,64},{64,7... | collective-permute-start | bytes 270344 | tf_op jit(solution)/shard_map/ppermute | solution.py:730
  24.2 8.0 %collective-permute-start.5 = (f32[11,16,128]{2,1,0:T(8,128)S(1)}, f32[11,16,128]{2,1,0:T(8,128)S(1)}, u32[]{:S(2)}, u32[]{:S(2)}) collective-permute-start(f32[11,16,128]{2,1,0:T(8,128)S(1)} %get-tuple-element.62), channel_id=1, source_target_pairs={{0,248},{8,0},{16,8},{24,16},{32,24},{40,32},{48,40},{56,48},{64,5... | collective-permute-start | bytes 270344 | tf_op jit(solution)/shard_map/ppermute | solution.py:730
  32.3 4.7 %collective-permute-start.6 = (f32[32,16,128]{2,1,0:T(8,128)S(1)}, f32[32,16,128]{2,1,0:T(8,128)S(1)}, u32[]{:S(2)}, u32[]{:S(2)}) collective-permute-start(f32[32,16,128]{2,1,0:T(8,128)S(1)} %get-tuple-element.71), channel_id=1, source_target_pairs={{0,1},{1,2},{2,3},{3,4},{4,5},{5,6},{6,7},{7,0},{8,9},{9,10},{10,1... | collective-permute-start | bytes 786440 | tf_op jit(solution)/shard_map/ppermute | solution.py:730
  33.7 7.0 %collective-permute-start.7 = (f32[32,16,128]{2,1,0:T(8,128)S(1)}, f32[32,16,128]{2,1,0:T(8,128)S(1)}, u32[]{:S(2)}, u32[]{:S(2)}) collective-permute-start(f32[32,16,128]{2,1,0:T(8,128)S(1)} %get-tuple-element.72), channel_id=1, source_target_pairs={{0,7},{1,0},{2,1},{3,2},{4,3},{5,4},{6,5},{7,6},{8,15},{9,8},{10,9... | collective-permute-start | bytes 786440 | tf_op jit(solution)/shard_map/ppermute | solution.py:730
  42.6 7.1 %collective-permute-start.8 = (f32[23,8,128]{2,1,0:T(8,128)S(1)}, f32[23,8,128]{2,1,0:T(8,128)S(1)}, u32[]{:S(2)}, u32[]{:S(2)}) collective-permute-start(f32[23,8,128]{2,1,0:T(8,128)S(1)} %get-tuple-element.74), channel_id=1, source_target_pairs={{0,8},{8,16},{16,24},{24,32},{32,40},{40,48},{48,56},{56,64},{64,7... | collective-permute-start | bytes 282632 | tf_op jit(solution)/shard_map/ppermute | solution.py:730
  42.7 7.0 %collective-permute-start.9 = (f32[23,8,128]{2,1,0:T(8,128)S(1)}, f32[23,8,128]{2,1,0:T(8,128)S(1)}, u32[]{:S(2)}, u32[]{:S(2)}) collective-permute-start(f32[23,8,128]{2,1,0:T(8,128)S(1)} %get-tuple-element.75), channel_id=1, source_target_pairs={{0,248},{8,0},{16,8},{24,16},{32,24},{40,32},{48,40},{56,48},{64,5... | collective-permute-start | bytes 282632 | tf_op jit(solution)/shard_map/ppermute | solution.py:730
  49.7 3.0 %collective-permute-start.10 = (f32[35,8,128]{2,1,0:T(8,128)S(1)}, f32[35,8,128]{2,1,0:T(8,128)S(1)}, u32[]{:S(2)}, u32[]{:S(2)}) collective-permute-start(f32[35,8,128]{2,1,0:T(8,128)S(1)} %get-tuple-element.77), channel_id=1, source_target_pairs={{0,1},{1,2},{2,3},{3,4},{4,5},{5,6},{6,7},{7,0},{8,9},{9,10},{10,1... | collective-permute-start | bytes 430088 | tf_op jit(solution)/shard_map/ppermute | solution.py:730
  50.7 5.7 %collective-permute-start.11 = (f32[35,8,128]{2,1,0:T(8,128)S(1)}, f32[35,8,128]{2,1,0:T(8,128)S(1)}, u32[]{:S(2)}, u32[]{:S(2)}) collective-permute-start(f32[35,8,128]{2,1,0:T(8,128)S(1)} %get-tuple-element.76.sent.ext), channel_id=1, source_target_pairs={{0,7},{1,0},{2,1},{3,2},{4,3},{5,4},{6,5},{7,6},{8,15},{9,8},{10,9... | collective-permute-start | bytes 430088 | tf_op jit(solution)/shard_map/ppermute | solution.py:730
